TPU v7x, 128 devices: a whole 4x4x4 slice. The times are simulated.
128 devices in a mesh: slab: 4 (over x), dev: 32 (over z, y, core).
Axes of the slice: x: 4, y: 4, z: 4, core: 2. Of those that a mesh axis runs over, the one named last changes fastest.
Arguments:
- table: float32 [524288, 128], P(('slab', 'dev')), may hold values from -6 to 6
- accum: float32 [524288, 128], P(('slab', 'dev')), may hold values from 0.1 to 1
- evict_delta: float32 [128, 128, 4, 128], P(('slab', 'dev')), may hold values from -6 to 6
- evict_ids: int32 [128, 128, 4], P(('slab', 'dev')), may hold values from 0 to 4095
- hot_ids: int32 [128, 16], P(('slab', 'dev')), may hold values from 0 to 4095
- cache_old: bfloat16 [2048, 128], replicated, may hold values from -6 to 6
- bag_index: int32 [65536, 16, 8], P(('slab', 'dev')), may hold values from 0 to 4095
- bag_length: int32 [65536, 16], P(('slab', 'dev')), may hold values from 1 to 8
- labels: int32 [65536], P(('slab', 'dev')), may hold values 0 or 1
- w_first: bfloat16 [2048, 2048], P(('slab', 'dev')), may hold values from -0.125 to 0.125
- w_out: bfloat16 [2048], replicated, may hold values from -0.125 to 0.125
Outputs:
- table_new: float32 [524288, 128], P(('slab', 'dev'))
- accum_new: float32 [524288, 128], P(('slab', 'dev'))
- grad_w1: float32 [2048, 2048], P(('slab', 'dev'))
- grad_w2: float32 [2048], replicated
All inputs are finite; a program needn't handle non-finite values. No bound on the sum of `labels` on one device may be relied on, other than what follows from the above.
Results may differ from a plain program's by a relative error of at most 0.003.
Values may be sent and summed in bfloat16 or wider, within the bound.
No kernel may reach another device: no remote copies, remote signals or barrier semaphores. Data moves between devices by JAX's collectives and lax.ppermute only.
A program may use at most 128 MiB of HBM per device.

v0:
```python
import jax
import jax.numpy as jnp
from jax import lax
from jax.sharding import PartitionSpec as P


def gelu_tanh(values):
    return jax.nn.gelu(values, approximate=True)


def pool_field(cache_all, field_index, field_length):
    samples, bag_most = field_index.shape
    columns = cache_all.shape[0]
    slot_line = lax.broadcasted_iota(jnp.int32, (1, columns), 1)
    counts = jnp.zeros((samples, columns), jnp.float32)
    for position in range(bag_most):
        pick = jnp.where(position < field_length, field_index[:, position], -1)
        counts = counts + (pick[:, None] == slot_line).astype(jnp.float32)
    return jnp.dot(counts.astype(jnp.bfloat16), cache_all, preferred_element_type=jnp.float32)


def per_device(
    table,
    accum,
    evict_delta,
    evict_ids,
    hot_ids,
    cache_old,
    bag_index,
    bag_length,
    labels,
    w_first,
    w_out,
):
    width = table.shape[1]
    deltas = evict_delta[0]
    slot_ids = evict_ids[0]
    got_delta, got_ids = (
        lax.all_to_all(deltas, ("slab", "dev"), split_axis=0, concat_axis=0, tiled=True),
        lax.all_to_all(slot_ids, ("slab", "dev"), split_axis=0, concat_axis=0, tiled=True),
    )
    got_delta = got_delta.reshape(-1, width)
    got_ids = got_ids.reshape(-1)
    summed = jnp.zeros_like(table).at[got_ids].add(got_delta)
    accum_new = accum + summed * summed
    table_new = table - 0.5 * summed * lax.rsqrt(accum_new)
    fresh = jnp.take(table_new, hot_ids[0], axis=0).astype(jnp.bfloat16)
    new_rows = lax.all_gather(fresh, ("slab", "dev"), axis=0, tiled=True)
    cache_all = jnp.concatenate([cache_old, new_rows], axis=0)
    samples, fields, bag_most = bag_index.shape
    pieces = []
    for field in range(fields):
        pieces.append(pool_field(cache_all, bag_index[:, field, :], bag_length[:, field]))
    pooled = jnp.concatenate(pieces, axis=1).astype(jnp.bfloat16)
    full_weight = lax.all_gather(w_first, ("slab", "dev"), axis=0, tiled=True)
    hidden = jnp.dot(pooled, full_weight, preferred_element_type=jnp.float32)
    act, backward = jax.vjp(gelu_tanh, hidden)
    slope = backward(jnp.ones_like(hidden))[0]
    act_b = act.astype(jnp.bfloat16)
    logit = jnp.dot(act_b, w_out, preferred_element_type=jnp.float32)
    grad_logit = 0.125 * (jax.nn.sigmoid(logit) - labels.astype(jnp.float32))
    grad_hidden = (grad_logit[:, None] * w_out.astype(jnp.float32)[None, :] * slope).astype(
        jnp.bfloat16
    )
    out_term = jnp.dot(grad_logit, act_b, preferred_element_type=jnp.float32)
    grad_w2 = lax.psum(out_term, ("slab", "dev"))
    whole_term = jnp.dot(pooled.T, grad_hidden, preferred_element_type=jnp.float32)
    grad_w1 = lax.psum_scatter(whole_term, ("slab", "dev"), scatter_dimension=0, tiled=True)
    return (table_new, accum_new, grad_w1, grad_w2)


def solution(mesh):
    placed = (
        P(("slab", "dev"), None),
        P(("slab", "dev"), None),
        P(("slab", "dev"), None, None, None),
        P(("slab", "dev"), None, None),
        P(("slab", "dev"), None),
        P(),
        P(("slab", "dev"), None, None),
        P(("slab", "dev"), None),
        P(("slab", "dev")),
        P(("slab", "dev"), None),
        P(),
    )
    return jax.shard_map(
        per_device,
        mesh=mesh,
        in_specs=placed,
        out_specs=(
            P(("slab", "dev"), None),
            P(("slab", "dev"), None),
            P(("slab", "dev"), None),
            P(),
        ),
        check_vma=False,
    )
```

profile of v0, /device:TPU:1, one launch (start us, length us, event | category | flops | bytes accessed | tf_op | source)
XLA Modules:
  0.0 954.9 jit_solution(823217247395527381)
XLA Ops:
  7.2 0.0 all-gather.2.cloned.1.call-start
  7.2 0.7 all-gather.2.cloned.1.call-update
  7.9 1.4 copy.17
  9.3 11.5 %all-to-all-start = ((s32[128,1,4]{2,1,0:T(1,128)}), s32[128,1,4]{2,1,0:T(1,128)S(1)}, u32[]{:S(2)}, u32[]{:S(2)}) async-start(s32[128,1,4]{2,1,0:T(1,128)} %bitcast), calls=%async_computation | async-start | bytes 131072 | tf_op jit(solution)/shard_map/all_to_all | solution.py:40
  20.8 0.7 fusion.69
  21.5 0.9 slice_bitcast_fusion
  22.4 1.3 compare_select_fusion.8
  23.7 1.3 compare_select_fusion.24
  25.1 1.3 compare_select_fusion.32
  26.4 1.3 compare_select_fusion.40
  27.8 0.7 compare_select_fusion.48
  28.5 0.7 compare_select_fusion.56
  29.3 0.7 compare_select_fusion.64
  30.0 0.7 compare_select_fusion.72
  30.8 1.3 compare_select_fusion.80
  32.1 1.3 compare_select_fusion.88
  33.4 1.3 compare_select_fusion.96
  34.8 1.3 compare_select_fusion.104
  36.1 1.3 compare_select_fusion.112
  37.5 1.3 compare_select_fusion.120
  38.8 1.3 compare_select_fusion.128
  40.2 1.3 compare_select_fusion.16
  41.5 1.1 constant_dynamic-update-slice_fusion.1
  42.6 1.2 compare_and_fusion
  43.8 0.0 all-to-all-done
  43.8 9.8 %all-to-all-start.1 = ((f32[128,4,128]{2,1,0:T(4,128)}), f32[128,4,128]{2,1,0:T(4,128)S(1)}, u32[]{:S(2)}, u32[]{:S(2)}) async-start(f32[128,4,128]{2,1,0:T(4,128)} %bitcast.196), calls=%async_computation.1 | async-start | bytes 524288 | tf_op jit(solution)/shard_map/all_to_all | solution.py:39
  53.6 0.0 reduce-scatter.2.cloned.1.call-start
  53.6 1.3 convert_element_type.595
  54.9 1.3 reshape.100
  56.2 0.5 broadcast.514
  56.7 0.8 reduce.3
  57.6 0.1 reshape.82
  57.7 0.6 compare_select_fusion
  58.2 6.1 all-to-all-done.1
  64.4 2.9 scatter_custom_fusion
  67.3 4.6 multiply_subtract_fusion
  72.0 2.3 gather_fusion
  74.3 0.1 select_convert_fusion
  74.3 34.5 %all_gather.6 = bf16[2048,128]{1,0:T(8,128)(2,1)S(1)} all-gather(bf16[16,128]{1,0:T(8,128)(2,1)S(1)} %select_convert_fusion), channel_id=1, replica_groups=mesh['slab'=4,'dev'=32] {'slab','dev'}, dimensions={0}, use_global_device_ids=true | all-gather | bytes 528384 | tf_op jit(solution)/shard_map/all_gather | solution.py:48
  108.8 0.1 constant_dynamic-update-slice_fusion
  109.1 9.9 %fusion.50 = bf16[512,2048]{0,1:T(8,128)(2,1)} fusion(bf16[4096,128]{1,0:T(8,128)(2,1)S(1)} %constant_dynamic-update-slice_fusion, s32[512]{0:T(512)S(1)} %bitcast.322, s32[512]{0:T(512)S(1)} %bitcast.323, s32[512]{0:T(512)S(1)} %bitcast.324, s32[512]{0:T(512)S(1)} %bitcast.325, s32[512]{0:T(512)S(1)} %bitcast.326, s32[512]{0:T(512)S(1)} %bitcast.327, ...), kind=kOutput, calls=%fused_computation.200 | convolution fusion | flops 587268096 | bytes 1196032 | tf_op jit(solution)/shard_map/dot_general | solution.py:19
  119.1 9.9 %fusion.51 = bf16[512,2048]{0,1:T(8,128)(2,1)} fusion(bf16[512,2048]{0,1:T(8,128)(2,1)} %fusion.50, bf16[4096,128]{1,0:T(8,128)(2,1)S(1)} %constant_dynamic-update-slice_fusion, s32[512]{0:T(512)S(1)} %bitcast.314, s32[512]{0:T(512)S(1)} %bitcast.315, s32[512]{0:T(512)S(1)} %bitcast.316, s32[512]{0:T(512)S(1)} %bitcast.317, s32[512]{0:T(512)S(1)} %bitcast.318, ...), kind=kOutput, calls=%fused_computation.201 | convolution fusion | flops 587268096 | bytes 1196032 | tf_op jit(solution)/shard_map/dot_general | solution.py:19
  129.1 10.3 %fusion.52 = bf16[512,2048]{0,1:T(8,128)(2,1)} fusion(bf16[512,2048]{0,1:T(8,128)(2,1)} %fusion.51, bf16[4096,128]{1,0:T(8,128)(2,1)S(1)} %constant_dynamic-update-slice_fusion, s32[512]{0:T(512)S(1)} %bitcast.306, s32[512]{0:T(512)S(1)} %bitcast.307, s32[512]{0:T(512)S(1)} %bitcast.308, s32[512]{0:T(512)S(1)} %bitcast.309, s32[512]{0:T(512)S(1)} %bitcast.310, ...), kind=kOutput, calls=%fused_computation.202 | convolution fusion | flops 587268096 | bytes 1196032 | tf_op jit(solution)/shard_map/dot_general | solution.py:19
  139.6 9.9 %fusion.53 = bf16[512,2048]{0,1:T(8,128)(2,1)} fusion(bf16[512,2048]{0,1:T(8,128)(2,1)} %fusion.52, bf16[4096,128]{1,0:T(8,128)(2,1)S(1)} %constant_dynamic-update-slice_fusion, s32[512]{0:T(512)S(1)} %bitcast.298, s32[512]{0:T(512)S(1)} %bitcast.299, s32[512]{0:T(512)S(1)} %bitcast.300, s32[512]{0:T(512)S(1)} %bitcast.301, s32[512]{0:T(512)S(1)} %bitcast.302, ...), kind=kOutput, calls=%fused_computation.203 | convolution fusion | flops 587268096 | bytes 1196032 | tf_op jit(solution)/shard_map/dot_general | solution.py:19
  149.6 10.1 %fusion.54 = bf16[512,2048]{0,1:T(8,128)(2,1)} fusion(bf16[512,2048]{0,1:T(8,128)(2,1)} %fusion.53, bf16[4096,128]{1,0:T(8,128)(2,1)S(1)} %constant_dynamic-update-slice_fusion, s32[512]{0:T(512)S(1)} %bitcast.290, s32[512]{0:T(512)S(1)} %bitcast.291, s32[512]{0:T(512)S(1)} %bitcast.292, s32[512]{0:T(512)S(1)} %bitcast.293, s32[512]{0:T(512)S(1)} %bitcast.294, ...), kind=kOutput, calls=%fused_computation.204 | convolution fusion | flops 587268096 | bytes 1196032 | tf_op jit(solution)/shard_map/dot_general | solution.py:19
  159.8 9.9 %fusion.55 = bf16[512,2048]{0,1:T(8,128)(2,1)} fusion(bf16[512,2048]{0,1:T(8,128)(2,1)} %fusion.54, bf16[4096,128]{1,0:T(8,128)(2,1)S(1)} %constant_dynamic-update-slice_fusion, s32[512]{0:T(512)S(1)} %bitcast.282, s32[512]{0:T(512)S(1)} %bitcast.283, s32[512]{0:T(512)S(1)} %bitcast.284, s32[512]{0:T(512)S(1)} %bitcast.285, s32[512]{0:T(512)S(1)} %bitcast.286, ...), kind=kOutput, calls=%fused_computation.205 | convolution fusion | flops 587268096 | bytes 1196032 | tf_op jit(solution)/shard_map/dot_general | solution.py:19
  169.7 10.1 %fusion.56 = bf16[512,2048]{0,1:T(8,128)(2,1)} fusion(bf16[512,2048]{0,1:T(8,128)(2,1)} %fusion.55, bf16[4096,128]{1,0:T(8,128)(2,1)S(1)} %constant_dynamic-update-slice_fusion, s32[512]{0:T(512)S(1)} %bitcast.274, s32[512]{0:T(512)S(1)} %bitcast.275, s32[512]{0:T(512)S(1)} %bitcast.276, s32[512]{0:T(512)S(1)} %bitcast.277, s32[512]{0:T(512)S(1)} %bitcast.278, ...), kind=kOutput, calls=%fused_computation.206 | convolution fusion | flops 587268096 | bytes 1196032 | tf_op jit(solution)/shard_map/dot_general | solution.py:19
  179.8 9.8 %fusion.57 = bf16[512,2048]{0,1:T(8,128)(2,1)} fusion(bf16[512,2048]{0,1:T(8,128)(2,1)} %fusion.56, bf16[4096,128]{1,0:T(8,128)(2,1)S(1)} %constant_dynamic-update-slice_fusion, s32[512]{0:T(512)S(1)} %bitcast.258, s32[512]{0:T(512)S(1)} %bitcast.259, s32[512]{0:T(512)S(1)} %bitcast.260, s32[512]{0:T(512)S(1)} %bitcast.261, s32[512]{0:T(512)S(1)} %bitcast.262, ...), kind=kOutput, calls=%fused_computation.207 | convolution fusion | flops 587268096 | bytes 1196032 | tf_op jit(solution)/shard_map/dot_general | solution.py:19
  189.6 10.2 %fusion.58 = bf16[512,2048]{0,1:T(8,128)(2,1)} fusion(bf16[512,2048]{0,1:T(8,128)(2,1)} %fusion.57, bf16[4096,128]{1,0:T(8,128)(2,1)S(1)} %constant_dynamic-update-slice_fusion, s32[512]{0:T(512)S(1)} %bitcast.250, s32[512]{0:T(512)S(1)} %bitcast.251, s32[512]{0:T(512)S(1)} %bitcast.252, s32[512]{0:T(512)S(1)} %bitcast.253, s32[512]{0:T(512)S(1)} %bitcast.254, ...), kind=kOutput, calls=%fused_computation.208 | convolution fusion | flops 587268096 | bytes 1196032 | tf_op jit(solution)/shard_map/dot_general | solution.py:19
  199.8 9.9 %fusion.59 = bf16[512,2048]{0,1:T(8,128)(2,1)} fusion(bf16[512,2048]{0,1:T(8,128)(2,1)} %fusion.58, bf16[4096,128]{1,0:T(8,128)(2,1)S(1)} %constant_dynamic-update-slice_fusion, s32[512]{0:T(512)S(1)} %bitcast.242, s32[512]{0:T(512)S(1)} %bitcast.243, s32[512]{0:T(512)S(1)} %bitcast.244, s32[512]{0:T(512)S(1)} %bitcast.245, s32[512]{0:T(512)S(1)} %bitcast.246, ...), kind=kOutput, calls=%fused_computation.209 | convolution fusion | flops 587268096 | bytes 1196032 | tf_op jit(solution)/shard_map/dot_general | solution.py:19
  209.7 10.0 %fusion.60 = bf16[512,2048]{0,1:T(8,128)(2,1)} fusion(bf16[512,2048]{0,1:T(8,128)(2,1)} %fusion.59, bf16[4096,128]{1,0:T(8,128)(2,1)S(1)} %constant_dynamic-update-slice_fusion, s32[512]{0:T(512)S(1)} %bitcast.234, s32[512]{0:T(512)S(1)} %bitcast.235, s32[512]{0:T(512)S(1)} %bitcast.236, s32[512]{0:T(512)S(1)} %bitcast.237, s32[512]{0:T(512)S(1)} %bitcast.238, ...), kind=kOutput, calls=%fused_computation.210 | convolution fusion | flops 587268096 | bytes 1196032 | tf_op jit(solution)/shard_map/dot_general | solution.py:19
  219.9 9.9 %fusion.61 = bf16[512,2048]{0,1:T(8,128)(2,1)} fusion(bf16[512,2048]{0,1:T(8,128)(2,1)} %fusion.60, bf16[4096,128]{1,0:T(8,128)(2,1)S(1)} %constant_dynamic-update-slice_fusion, s32[512]{0:T(512)S(1)} %bitcast.226, s32[512]{0:T(512)S(1)} %bitcast.227, s32[512]{0:T(512)S(1)} %bitcast.228, s32[512]{0:T(512)S(1)} %bitcast.229, s32[512]{0:T(512)S(1)} %bitcast.230, ...), kind=kOutput, calls=%fused_computation.211 | convolution fusion | flops 587268096 | bytes 1196032 | tf_op jit(solution)/shard_map/dot_general | solution.py:19
  229.9 10.1 %fusion.62 = bf16[512,2048]{0,1:T(8,128)(2,1)} fusion(bf16[512,2048]{0,1:T(8,128)(2,1)} %fusion.61, bf16[4096,128]{1,0:T(8,128)(2,1)S(1)} %constant_dynamic-update-slice_fusion, s32[512]{0:T(512)S(1)} %bitcast.218, s32[512]{0:T(512)S(1)} %bitcast.219, s32[512]{0:T(512)S(1)} %bitcast.220, s32[512]{0:T(512)S(1)} %bitcast.221, s32[512]{0:T(512)S(1)} %bitcast.222, ...), kind=kOutput, calls=%fused_computation.212 | convolution fusion | flops 587268096 | bytes 1196032 | tf_op jit(solution)/shard_map/dot_general | solution.py:19
  240.2 9.9 %fusion.63 = bf16[512,2048]{0,1:T(8,128)(2,1)} fusion(bf16[512,2048]{0,1:T(8,128)(2,1)} %fusion.62, bf16[4096,128]{1,0:T(8,128)(2,1)S(1)} %constant_dynamic-update-slice_fusion, s32[512]{0:T(512)S(1)} %bitcast.210, s32[512]{0:T(512)S(1)} %bitcast.211, s32[512]{0:T(512)S(1)} %bitcast.212, s32[512]{0:T(512)S(1)} %bitcast.213, s32[512]{0:T(512)S(1)} %bitcast.214, ...), kind=kOutput, calls=%fused_computation.213 | convolution fusion | flops 587268096 | bytes 1196032 | tf_op jit(solution)/shard_map/dot_general | solution.py:19
  250.2 10.1 %fusion.64 = bf16[512,2048]{0,1:T(8,128)(2,1)} fusion(bf16[512,2048]{0,1:T(8,128)(2,1)} %fusion.63, bf16[4096,128]{1,0:T(8,128)(2,1)S(1)} %constant_dynamic-update-slice_fusion, s32[512]{0:T(512)S(1)} %bitcast.266, s32[512]{0:T(512)S(1)} %bitcast.267, s32[512]{0:T(512)S(1)} %bitcast.268, s32[512]{0:T(512)S(1)} %bitcast.269, s32[512]{0:T(512)S(1)} %bitcast.270, ...), kind=kOutput, calls=%fused_computation.214 | convolution fusion | flops 587268096 | bytes 1196032 | tf_op jit(solution)/shard_map/dot_general | solution.py:19
  260.4 9.9 %fusion.65 = bf16[512,2048]{0,1:T(8,128)(2,1)} fusion(bf16[512,2048]{0,1:T(8,128)(2,1)} %fusion.64, bf16[4096,128]{1,0:T(8,128)(2,1)S(1)} %constant_dynamic-update-slice_fusion, s32[512]{0:T(512)S(1)} %bitcast.202, s32[512]{0:T(512)S(1)} %bitcast.203, s32[512]{0:T(512)S(1)} %bitcast.204, s32[512]{0:T(512)S(1)} %bitcast.205, s32[512]{0:T(512)S(1)} %bitcast.206, ...), kind=kOutput, calls=%fused_computation.215 | convolution fusion | flops 587268096 | bytes 1196032 | tf_op jit(solution)/shard_map/dot_general | solution.py:19
  270.3 0.0 all-gather.2.cloned.1.call-done
  270.3 8.9 multiply_convert_fusion
  279.2 0.6 fusion.76
  279.9 10.9 %fusion.24 = f32[2048,2048]{1,0:T(8,128)} fusion(bf16[512,2048]{0,1:T(8,128)(2,1)} %fusion.65, f32[512,2048]{1,0:T(8,128)S(1)} %get-tuple-element.151, f32[2048]{0:T(1024)S(1)} %copy-done.1, f32[512]{0:T(512)S(1)} %fusion.68), kind=kOutput, calls=%fused_computation.173 | convolution fusion | flops 4315938816 | bytes 23078912 | tf_op jit(solution)/shard_map/dot_general | solution.py:67
  290.8 0.0 reduce-scatter.2.cloned.1.call-update
  290.8 0.4 fusion.77
  291.2 63.7 %psum.7 = f32[2048]{0:T(1024)} all-reduce(f32[2048]{0:T(1024)S(1)} %bitcast.198), channel_id=1, replica_groups=mesh['slab'=4,'dev'=32] {'slab','dev'}, use_global_device_ids=true, to_apply=%region_2.3 | all-reduce | flops 2048 | bytes 16384 | tf_op jit(solution)/shard_map/psum | solution.py:66
  354.9 593.0 %reduce-scatter.2.cloned.1.call-done = f32[16,2048]{1,0:T(8,128)} async-done(((f32[2048,2048]{1,0:T(8,128)}), f32[16,2048]{1,0:T(8,128)}) %reduce-scatter.2.cloned.1.call-update) | async-done | bytes 131088 | tf_op jit(solution)/shard_map/reduce_scatter | solution.py:68
  (196 shorter events, 0.4 us)
Async XLA Ops:
  7.2 263.1 %all-gather.2.cloned.1.call-start = ((), (), s32[]{:S(2)}) async-start(), calls=%async_computation.3 | async-start | bytes 8454144 | tf_op jit(solution)/shard_map/all_gather | solution.py:55
  9.3 34.5 %all-to-all-start = ((s32[128,1,4]{2,1,0:T(1,128)}), s32[128,1,4]{2,1,0:T(1,128)S(1)}, u32[]{:S(2)}, u32[]{:S(2)}) async-start(s32[128,1,4]{2,1,0:T(1,128)} %bitcast), calls=%async_computation | async-start | bytes 131072 | tf_op jit(solution)/shard_map/all_to_all | solution.py:40
  43.8 20.5 %all-to-all-start.1 = ((f32[128,4,128]{2,1,0:T(4,128)}), f32[128,4,128]{2,1,0:T(4,128)S(1)}, u32[]{:S(2)}, u32[]{:S(2)}) async-start(f32[128,4,128]{2,1,0:T(4,128)} %bitcast.196), calls=%async_computation.1 | async-start | bytes 524288 | tf_op jit(solution)/shard_map/all_to_all | solution.py:39
  53.6 894.3 %reduce-scatter.2.cloned.1.call-start = ((), (), s32[]{:S(2)}) async-start(), calls=%async_computation.4 | async-start | bytes 16908288 | tf_op jit(solution)/shard_map/reduce_scatter | solution.py:68
  67.3 41.7 %copy-start.88 = (s32[512,1]{0,1:T(1,128)S(1)}, s32[512,1]{0,1:T(1,128)}, u32[]{:S(2)}) copy-start(s32[512,1]{0,1:T(1,128)} %get-tuple-element.142) | copy-start | bytes 6148
  67.3 41.7 %copy-start.89 = (s32[512,1]{0,1:T(1,128)S(1)}, s32[512,1]{0,1:T(1,128)}, u32[]{:S(2)}) copy-start(s32[512,1]{0,1:T(1,128)} %get-tuple-element.143) | copy-start | bytes 6148
  67.3 41.7 %copy-start.90 = (s32[512,1]{0,1:T(1,128)S(1)}, s32[512,1]{0,1:T(1,128)}, u32[]{:S(2)}) copy-start(s32[512,1]{0,1:T(1,128)} %get-tuple-element.144) | copy-start | bytes 6148
  67.3 41.7 %copy-start.91 = (s32[512,1]{0,1:T(1,128)S(1)}, s32[512,1]{0,1:T(1,128)}, u32[]{:S(2)}) copy-start(s32[512,1]{0,1:T(1,128)} %get-tuple-element.145) | copy-start | bytes 6148
  67.3 41.7 %copy-start.92 = (s32[512,1]{0,1:T(1,128)S(1)}, s32[512,1]{0,1:T(1,128)}, u32[]{:S(2)}) copy-start(s32[512,1]{0,1:T(1,128)} %get-tuple-element.146) | copy-start | bytes 6148
  67.3 41.7 %copy-start.93 = (s32[512,1]{0,1:T(1,128)S(1)}, s32[512,1]{0,1:T(1,128)}, u32[]{:S(2)}) copy-start(s32[512,1]{0,1:T(1,128)} %get-tuple-element.147) | copy-start | bytes 6148
  67.3 41.7 %copy-start.94 = (s32[512,1]{0,1:T(1,128)S(1)}, s32[512,1]{0,1:T(1,128)}, u32[]{:S(2)}) copy-start(s32[512,1]{0,1:T(1,128)} %get-tuple-element.148) | copy-start | bytes 6148
  67.3 41.7 %copy-start.95 = (s32[512,1]{0,1:T(1,128)S(1)}, s32[512,1]{0,1:T(1,128)}, u32[]{:S(2)}) copy-start(s32[512,1]{0,1:T(1,128)} %get-tuple-element.149) | copy-start | bytes 6148
  109.0 10.0 %copy-start.80 = (s32[512,1]{0,1:T(1,128)S(1)}, s32[512,1]{0,1:T(1,128)}, u32[]{:S(2)}) copy-start(s32[512,1]{0,1:T(1,128)} %get-tuple-element.134) | copy-start | bytes 6148
  109.0 10.0 %copy-start.81 = (s32[512,1]{0,1:T(1,128)S(1)}, s32[512,1]{0,1:T(1,128)}, u32[]{:S(2)}) copy-start(s32[512,1]{0,1:T(1,128)} %get-tuple-element.135) | copy-start | bytes 6148
  119.0 10.0 %copy-start.72 = (s32[512,1]{0,1:T(1,128)S(1)}, s32[512,1]{0,1:T(1,128)}, u32[]{:S(2)}) copy-start(s32[512,1]{0,1:T(1,128)} %get-tuple-element.126) | copy-start | bytes 6148
  119.0 10.0 %copy-start.73 = (s32[512,1]{0,1:T(1,128)S(1)}, s32[512,1]{0,1:T(1,128)}, u32[]{:S(2)}) copy-start(s32[512,1]{0,1:T(1,128)} %get-tuple-element.127) | copy-start | bytes 6148
  119.0 9.9 %copy-start.74 = (s32[512,1]{0,1:T(1,128)S(1)}, s32[512,1]{0,1:T(1,128)}, u32[]{:S(2)}) copy-start(s32[512,1]{0,1:T(1,128)} %get-tuple-element.128) | copy-start | bytes 6148
  129.0 10.4 %copy-start.64 = (s32[512,1]{0,1:T(1,128)S(1)}, s32[512,1]{0,1:T(1,128)}, u32[]{:S(2)}) copy-start(s32[512,1]{0,1:T(1,128)} %get-tuple-element.118) | copy-start | bytes 6148
  129.0 10.4 %copy-start.65 = (s32[512,1]{0,1:T(1,128)S(1)}, s32[512,1]{0,1:T(1,128)}, u32[]{:S(2)}) copy-start(s32[512,1]{0,1:T(1,128)} %get-tuple-element.119) | copy-start | bytes 6148
  129.0 10.4 %copy-start.66 = (s32[512,1]{0,1:T(1,128)S(1)}, s32[512,1]{0,1:T(1,128)}, u32[]{:S(2)}) copy-start(s32[512,1]{0,1:T(1,128)} %get-tuple-element.120) | copy-start | bytes 6148
  129.1 10.4 %copy-start.67 = (s32[512,1]{0,1:T(1,128)S(1)}, s32[512,1]{0,1:T(1,128)}, u32[]{:S(2)}) copy-start(s32[512,1]{0,1:T(1,128)} %get-tuple-element.121) | copy-start | bytes 6148
  129.1 10.4 %copy-start.68 = (s32[512,1]{0,1:T(1,128)S(1)}, s32[512,1]{0,1:T(1,128)}, u32[]{:S(2)}) copy-start(s32[512,1]{0,1:T(1,128)} %get-tuple-element.122) | copy-start | bytes 6148
  129.1 10.4 %copy-start.69 = (s32[512,1]{0,1:T(1,128)S(1)}, s32[512,1]{0,1:T(1,128)}, u32[]{:S(2)}) copy-start(s32[512,1]{0,1:T(1,128)} %get-tuple-element.123) | copy-start | bytes 6148
  129.1 10.4 %copy-start.70 = (s32[512,1]{0,1:T(1,128)S(1)}, s32[512,1]{0,1:T(1,128)}, u32[]{:S(2)}) copy-start(s32[512,1]{0,1:T(1,128)} %get-tuple-element.124) | copy-start | bytes 6148
  129.1 10.4 %copy-start.71 = (s32[512,1]{0,1:T(1,128)S(1)}, s32[512,1]{0,1:T(1,128)}, u32[]{:S(2)}) copy-start(s32[512,1]{0,1:T(1,128)} %get-tuple-element.125) | copy-start | bytes 6148
  139.5 10.0 %copy-start.56 = (s32[512,1]{0,1:T(1,128)S(1)}, s32[512,1]{0,1:T(1,128)}, u32[]{:S(2)}) copy-start(s32[512,1]{0,1:T(1,128)} %get-tuple-element.110) | copy-start | bytes 6148
  149.5 10.1 %copy-start.48 = (s32[512,1]{0,1:T(1,128)S(1)}, s32[512,1]{0,1:T(1,128)}, u32[]{:S(2)}) copy-start(s32[512,1]{0,1:T(1,128)} %get-tuple-element.102) | copy-start | bytes 6148
  149.5 10.1 %copy-start.49 = (s32[512,1]{0,1:T(1,128)S(1)}, s32[512,1]{0,1:T(1,128)}, u32[]{:S(2)}) copy-start(s32[512,1]{0,1:T(1,128)} %get-tuple-element.103) | copy-start | bytes 6148
  149.5 10.1 %copy-start.50 = (s32[512,1]{0,1:T(1,128)S(1)}, s32[512,1]{0,1:T(1,128)}, u32[]{:S(2)}) copy-start(s32[512,1]{0,1:T(1,128)} %get-tuple-element.104) | copy-start | bytes 6148
  149.6 10.1 %copy-start.51 = (s32[512,1]{0,1:T(1,128)S(1)}, s32[512,1]{0,1:T(1,128)}, u32[]{:S(2)}) copy-start(s32[512,1]{0,1:T(1,128)} %get-tuple-element.105) | copy-start | bytes 6148
  149.6 10.1 %copy-start.52 = (s32[512,1]{0,1:T(1,128)S(1)}, s32[512,1]{0,1:T(1,128)}, u32[]{:S(2)}) copy-start(s32[512,1]{0,1:T(1,128)} %get-tuple-element.106) | copy-start | bytes 6148
  149.6 10.1 %copy-start.53 = (s32[512,1]{0,1:T(1,128)S(1)}, s32[512,1]{0,1:T(1,128)}, u32[]{:S(2)}) copy-start(s32[512,1]{0,1:T(1,128)} %get-tuple-element.107) | copy-start | bytes 6148
  149.6 10.1 %copy-start.54 = (s32[512,1]{0,1:T(1,128)S(1)}, s32[512,1]{0,1:T(1,128)}, u32[]{:S(2)}) copy-start(s32[512,1]{0,1:T(1,128)} %get-tuple-element.108) | copy-start | bytes 6148
  149.6 10.1 %copy-start.55 = (s32[512,1]{0,1:T(1,128)S(1)}, s32[512,1]{0,1:T(1,128)}, u32[]{:S(2)}) copy-start(s32[512,1]{0,1:T(1,128)} %get-tuple-element.109) | copy-start | bytes 6148
  209.7 10.1 %copy-start.27 = (s32[512,1]{0,1:T(1,128)S(1)}, s32[512,1]{0,1:T(1,128)}, u32[]{:S(2)}) copy-start(s32[512,1]{0,1:T(1,128)} %get-tuple-element.54) | copy-start | bytes 6148
  209.7 10.1 %copy-start.28 = (s32[512,1]{0,1:T(1,128)S(1)}, s32[512,1]{0,1:T(1,128)}, u32[]{:S(2)}) copy-start(s32[512,1]{0,1:T(1,128)} %get-tuple-element.55) | copy-start | bytes 6148
  209.7 10.1 %copy-start.29 = (s32[512,1]{0,1:T(1,128)S(1)}, s32[512,1]{0,1:T(1,128)}, u32[]{:S(2)}) copy-start(s32[512,1]{0,1:T(1,128)} %get-tuple-element.56) | copy-start | bytes 6148
  209.7 10.1 %copy-start.30 = (s32[512,1]{0,1:T(1,128)S(1)}, s32[512,1]{0,1:T(1,128)}, u32[]{:S(2)}) copy-start(s32[512,1]{0,1:T(1,128)} %get-tuple-element.57) | copy-start | bytes 6148
  209.7 10.1 %copy-start.31 = (s32[512,1]{0,1:T(1,128)S(1)}, s32[512,1]{0,1:T(1,128)}, u32[]{:S(2)}) copy-start(s32[512,1]{0,1:T(1,128)} %get-tuple-element.58) | copy-start | bytes 6148
  209.7 10.1 %copy-start.32 = (s32[512,1]{0,1:T(1,128)S(1)}, s32[512,1]{0,1:T(1,128)}, u32[]{:S(2)}) copy-start(s32[512,1]{0,1:T(1,128)} %get-tuple-element.59) | copy-start | bytes 6148
  209.7 10.1 %copy-start.33 = (s32[512,1]{0,1:T(1,128)S(1)}, s32[512,1]{0,1:T(1,128)}, u32[]{:S(2)}) copy-start(s32[512,1]{0,1:T(1,128)} %get-tuple-element.60) | copy-start | bytes 6148
  209.7 10.1 %copy-start.34 = (s32[512,1]{0,1:T(1,128)S(1)}, s32[512,1]{0,1:T(1,128)}, u32[]{:S(2)}) copy-start(s32[512,1]{0,1:T(1,128)} %get-tuple-element.61) | copy-start | bytes 6148
  219.8 10.0 %copy-start.19 = (s32[512,1]{0,1:T(1,128)S(1)}, s32[512,1]{0,1:T(1,128)}, u32[]{:S(2)}) copy-start(s32[512,1]{0,1:T(1,128)} %get-tuple-element.46) | copy-start | bytes 6148
  219.8 10.0 %copy-start.20 = (s32[512,1]{0,1:T(1,128)S(1)}, s32[512,1]{0,1:T(1,128)}, u32[]{:S(2)}) copy-start(s32[512,1]{0,1:T(1,128)} %get-tuple-element.47) | copy-start | bytes 6148
  219.8 9.9 %copy-start.21 = (s32[512,1]{0,1:T(1,128)S(1)}, s32[512,1]{0,1:T(1,128)}, u32[]{:S(2)}) copy-start(s32[512,1]{0,1:T(1,128)} %get-tuple-element.48) | copy-start | bytes 6148
  229.9 10.2 %copy-start.11 = (s32[512,1]{0,1:T(1,128)S(1)}, s32[512,1]{0,1:T(1,128)}, u32[]{:S(2)}) copy-start(s32[512,1]{0,1:T(1,128)} %get-tuple-element.38) | copy-start | bytes 6148
  229.9 10.2 %copy-start.12 = (s32[512,1]{0,1:T(1,128)S(1)}, s32[512,1]{0,1:T(1,128)}, u32[]{:S(2)}) copy-start(s32[512,1]{0,1:T(1,128)} %get-tuple-element.39) | copy-start | bytes 6148
  229.9 10.2 %copy-start.13 = (s32[512,1]{0,1:T(1,128)S(1)}, s32[512,1]{0,1:T(1,128)}, u32[]{:S(2)}) copy-start(s32[512,1]{0,1:T(1,128)} %get-tuple-element.40) | copy-start | bytes 6148
  229.9 10.2 %copy-start.14 = (s32[512,1]{0,1:T(1,128)S(1)}, s32[512,1]{0,1:T(1,128)}, u32[]{:S(2)}) copy-start(s32[512,1]{0,1:T(1,128)} %get-tuple-element.41) | copy-start | bytes 6148
  229.9 10.2 %copy-start.15 = (s32[512,1]{0,1:T(1,128)S(1)}, s32[512,1]{0,1:T(1,128)}, u32[]{:S(2)}) copy-start(s32[512,1]{0,1:T(1,128)} %get-tuple-element.42) | copy-start | bytes 6148
  229.9 10.2 %copy-start.16 = (s32[512,1]{0,1:T(1,128)S(1)}, s32[512,1]{0,1:T(1,128)}, u32[]{:S(2)}) copy-start(s32[512,1]{0,1:T(1,128)} %get-tuple-element.43) | copy-start | bytes 6148
  229.9 10.2 %copy-start.17 = (s32[512,1]{0,1:T(1,128)S(1)}, s32[512,1]{0,1:T(1,128)}, u32[]{:S(2)}) copy-start(s32[512,1]{0,1:T(1,128)} %get-tuple-element.44) | copy-start | bytes 6148
  229.9 10.2 %copy-start.18 = (s32[512,1]{0,1:T(1,128)S(1)}, s32[512,1]{0,1:T(1,128)}, u32[]{:S(2)}) copy-start(s32[512,1]{0,1:T(1,128)} %get-tuple-element.45) | copy-start | bytes 6148
  240.1 10.0 %copy-start.35 = (s32[512,1]{0,1:T(1,128)S(1)}, s32[512,1]{0,1:T(1,128)}, u32[]{:S(2)}) copy-start(s32[512,1]{0,1:T(1,128)} %get-tuple-element.30) | copy-start | bytes 6148
  240.1 10.0 %copy-start.36 = (s32[512,1]{0,1:T(1,128)S(1)}, s32[512,1]{0,1:T(1,128)}, u32[]{:S(2)}) copy-start(s32[512,1]{0,1:T(1,128)} %get-tuple-element.31) | copy-start | bytes 6148
  240.1 9.9 %copy-start.37 = (s32[512,1]{0,1:T(1,128)S(1)}, s32[512,1]{0,1:T(1,128)}, u32[]{:S(2)}) copy-start(s32[512,1]{0,1:T(1,128)} %get-tuple-element.32) | copy-start | bytes 6148
  250.1 10.2 %copy-start.3 = (s32[512,1]{0,1:T(1,128)S(1)}, s32[512,1]{0,1:T(1,128)}, u32[]{:S(2)}) copy-start(s32[512,1]{0,1:T(1,128)} %get-tuple-element.22) | copy-start | bytes 6148
  250.1 10.2 %copy-start.4 = (s32[512,1]{0,1:T(1,128)S(1)}, s32[512,1]{0,1:T(1,128)}, u32[]{:S(2)}) copy-start(s32[512,1]{0,1:T(1,128)} %get-tuple-element.23) | copy-start | bytes 6148
  250.1 10.2 %copy-start.5 = (s32[512,1]{0,1:T(1,128)S(1)}, s32[512,1]{0,1:T(1,128)}, u32[]{:S(2)}) copy-start(s32[512,1]{0,1:T(1,128)} %get-tuple-element.24) | copy-start | bytes 6148
  250.1 10.2 %copy-start.6 = (s32[512,1]{0,1:T(1,128)S(1)}, s32[512,1]{0,1:T(1,128)}, u32[]{:S(2)}) copy-start(s32[512,1]{0,1:T(1,128)} %get-tuple-element.25) | copy-start | bytes 6148
  250.2 10.2 %copy-start.7 = (s32[512,1]{0,1:T(1,128)S(1)}, s32[512,1]{0,1:T(1,128)}, u32[]{:S(2)}) copy-start(s32[512,1]{0,1:T(1,128)} %get-tuple-element.26) | copy-start | bytes 6148
  250.2 10.2 %copy-start.8 = (s32[512,1]{0,1:T(1,128)S(1)}, s32[512,1]{0,1:T(1,128)}, u32[]{:S(2)}) copy-start(s32[512,1]{0,1:T(1,128)} %get-tuple-element.27) | copy-start | bytes 6148
  250.2 10.2 %copy-start.9 = (s32[512,1]{0,1:T(1,128)S(1)}, s32[512,1]{0,1:T(1,128)}, u32[]{:S(2)}) copy-start(s32[512,1]{0,1:T(1,128)} %get-tuple-element.28) | copy-start | bytes 6148
  250.2 10.2 %copy-start.10 = (s32[512,1]{0,1:T(1,128)S(1)}, s32[512,1]{0,1:T(1,128)}, u32[]{:S(2)}) copy-start(s32[512,1]{0,1:T(1,128)} %get-tuple-element.29) | copy-start | bytes 6148
  (37 other events, 362.9 us)
Sparse Core Ops, SparseCore 0:
  11.0 73.9 all-gather.1
  290.9 656.9 reduce-scatter.1
where the time goes:
time: 968 us; the launch traced here: 955 us
  waiting for transfers between devices  600 us (62%)
  matrix products  181 us (19%)
  blocking collectives  98.2 us (10%)
  other arithmetic  31.3 us (3%)
  starting transfers between devices  21.3 us (2%)
  between operations  15.6 us (2%)
    reduce_scatter x1, waiting for transfers between devices, per_device(): lax.psum_scatter(whole_term, ('slab', 'dev'), scatter_dimension=0, tiled=...  593 us
    dot_general x16, matrix products, pool_field(): jnp.dot(counts.astype(jnp.bfloat16), cache_all, preferred_element_type=jn...  160 us
    psum x1, blocking collectives, per_device(): grad_w2 = lax.psum(out_term, ('slab', 'dev'))  63.7 us
    all_gather x1, blocking collectives, per_device(): new_rows = lax.all_gather(fresh, ('slab', 'dev'), axis=0, tiled=True)  34.5 us
  transfers between devices with their start and end apart: 4, of which 2 were waited for; matrix products, arithmetic and copies ran while one was open for 21% of the time, Pallas kernels for 0%

commit v1 on v0

v1 whole, which is shorter than its diff:
```python
import jax
import jax.numpy as jnp
from jax import lax
from jax.experimental import pallas as pl
from jax.experimental.pallas import tpu as pltpu
from jax.sharding import Mesh
from jax.sharding import PartitionSpec as P

ALL = ("x", "z", "y", "core")
CHIPS = ("x", "z", "y")
SWAP = ((0, 1), (1, 0))
N_ALL = 128
N_CHIPS = 64
LO = 256
FIELDS = 8
SHIFT = 2.0 ** 24


def split_index(idx, length):
    most, samples = idx.shape
    live = lax.broadcasted_iota(jnp.int32, idx.shape, 0) < length
    low = idx & (LO - 1)
    high = idx >> 8
    unit = jnp.int32(1) << (4 * (high & 7))
    old = jnp.where(live & (high < 8), unit, 0)
    new = jnp.where(live & (high >= 8), unit, 0)
    return low, old, new


def field_counts(word, k):
    if k == FIELDS - 1:
        return lax.shift_right_logical(word, 28).astype(jnp.float32)
    return (word & (15 << (4 * k))).astype(jnp.float32)


def count_kernel(idx_ref, len_ref, told_ref, words_ref, part_ref, low_ref, old_ref, new_ref, c_ref):
    most, samples = idx_ref.shape[1:]
    low, old, new = split_index(idx_ref[0], len_ref[0])
    for j in range(most):
        rows = slice(8 * j, 8 * j + 8)
        low_ref[rows] = jnp.broadcast_to(low[j : j + 1], (8, samples))
        old_ref[rows] = jnp.broadcast_to(old[j : j + 1], (8, samples))
        new_ref[rows] = jnp.broadcast_to(new[j : j + 1], (8, samples))
    line = lax.broadcasted_iota(jnp.int32, (8, 128), 0)

    def chunk(step, carry):
        base = pl.multiple_of(step * 32, 32)
        for lane in range(samples // 128):
            lanes = slice(128 * lane, 128 * lane + 128)
            a_old = [jnp.zeros((8, 128), jnp.int32) for _ in range(4)]
            a_new = [jnp.zeros((8, 128), jnp.int32) for _ in range(4)]
            for j in range(most):
                rows = slice(8 * j, 8 * j + 8)
                lo = low_ref[rows, lanes] - base
                v_old = old_ref[rows, lanes]
                v_new = new_ref[rows, lanes]
                for t in range(4):
                    hit = lo == line + 8 * t
                    a_old[t] = a_old[t] + jnp.where(hit, v_old, 0)
                    a_new[t] = a_new[t] + jnp.where(hit, v_new, 0)
            words_ref[0, pl.ds(base, 32), lanes] = jnp.concatenate(a_new, axis=0)
            word = jnp.concatenate(a_old, axis=0)
            for k in range(FIELDS):
                c_ref[pl.ds(pl.multiple_of(LO * k + base, 32), 32), lanes] = field_counts(word, k).astype(jnp.bfloat16)
        return carry

    lax.fori_loop(0, LO // 32, chunk, 0)
    part_ref[0] = jnp.dot(told_ref[...], c_ref[...], preferred_element_type=jnp.float32)


def count_call(idx, length, told):
    fields, most, samples = idx.shape
    width = told.shape[0]
    return pl.pallas_call(
        count_kernel,
        grid=(fields,),
        in_specs=[
            pl.BlockSpec((1, most, samples), lambda f: (f, 0, 0)),
            pl.BlockSpec((1, 1, samples), lambda f: (f, 0, 0)),
            pl.BlockSpec(told.shape, lambda f: (0, 0)),
        ],
        out_specs=[
            pl.BlockSpec((1, LO, samples), lambda f: (f, 0, 0)),
            pl.BlockSpec((1, width, samples), lambda f: (f, 0, 0)),
        ],
        out_shape=[
            jax.ShapeDtypeStruct((fields, LO, samples), jnp.int32),
            jax.ShapeDtypeStruct((fields, width, samples), jnp.float32),
        ],
        scratch_shapes=[
            pltpu.VMEM((8 * most, samples), jnp.int32),
            pltpu.VMEM((8 * most, samples), jnp.int32),
            pltpu.VMEM((8 * most, samples), jnp.int32),
            pltpu.VMEM((LO * FIELDS, samples), jnp.bfloat16),
        ],
        compiler_params=pltpu.CompilerParams(vmem_limit_bytes=32 * 1024 * 1024),
        cost_estimate=pl.CostEstimate(flops=2 * fields * samples * 2048 * 128, bytes_accessed=20 << 20, transcendentals=0),
        name="count_bags",
    )(idx, length.reshape(fields, 1, samples), told)


def new_kernel(words_ref, part_ref, tnew_ref, pooled_ref, c_ref):
    samples = words_ref.shape[2]

    def chunk(step, carry):
        base = pl.multiple_of(step * 32, 32)
        for lane in range(samples // 128):
            lanes = slice(128 * lane, 128 * lane + 128)
            word = words_ref[0, pl.ds(base, 32), lanes]
            for k in range(FIELDS):
                c_ref[pl.ds(pl.multiple_of(LO * k + base, 32), 32), lanes] = field_counts(word, k).astype(jnp.bfloat16)
        return carry

    lax.fori_loop(0, LO // 32, chunk, 0)
    new = jnp.dot(tnew_ref[...], c_ref[...], preferred_element_type=jnp.float32)
    pooled_ref[...] = ((part_ref[0] + new) * (1.0 / SHIFT)).astype(jnp.bfloat16)


def new_call(words, part, tnew):
    fields, low, samples = words.shape
    width = part.shape[1]
    return pl.pallas_call(
        new_kernel,
        grid=(fields,),
        in_specs=[
            pl.BlockSpec((1, low, samples), lambda f: (f, 0, 0)),
            pl.BlockSpec((1, width, samples), lambda f: (f, 0, 0)),
            pl.BlockSpec(tnew.shape, lambda f: (0, 0)),
        ],
        out_specs=pl.BlockSpec((width, samples), lambda f: (f, 0)),
        out_shape=jax.ShapeDtypeStruct((fields * width, samples), jnp.bfloat16),
        scratch_shapes=[pltpu.VMEM((LO * FIELDS, samples), jnp.bfloat16)],
        compiler_params=pltpu.CompilerParams(vmem_limit_bytes=32 * 1024 * 1024),
        cost_estimate=pl.CostEstimate(flops=2 * fields * samples * 2048 * 128, bytes_accessed=20 << 20, transcendentals=0),
        name="pool_new",
    )(words, part, tnew)


def scaled_columns(rows):
    k = jnp.arange(FIELDS)
    level = jnp.where(k < FIELDS - 1, 2.0 ** (24 - 4.0 * k), 2.0 ** 24).astype(jnp.float32)
    return (rows.astype(jnp.float32).T * jnp.repeat(level, LO)[None, :]).astype(jnp.bfloat16)


def gelu_tanh(values):
    return jax.nn.gelu(values, approximate=True)


def per_device(
    table, accum, evict_delta, evict_ids, hot_ids, cache_old, bag_index, bag_length, labels, w_first, w_out
):
    width = table.shape[1]
    core = lax.axis_index("core")
    half = w_first.shape[1] // 2

    rows = w_first.shape[0]
    mine = lax.dynamic_slice_in_dim(w_first, core * half, half, axis=1)
    other = lax.dynamic_slice_in_dim(w_first, (1 - core) * half, half, axis=1)
    got = lax.ppermute(other, "core", SWAP)
    pair = jnp.where(core == 0, jnp.concatenate([mine, got], axis=0), jnp.concatenate([got, mine], axis=0))
    weight = lax.all_gather(pair, CHIPS, axis=0, tiled=True)

    deltas = evict_delta[0]
    ids = evict_ids[0]
    got_delta = lax.all_to_all(deltas, ALL, split_axis=0, concat_axis=0, tiled=True).reshape(-1, width)
    got_ids = lax.all_to_all(ids, ALL, split_axis=0, concat_axis=0, tiled=True).reshape(-1)

    hot = hot_ids[0]
    hot_table, hot_accum = jnp.take(table, hot, axis=0), jnp.take(accum, hot, axis=0)
    match = (hot[:, None] == got_ids[None, :]).astype(jnp.float32)
    hot_sum = jnp.dot(match, got_delta, precision=lax.Precision.HIGHEST, preferred_element_type=jnp.float32)
    fresh = hot_table - 0.5 * hot_sum * lax.rsqrt(hot_accum + hot_sum * hot_sum)
    fresh = fresh.astype(jnp.bfloat16)
    copies = jnp.broadcast_to(fresh[None], (N_ALL,) + fresh.shape)
    new_rows = lax.all_to_all(copies, ALL, split_axis=0, concat_axis=0, tiled=True).reshape(-1, width)

    words, part = count_call(jnp.transpose(bag_index, (1, 2, 0)), bag_length.T, scaled_columns(cache_old))
    pooled_mine = new_call(words, part, scaled_columns(new_rows))
    pooled_peer = lax.ppermute(pooled_mine, "core", SWAP)
    samples = pooled_mine.shape[1]
    pooled = jnp.concatenate([pooled_mine, pooled_peer], axis=1)
    marks = labels.astype(jnp.float32)
    marks = jnp.concatenate([marks, lax.ppermute(marks, "core", SWAP)])

    out_w = lax.dynamic_slice_in_dim(w_out, core * half, half)
    hidden = lax.dot_general(pooled, weight, (((0,), (0,)), ((), ())), preferred_element_type=jnp.float32)
    act, backward = jax.vjp(gelu_tanh, hidden)
    slope = backward(jnp.ones_like(hidden))[0]
    act_b = act.astype(jnp.bfloat16)
    logit = jnp.dot(act_b, out_w, preferred_element_type=jnp.float32)
    swapped = lax.ppermute(logit, "core", SWAP)
    logit = logit + jnp.concatenate([swapped[samples:], swapped[:samples]])
    grad_logit = 0.125 * (jax.nn.sigmoid(logit) - marks)
    grad_hidden = (grad_logit[:, None] * out_w.astype(jnp.float32)[None, :] * slope).astype(jnp.bfloat16)
    out_term = jnp.dot(grad_logit, act_b.astype(jnp.float32), precision=lax.Precision.HIGHEST)
    whole_term = jnp.dot(pooled, grad_hidden, preferred_element_type=jnp.float32)

    top = out_term.astype(jnp.bfloat16)
    rest = (out_term - top.astype(jnp.float32)).astype(jnp.bfloat16)
    extra = jnp.broadcast_to(jnp.stack([top, rest])[None], (N_CHIPS, 2, half))
    blocks = jnp.concatenate([whole_term.astype(jnp.bfloat16).reshape(N_CHIPS, 2 * rows, half), extra], axis=1)
    terms = lax.all_to_all(blocks, CHIPS, split_axis=0, concat_axis=0, tiled=True)
    total = jnp.sum(terms.astype(jnp.float32), axis=0)
    out_half = total[2 * rows] + total[2 * rows + 1]
    grads = total[: 2 * rows].reshape(2, rows, half)
    keep, give = jnp.where(core == 0, grads[0], grads[1]), jnp.where(core == 0, grads[1], grads[0])
    got = lax.ppermute(jnp.concatenate([give, out_half[None]], axis=0), "core", SWAP)
    left = jnp.where(core == 0, keep, got[:rows])
    right = jnp.where(core == 0, got[:rows], keep)
    grad_w1 = jnp.concatenate([left, right], axis=1)
    grad_w2 = jnp.where(
        core == 0, jnp.concatenate([out_half, got[rows]]), jnp.concatenate([got[rows], out_half])
    )

    summed = jnp.zeros_like(table).at[got_ids].add(got_delta)
    accum_new = accum + summed * summed
    table_new = table - 0.5 * summed * lax.rsqrt(accum_new)
    return (table_new, accum_new, grad_w1, grad_w2)


def solution(mesh):
    fine = Mesh(mesh.devices.reshape(4, 4, 4, 2), ALL)
    placed = (
        P(ALL, None),
        P(ALL, None),
        P(ALL, None, None, None),
        P(ALL, None, None),
        P(ALL, None),
        P(),
        P(ALL, None, None),
        P(ALL, None),
        P(ALL),
        P(ALL, None),
        P(),
    )
    return jax.shard_map(
        per_device,
        mesh=fine,
        in_specs=placed,
        out_specs=(P(ALL, None), P(ALL, None), P(ALL, None), P()),
        check_vma=False,
    )
```

time: 968 us -> 237 us (0.24); the launches traced: 955 us -> 234 us
  waiting for transfers between devices: 600 us -> 96.8 us
  matrix products: 181 us -> 18.1 us
  blocking collectives: 98.2 us -> 0 us
  Pallas kernels: 0 us -> 47.5 us
  other arithmetic: 31.3 us -> 16.8 us
  starting transfers between devices: 21.3 us -> 31 us
    reduce_scatter x1 -> x0, waiting for transfers between devices: 593 us -> none  [per_device(): lax.psum_scatter(whole_term, ('slab', 'dev'), scatter_dimension=0, tiled=...]
    dot_general x20 -> x5, matrix products: 181 us -> 18.1 us  [the longest x1 8.32 us: per_device(): lax.dot_general(pooled, weight, (((0,), (0,)), ((), ())), preferred_eleme...]
    all_to_all x2 -> x4, waiting for transfers between devices: 6.12 us -> 91.1 us  [the longest x1 64.5 us: per_device(): lax.all_to_all(blocks, CHIPS, split_axis=0, concat_axis=0, tiled=True)]
    psum x1 -> x0, blocking collectives: 63.7 us -> none  [per_device(): grad_w2 = lax.psum(out_term, ('slab', 'dev'))]
    pallas_call x0 -> x2, Pallas kernels: none -> 47.5 us  [the longest x1 31.7 us: count_call(): pl.pallas_call(count_kernel, grid=(fields,), in_specs=[pl.BlockSpec((1, m...]
    all_gather x1 -> x0, blocking collectives: 34.5 us -> none  [per_device(): new_rows = lax.all_gather(fresh, ('slab', 'dev'), axis=0, tiled=True)]
    select_n x17 -> x6, other arithmetic: 19.7 us -> 1.94 us  [the longest x1 0.66 us: per_device(): jnp.take(table, hot, axis=0)]
    all_to_all x2 -> x4, starting transfers between devices: 21.3 us -> 25.5 us  [the longest x1 10.4 us: per_device(): lax.all_to_all(ids, ALL, split_axis=0, concat_axis=0, tiled=True)]
  transfers between devices with their start and end apart: 4 -> 10, of which waited for: 2 -> 8; matrix products, arithmetic and copies ran while one was open for 21% -> 8% of each run, Pallas kernels for 0% -> 20%
where the time goes in v1:
time: 237 us; the launch traced here: 234 us
  waiting for transfers between devices  96.8 us (41%)
  Pallas kernels  47.5 us (20%)
  starting transfers between devices  31 us (13%)
  matrix products  18.1 us (8%)
  other arithmetic  16.8 us (7%)
  between operations  14.3 us (6%)
  local copies, waits for them, and re-layouts  9.98 us (4%)
    all_to_all x1, waiting for transfers between devices, per_device(): lax.all_to_all(blocks, CHIPS, split_axis=0, concat_axis=0, tiled=True)  64.5 us
    pallas_call x1, Pallas kernels, count_call(): pl.pallas_call(count_kernel, grid=(fields,), in_specs=[pl.BlockSpec((1, m...  31.7 us
    pallas_call x1, Pallas kernels, new_call(): pl.pallas_call(new_kernel, grid=(fields,), in_specs=[pl.BlockSpec((1, low...  15.8 us
    all_to_all x1, waiting for transfers between devices, per_device(): lax.all_to_all(copies, ALL, split_axis=0, concat_axis=0, tiled=True)  12.1 us
    all_to_all x1, starting transfers between devices, per_device(): lax.all_to_all(ids, ALL, split_axis=0, concat_axis=0, tiled=True)  10.4 us
    all_to_all x1, waiting for transfers between devices, per_device(): lax.all_to_all(ids, ALL, split_axis=0, concat_axis=0, tiled=True)  8.76 us
    dot_general x1, matrix products, per_device(): lax.dot_general(pooled, weight, (((0,), (0,)), ((), ())), preferred_eleme...  8.32 us
    dot_general x1, matrix products, per_device(): jnp.dot(pooled, grad_hidden, preferred_element_type=jnp.float32)  7.28 us
  transfers between devices with their start and end apart: 10, of which 8 were waited for; matrix products, arithmetic and copies ran while one was open for 8% of the time, Pallas kernels for 20%

profile of v1, /device:TPU:1, one launch (start us, length us, event | category | flops | bytes accessed | tf_op | source)
XLA Modules:
  0.0 234.3 jit_solution(1691164457358813004)
XLA Ops:
  7.2 0.0 copy-start.3
  7.2 0.0 all-gather.2.cloned.1.call-start
  7.2 0.8 constant_dynamic-slice_fusion.1
  8.0 1.4 collective-permute-start.1
  9.4 0.9 collective-permute-done.1
  10.3 0.6 maximum_select_fusion
  10.9 0.0 all-gather.2.cloned.1.call-update
  11.0 1.4 copy.21
  12.4 10.4 %all-to-all-start = ((s32[128,1,4]{2,1,0:T(1,128)}), s32[128,1,4]{2,1,0:T(1,128)S(1)}, u32[]{:S(2)}, u32[]{:S(2)}) async-start(s32[128,1,4]{2,1,0:T(1,128)} %bitcast), calls=%async_computation | async-start | bytes 131072 | tf_op jit(solution)/shard_map/all_to_all | solution.py:166
  22.8 0.7 compare_select_fusion.1
  23.5 8.8 %all-to-all-done = s32[128,1,4]{2,1,0:T(1,128)S(1)} async-done(((s32[128,1,4]{2,1,0:T(1,128)}), s32[128,1,4]{2,1,0:T(1,128)S(1)}, u32[]{:S(2)}, u32[]{:S(2)}) %all-to-all-start) | async-done | bytes 2080 | tf_op jit(solution)/shard_map/all_to_all | solution.py:166
  32.2 4.6 %all-to-all-start.1 = ((f32[128,4,128]{2,1,0:T(4,128)}), f32[128,4,128]{2,1,0:T(4,128)S(1)}, u32[]{:S(2)}, u32[]{:S(2)}) async-start(f32[128,4,128]{2,1,0:T(4,128)} %bitcast.38), calls=%async_computation.1 | async-start | bytes 524288 | tf_op jit(solution)/shard_map/all_to_all | solution.py:165
  36.9 2.2 gather_fusion
  39.0 2.2 gather_fusion.1
  41.2 0.7 compare_and_fusion
  41.8 0.1 eq.12
  42.0 5.7 %all-to-all-done.1 = f32[128,4,128]{2,1,0:T(4,128)S(1)} async-done(((f32[128,4,128]{2,1,0:T(4,128)}), f32[128,4,128]{2,1,0:T(4,128)S(1)}, u32[]{:S(2)}, u32[]{:S(2)}) %all-to-all-start.1) | async-done | bytes 262176 | tf_op jit(solution)/shard_map/all_to_all | solution.py:165
  47.6 0.9 fusion.29
  48.5 0.9 broadcast_in_dim.42
  49.4 0.0 copy-start
  49.4 4.8 %all-to-all-start.2 = ((bf16[128,16,128]{2,1,0:T(8,128)(2,1)}), bf16[128,16,128]{2,1,0:T(8,128)(2,1)S(1)}, u32[]{:S(2)}, u32[]{:S(2)}) async-start(bf16[128,16,128]{2,1,0:T(8,128)(2,1)} %broadcast_in_dim.42), calls=%async_computation.2 | async-start | bytes 1048576 | tf_op jit(solution)/shard_map/all_to_all | solution.py:175
  54.2 1.3 copy.22
  55.4 0.1 broadcast_bitcast_fusion
  55.5 0.0 copy-done.3
  55.5 12.1 %all-to-all-done.2 = bf16[128,16,128]{2,1,0:T(8,128)(2,1)S(1)} async-done(((bf16[128,16,128]{2,1,0:T(8,128)(2,1)}), bf16[128,16,128]{2,1,0:T(8,128)(2,1)S(1)}, u32[]{:S(2)}, u32[]{:S(2)}) %all-to-all-start.2) | async-done | bytes 524320 | tf_op jit(solution)/shard_map/all_to_all | solution.py:175
  67.7 0.1 bitcast_convert_fusion
  67.8 0.3 copy.23
  68.1 0.2 fusion.21
  68.3 0.0 copy-done
  68.3 31.7 %count_bags.1 = (s32[16,256,512]{2,1,0:T(8,128)S(1)}, f32[16,128,512]{2,1,0:T(8,128)S(1)}) custom-call(s32[16,8,512]{2,1,0:T(8,128)S(1)} %bitcast.33, s32[16,1,512]{2,1,0:T(1,128)S(1)} %reshape.76.len_ref, bf16[128,2048]{1,0:T(8,128)(2,1)S(1)} %get-tuple-element.20.told_ref), custom_call_target="tpu_custom_call" | custom-call | flops 4294967296 | bytes 20971520 | tf_op jit(solution)/shard_map/count_bags/pallas_call | solution.py:74
  100.0 0.0 copy-start.5
  100.1 15.8 %pool_new.1 = bf16[2048,512]{1,0:T(8,128)(2,1)S(1)} custom-call(s32[16,256,512]{2,1,0:T(8,128)S(1)} %get-tuple-element.7.words_ref, f32[16,128,512]{2,1,0:T(8,128)S(1)} %get-tuple-element.8.part_ref, bf16[128,2048]{1,0:T(8,128)(2,1)S(1)} %get-tuple-element.19.tnew_ref), custom_call_target="tpu_custom_call" | custom-call | flops 4294967296 | bytes 20971520 | tf_op jit(solution)/shard_map/pool_new/pallas_call | solution.py:122
  115.8 1.3 collective-permute-start
  117.2 0.0 copy-done.5
  117.2 0.0 copy-start.4
  117.2 3.9 %collective-permute-done = bf16[2048,512]{1,0:T(8,128)(2,1)} collective-permute-done((bf16[2048,512]{1,0:T(8,128)(2,1)S(1)}, bf16[2048,512]{1,0:T(8,128)(2,1)}, u32[]{:S(2)}, u32[]{:S(2)}) %collective-permute-start) | collective-permute-done | bytes 2097184 | tf_op jit(solution)/shard_map/ppermute | solution.py:179
  121.1 0.0 all-gather.2.cloned.1.call-done
  121.1 8.3 %multiply_convert_fusion = (bf16[1024,1024]{1,0:T(8,128)(2,1)S(1)}, f32[1024,1024]{1,0:T(8,128)S(1)}) fusion(bf16[2048,1024]{1,0:T(8,128)(2,1)} %all-gather.2.cloned.1.call-done, bf16[2048,512]{1,0:T(8,128)(2,1)} %collective-permute-done, bf16[2048,512]{1,0:T(8,128)(2,1)S(1)} %pool_new.1), kind=kOutput, calls=%fused_computation.16 | convolution fusion | flops 4312793088 | bytes 14680064 | tf_op jit(solution)/shard_map/dot_general | solution.py:186
  129.4 0.6 fusion.51
  130.0 0.4 collective-permute-start.2
  130.4 0.0 copy-done.4
  130.4 0.3 collective-permute-start.3
  130.7 0.6 collective-permute-done.2
  131.3 0.3 collective-permute-done.3
  131.6 0.9 fusion.52
  132.6 7.3 %convolution_convert_fusion = bf16[2048,1024]{1,0:T(8,128)(2,1)S(1)} fusion(bf16[2048,512]{1,0:T(8,128)(2,1)} %collective-permute-done, bf16[2048,512]{1,0:T(8,128)(2,1)S(1)} %pool_new.1, f32[1024,1024]{1,0:T(8,128)S(1)} %get-tuple-element.24, f32[1024]{0:T(1024)S(1)} %get-tuple-element.9, f32[1024]{0:T(1024)S(1)} %fusion.37), kind=kOutput, calls=%fused_computation.17 | convolution fusion | flops 4326424576 | bytes 12591104 | tf_op jit(solution)/shard_map/dot_general | solution.py:196
  139.9 0.1 broadcast_in_dim.43
  140.0 3.3 %pad_maximum_fusion = bf16[64,34,1024]{2,1,0:T(8,128)(2,1)} fusion(bf16[64,2,1024]{2,1,0:T(2,128)(2,1)S(1)} %broadcast_in_dim.43, bf16[64,32,1024]{2,1,0:T(8,128)(2,1)S(1)} %bitcast.34), kind=kLoop, calls=%fused_computation.6 | loop fusion | flops 8912896 | bytes 8912896 | tf_op jit(solution)/shard_map/concatenate | solution.py:201
  143.3 5.7 %all-to-all-start.3 = ((bf16[64,34,1024]{2,1,0:T(8,128)(2,1)}), bf16[64,34,1024]{2,1,0:T(8,128)(2,1)}, u32[]{:S(2)}, u32[]{:S(2)}) async-start(bf16[64,34,1024]{2,1,0:T(8,128)(2,1)} %pad_maximum_fusion), calls=%async_computation.3 | async-start | bytes 10485760 | tf_op jit(solution)/shard_map/all_to_all | solution.py:202
  149.0 0.5 broadcast.123
  149.5 0.8 reduce.5
  150.3 0.1 reshape.74
  150.4 2.8 %scatter_custom_fusion = f32[4096,128]{1,0:T(8,128)S(1)} fusion(s32[512]{0:T(512)S(1)} %bitcast.47, f32[512,128]{1,0:T(8,128)S(1)} %bitcast.36, f32[]{:T(128)} %constant.27.clone.1), kind=kCustom, calls=%fused_computation.31 | custom fusion | flops 65536 | bytes 2097156 | tf_op jit(solution)/shard_map/scatter-add | solution.py:215
  153.2 64.5 %all-to-all-done.3 = bf16[64,34,1024]{2,1,0:T(8,128)(2,1)} async-done(((bf16[64,34,1024]{2,1,0:T(8,128)(2,1)}), bf16[64,34,1024]{2,1,0:T(8,128)(2,1)}, u32[]{:S(2)}, u32[]{:S(2)}) %all-to-all-start.3) | async-done | bytes 4456480 | tf_op jit(solution)/shard_map/all_to_all | solution.py:202
  217.7 0.0 copy-start.1
  217.7 0.0 copy-start.2
  217.7 3.9 %convert_reduce_fusion = f32[34,1024]{1,0:T(8,128)S(1)} fusion(bf16[64,34,1024]{2,1,0:T(8,128)(2,1)} %all-to-all-done.3), kind=kLoop, calls=%fused_computation.3 | loop fusion | flops 4421632 | bytes 4595712 | tf_op jit(solution)/shard_map/reduce_sum | solution.py:203
  221.6 2.1 collective-permute-start.4
  223.7 0.0 copy-done.1
  223.7 0.0 copy-done.2
  223.7 2.5 %multiply_subtract_fusion = (f32[4096,128]{1,0:T(8,128)}, f32[4096,128]{1,0:T(8,128)}) fusion(f32[4096,128]{1,0:T(8,128)S(1)} %copy-done.1, f32[4096,128]{1,0:T(8,128)S(1)} %scatter_custom_fusion, f32[4096,128]{1,0:T(8,128)S(1)} %copy-done.2), kind=kLoop, calls=%fused_computation.27 | loop fusion | flops 2621440 | bytes 10485760 | tf_op jit(solution)/shard_map/sub | solution.py:217
  226.2 0.0 collective-permute-done.4
  226.2 0.6 maximum_select_fusion.1
  226.8 0.7 pad_maximum_fusion.4
  (19 shorter events, 0.2 us)
Async XLA Ops:
  7.2 48.3 %copy-start.3 = (s32[512,16]{0,1:T(8,128)S(1)}, s32[512,16]{0,1:T(8,128)}, u32[]{:S(2)}) copy-start(s32[512,16]{0,1:T(8,128)} %param.20) | copy-start | bytes 98308
  7.2 113.9 %all-gather.2.cloned.1.call-start = ((), (), s32[]{:S(2)}) async-start(), calls=%async_computation.4 | async-start | bytes 4259840 | tf_op jit(solution)/shard_map/all_gather | solution.py:161
  8.0 2.3 collective-permute-start.1
  12.4 19.9 %all-to-all-start = ((s32[128,1,4]{2,1,0:T(1,128)}), s32[128,1,4]{2,1,0:T(1,128)S(1)}, u32[]{:S(2)}, u32[]{:S(2)}) async-start(s32[128,1,4]{2,1,0:T(1,128)} %bitcast), calls=%async_computation | async-start | bytes 131072 | tf_op jit(solution)/shard_map/all_to_all | solution.py:166
  32.2 15.4 %all-to-all-start.1 = ((f32[128,4,128]{2,1,0:T(4,128)}), f32[128,4,128]{2,1,0:T(4,128)S(1)}, u32[]{:S(2)}, u32[]{:S(2)}) async-start(f32[128,4,128]{2,1,0:T(4,128)} %bitcast.38), calls=%async_computation.1 | async-start | bytes 524288 | tf_op jit(solution)/shard_map/all_to_all | solution.py:165
  49.4 18.9 %copy-start = (s32[512,16,8]{0,2,1:T(8,128)S(1)}, s32[512,16,8]{0,2,1:T(8,128)}, u32[]{:S(2)}) copy-start(s32[512,16,8]{0,2,1:T(8,128)} %param.19) | copy-start | bytes 786436
  49.4 18.3 %all-to-all-start.2 = ((bf16[128,16,128]{2,1,0:T(8,128)(2,1)}), bf16[128,16,128]{2,1,0:T(8,128)(2,1)S(1)}, u32[]{:S(2)}, u32[]{:S(2)}) async-start(bf16[128,16,128]{2,1,0:T(8,128)(2,1)} %broadcast_in_dim.42), calls=%async_computation.2 | async-start | bytes 1048576 | tf_op jit(solution)/shard_map/all_to_all | solution.py:175
  100.0 17.1 %copy-start.5 = (bf16[2048]{0:T(1024)(128)(2,1)S(1)}, bf16[2048]{0:T(1024)(128)(2,1)}, u32[]{:S(2)}) copy-start(bf16[2048]{0:T(1024)(128)(2,1)} %param.23) | copy-start | bytes 12292
  115.8 5.2 %collective-permute-start = (bf16[2048,512]{1,0:T(8,128)(2,1)S(1)}, bf16[2048,512]{1,0:T(8,128)(2,1)}, u32[]{:S(2)}, u32[]{:S(2)}) collective-permute-start(bf16[2048,512]{1,0:T(8,128)(2,1)S(1)} %pool_new.1), channel_id=1, source_target_pairs={{0,1},{1,0},{2,3},{3,2},{4,5},{5,4},{6,7},{7,6},{8,9},{9,8},{10,11... | collective-permute-start | bytes 6291464 | tf_op jit(solution)/shard_map/ppermute | solution.py:179
  117.2 13.3 %copy-start.4 = (s32[512]{0:T(512)S(1)}, s32[512]{0:T(512)}, u32[]{:S(2)}) copy-start(s32[512]{0:T(512)} %param.21) | copy-start | bytes 6148
  130.0 1.2 collective-permute-start.2
  130.4 1.2 collective-permute-start.3
  143.3 74.4 %all-to-all-start.3 = ((bf16[64,34,1024]{2,1,0:T(8,128)(2,1)}), bf16[64,34,1024]{2,1,0:T(8,128)(2,1)}, u32[]{:S(2)}, u32[]{:S(2)}) async-start(bf16[64,34,1024]{2,1,0:T(8,128)(2,1)} %pad_maximum_fusion), calls=%async_computation.3 | async-start | bytes 10485760 | tf_op jit(solution)/shard_map/all_to_all | solution.py:202
  217.7 6.0 %copy-start.1 = (f32[4096,128]{1,0:T(8,128)S(1)}, f32[4096,128]{1,0:T(8,128)}, u32[]{:S(2)}) copy-start(f32[4096,128]{1,0:T(8,128)} %param.13) | copy-start | bytes 6291460
  217.7 6.0 %copy-start.2 = (f32[4096,128]{1,0:T(8,128)S(1)}, f32[4096,128]{1,0:T(8,128)}, u32[]{:S(2)}) copy-start(f32[4096,128]{1,0:T(8,128)} %param.14) | copy-start | bytes 6291460
  221.6 4.6 %collective-permute-start.4 = (f32[17,1024]{1,0:T(8,128)S(1)}, f32[17,1024]{1,0:T(8,128)S(1)}, u32[]{:S(2)}, u32[]{:S(2)}) collective-permute-start(f32[17,1024]{1,0:T(8,128)S(1)} %pad_maximum_fusion.5), channel_id=1, source_target_pairs={{0,1},{1,0},{2,3},{3,2},{4,5},{5,4},{6,7},{7,6},{8,9},{9,8},{10,11... | collective-permute-start | bytes 208904 | tf_op jit(solution)/shard_map/ppermute | solution.py:207
Sparse Core Ops, SparseCore 0:
  11.5 73.5 all-gather.1

commit v2 on v1

v2 whole, which is shorter than its diff:
```python
import jax
import jax.numpy as jnp
from jax import lax
from jax.experimental import pallas as pl
from jax.experimental.pallas import tpu as pltpu
from jax.sharding import Mesh
from jax.sharding import PartitionSpec as P

ALL = ("x", "z", "y", "core")
CHIPS = ("x", "z", "y")
SWAP = ((0, 1), (1, 0))
N_ALL = 128
N_CHIPS = 64
ROOT = 0.7978845608028654
LO = 256
FIELDS = 8
SPAN = 32
SHIFT = 2.0 ** 24
GROUP = 2


def level_of(k):
    return 2.0 ** (24 - 4 * k) if k < FIELDS - 1 else SHIFT


def scaled_columns(rows):
    level = jnp.array([level_of(k) for k in range(FIELDS)], jnp.float32)
    return (rows.astype(jnp.float32).T * jnp.repeat(level, LO)[None, :]).astype(jnp.bfloat16)


def field_counts(word, k):
    if k == FIELDS - 1:
        return lax.shift_right_logical(word, 28).astype(jnp.float32)
    return (word & (15 << (4 * k))).astype(jnp.float32)


def unpack(word, c_ref, base, lanes):
    for k in range(FIELDS):
        c_ref[LO * k + base : LO * k + base + SPAN, lanes] = field_counts(word, k).astype(jnp.bfloat16)


def overlapped(group, samples, fill, dot, c_a, c_b):
    bufs = (c_a, c_b)
    for g in range(group + 1):
        for lane in range(samples // 128):
            lanes = slice(128 * lane, 128 * lane + 128)
            if g > 0 and lane % 2 == 0:
                dot(g - 1, bufs[(g - 1) % 2], slice(128 * lane, 128 * lane + 256))
            if g < group:
                fill(g, bufs[g % 2], lanes)


def count_kernel(idx_ref, len_ref, told_ref, words_ref, part_ref, low_ref, old_ref, new_ref, c_a, c_b):
    most, samples = idx_ref.shape[1:]
    line = lax.broadcasted_iota(jnp.int32, (8, 128), 0)
    for g in range(GROUP):
        idx = idx_ref[g]
        live = lax.broadcasted_iota(jnp.int32, idx.shape, 0) < len_ref[g]
        high = idx >> 8
        unit = jnp.int32(1) << (4 * (high & 7))
        low = idx & (LO - 1)
        old = jnp.where(live & (high < 8), unit, 0)
        new = jnp.where(live & (high >= 8), unit, 0)
        for j in range(most):
            rows = slice(8 * j, 8 * j + 8)
            low_ref[g, rows] = jnp.broadcast_to(low[j : j + 1], (8, samples))
            old_ref[g, rows] = jnp.broadcast_to(old[j : j + 1], (8, samples))
            new_ref[g, rows] = jnp.broadcast_to(new[j : j + 1], (8, samples))

    def fill(g, c_ref, lanes):
        for base in range(0, LO, SPAN):
            a_old = [jnp.zeros((8, 128), jnp.int32) for _ in range(SPAN // 8)]
            a_new = [jnp.zeros((8, 128), jnp.int32) for _ in range(SPAN // 8)]
            for j in range(most):
                rows = slice(8 * j, 8 * j + 8)
                lo = low_ref[g, rows, lanes] - base
                v_old = old_ref[g, rows, lanes]
                v_new = new_ref[g, rows, lanes]
                for t in range(SPAN // 8):
                    hit = lo == line + 8 * t
                    a_old[t] = a_old[t] + jnp.where(hit, v_old, 0)
                    a_new[t] = a_new[t] + jnp.where(hit, v_new, 0)
            words_ref[g, base : base + SPAN, lanes] = jnp.concatenate(a_new, axis=0)
            unpack(jnp.concatenate(a_old, axis=0), c_ref, base, lanes)

    def dot(g, c_ref, lanes):
        part_ref[g, :, lanes] = jnp.dot(told_ref[...], c_ref[:, lanes], preferred_element_type=jnp.float32)

    overlapped(GROUP, samples, fill, dot, c_a, c_b)


def count_call(idx, length, rows):
    fields, most, samples = idx.shape
    width = rows.shape[1]
    told = scaled_columns(rows)
    return pl.pallas_call(
        count_kernel,
        grid=(fields // GROUP,),
        in_specs=[
            pl.BlockSpec((GROUP, most, samples), lambda f: (f, 0, 0)),
            pl.BlockSpec((GROUP, 1, samples), lambda f: (f, 0, 0)),
            pl.BlockSpec(told.shape, lambda f: (0, 0)),
        ],
        out_specs=[
            pl.BlockSpec((GROUP, LO, samples), lambda f: (f, 0, 0)),
            pl.BlockSpec((GROUP, width, samples), lambda f: (f, 0, 0)),
        ],
        out_shape=[
            jax.ShapeDtypeStruct((fields, LO, samples), jnp.int32),
            jax.ShapeDtypeStruct((fields, width, samples), jnp.float32),
        ],
        scratch_shapes=[
            pltpu.VMEM((GROUP, 8 * most, samples), jnp.int32),
            pltpu.VMEM((GROUP, 8 * most, samples), jnp.int32),
            pltpu.VMEM((GROUP, 8 * most, samples), jnp.int32),
            pltpu.VMEM((LO * FIELDS, samples), jnp.bfloat16),
            pltpu.VMEM((LO * FIELDS, samples), jnp.bfloat16),
        ],
        compiler_params=pltpu.CompilerParams(vmem_limit_bytes=56 * 1024 * 1024),
        cost_estimate=pl.CostEstimate(flops=2 * fields * samples * 2048 * 128, bytes_accessed=20 << 20, transcendentals=0),
        name="count_bags",
    )(idx, length.reshape(fields, 1, samples), told)


def new_kernel(words_ref, part_ref, rows_ref, across_ref, pooled_ref, tnew_ref, c_a, c_b):
    width, samples = part_ref.shape[1:]

    @pl.when(pl.program_id(0) == 0)
    def _():
        for k in range(FIELDS):
            rows = rows_ref[LO * k : LO * k + LO].astype(jnp.float32) * level_of(k)
            tnew_ref[:, LO * k : LO * k + LO] = rows.T.astype(jnp.bfloat16)

    def fill(g, c_ref, lanes):
        for base in range(0, LO, SPAN):
            unpack(words_ref[g, base : base + SPAN, lanes], c_ref, base, lanes)

    def dot(g, c_ref, lanes):
        new = jnp.dot(tnew_ref[...], c_ref[:, lanes], preferred_element_type=jnp.float32)
        both = (part_ref[g, :, lanes] + new) * (1.0 / SHIFT)
        across_ref[width * g : width * g + width, lanes] = both.astype(jnp.bfloat16)
        pooled_ref[lanes, width * g : width * g + width] = both.T.astype(jnp.bfloat16)

    overlapped(GROUP, samples, fill, dot, c_a, c_b)


def new_call(words, part, rows):
    fields, low, samples = words.shape
    width = part.shape[1]
    return pl.pallas_call(
        new_kernel,
        grid=(fields // GROUP,),
        in_specs=[
            pl.BlockSpec((GROUP, low, samples), lambda f: (f, 0, 0)),
            pl.BlockSpec((GROUP, width, samples), lambda f: (f, 0, 0)),
            pl.BlockSpec(rows.shape, lambda f: (0, 0)),
        ],
        out_specs=[
            pl.BlockSpec((width * GROUP, samples), lambda f: (f, 0)),
            pl.BlockSpec((samples, width * GROUP), lambda f: (0, f)),
        ],
        out_shape=[
            jax.ShapeDtypeStruct((fields * width, samples), jnp.bfloat16),
            jax.ShapeDtypeStruct((samples, fields * width), jnp.bfloat16),
        ],
        scratch_shapes=[
            pltpu.VMEM((width, LO * FIELDS), jnp.bfloat16),
            pltpu.VMEM((LO * FIELDS, samples), jnp.bfloat16),
            pltpu.VMEM((LO * FIELDS, samples), jnp.bfloat16),
        ],
        compiler_params=pltpu.CompilerParams(vmem_limit_bytes=56 * 1024 * 1024),
        cost_estimate=pl.CostEstimate(flops=2 * fields * samples * 2048 * 128, bytes_accessed=20 << 20, transcendentals=0),
        name="pool_new",
    )(words, part, rows)


def dense_kernel(own_a, peer_a, own_b, peer_b, weight_ref, out_ref, act_ref, slope_ref, logit_ref):
    step = pl.program_id(0)
    w = out_ref[0].astype(jnp.float32)
    deep = own_a.shape[1]
    for m, (left, right) in enumerate(((own_a, own_b), (peer_a, peer_b))):
        for n in range(left.shape[0] // 256):
            rows = slice(256 * n, 256 * n + 256)
            hidden = jnp.dot(left[rows], weight_ref[:deep], preferred_element_type=jnp.float32)
            hidden = hidden + jnp.dot(right[rows], weight_ref[deep:], preferred_element_type=jnp.float32)
            square = hidden * hidden
            inner = hidden * (ROOT + ROOT * 0.044715 * square)
            t = jnp.tanh(inner)
            near = 0.5 + 0.5 * t
            act = (hidden * near).astype(jnp.bfloat16)
            slope = near + 0.5 * hidden * (1.0 - t * t) * (ROOT + 3.0 * ROOT * 0.044715 * square)
            here = slice(left.shape[0] * m + 256 * n, left.shape[0] * m + 256 * n + 256)
            act_ref[here] = act
            slope_ref[here] = slope * w
            term = jnp.sum(act.astype(jnp.float32) * w, axis=1, keepdims=True)
            logit_ref[here] = jnp.where(step == 0, term, logit_ref[here] + term)


def dense_call(own_a, peer_a, own_b, peer_b, weight, out_w):
    samples, deep = own_a.shape
    wide = weight.shape[1]
    whole = pl.BlockSpec((samples, deep), lambda n: (0, 0))
    return pl.pallas_call(
        dense_kernel,
        grid=(wide // 256,),
        in_specs=[whole, whole, whole, whole]
        + [pl.BlockSpec((2 * deep, 256), lambda n: (0, n)), pl.BlockSpec((1, 1, 256), lambda n: (n, 0, 0))],
        out_specs=[
            pl.BlockSpec((2 * samples, 256), lambda n: (0, n)),
            pl.BlockSpec((2 * samples, 256), lambda n: (0, n)),
            pl.BlockSpec((2 * samples, 1), lambda n: (0, 0)),
        ],
        out_shape=[
            jax.ShapeDtypeStruct((2 * samples, wide), jnp.bfloat16),
            jax.ShapeDtypeStruct((2 * samples, wide), jnp.float32),
            jax.ShapeDtypeStruct((2 * samples, 1), jnp.float32),
        ],
        compiler_params=pltpu.CompilerParams(vmem_limit_bytes=56 * 1024 * 1024),
        cost_estimate=pl.CostEstimate(flops=4 * samples * deep * 2 * wide, bytes_accessed=14 << 20, transcendentals=2 * samples * wide),
        name="dense_forward",
    )(own_a, peer_a, own_b, peer_b, weight, out_w.reshape(wide // 256, 1, 256))


def grad_kernel(own_a, peer_a, own_b, peer_b, act_ref, slope_ref, error_ref, blocks_ref, dh_ref, extra_ref):
    step = pl.program_id(0)
    samples = own_a.shape[1]
    wide = slope_ref.shape[1]

    @pl.when(step == 0)
    def _():
        total = jnp.zeros((8, wide), jnp.float32)
        for n in range(slope_ref.shape[0] // 64):
            rows = slice(64 * n, 64 * n + 64)
            error = error_ref[rows]
            dh_ref[rows] = (error * slope_ref[rows]).astype(jnp.bfloat16)
            weighted = error * act_ref[rows].astype(jnp.float32)
            total = total + jnp.sum(weighted.reshape(8, 8, wide), axis=0)
        total = jnp.sum(total, axis=0, keepdims=True)
        total = jnp.concatenate([total[:, 128 * c : 128 * c + 128] for c in range(wide // 128)], axis=0)
        top = total.astype(jnp.bfloat16).astype(jnp.float32)
        extra_ref[...] = jnp.concatenate([top, total - top], axis=0).astype(jnp.bfloat16)

    def product(own, peer):
        for c in range(wide // 256):
            columns = slice(256 * c, 256 * c + 256)
            term = jnp.dot(own[...], dh_ref[:samples, columns], preferred_element_type=jnp.float32)
            term = term + jnp.dot(peer[...], dh_ref[samples:, columns], preferred_element_type=jnp.float32)
            term = term.astype(jnp.bfloat16)
            for part in range(2):
                piece = term[:, 128 * part : 128 * part + 128].reshape(-1, 16, 128)
                blocks_ref[:, 16 * (2 * c + part) : 16 * (2 * c + part) + 16] = piece

    half = pl.num_programs(0) // 2
    pl.when(step < half)(lambda: product(own_a, peer_a))
    pl.when(step >= half)(lambda: product(own_b, peer_b))
    for d in range(blocks_ref.shape[0]):
        blocks_ref[d, wide // 8 :] = extra_ref[...]


def grad_call(own_a, peer_a, own_b, peer_b, act, slope, error):
    deep, samples = own_a.shape
    wide = act.shape[1]
    steps = 4
    rows = deep // steps
    early = pl.BlockSpec((rows, samples), lambda k: (jnp.minimum(k, steps - 1), 0))
    late = pl.BlockSpec((rows, samples), lambda k: (jnp.maximum(k - steps, 0), 0))
    fixed = lambda a: pl.BlockSpec(a.shape, lambda k: (0, 0))
    tall = wide // 8 + 16
    return pl.pallas_call(
        grad_kernel,
        grid=(2 * steps,),
        in_specs=[early, early, late, late, fixed(act), fixed(slope), fixed(error)],
        out_specs=pl.BlockSpec((rows // 16, tall, 128), lambda k: (k, 0, 0)),
        out_shape=jax.ShapeDtypeStruct((2 * deep // 16, tall, 128), jnp.bfloat16),
        scratch_shapes=[pltpu.VMEM(act.shape, jnp.bfloat16), pltpu.VMEM((16, 128), jnp.bfloat16)],
        compiler_params=pltpu.CompilerParams(vmem_limit_bytes=56 * 1024 * 1024),
        cost_estimate=pl.CostEstimate(flops=8 * samples * deep * wide, bytes_accessed=14 << 20, transcendentals=0),
        name="grad_terms",
    )(own_a, peer_a, own_b, peer_b, act, slope, error)


def per_device(
    table, accum, evict_delta, evict_ids, hot_ids, cache_old, bag_index, bag_length, labels, w_first, w_out
):
    width = table.shape[1]
    cap = evict_ids.shape[2]
    core = lax.axis_index("core")
    half = w_first.shape[1] // 2
    rows = w_first.shape[0]

    numbers = jnp.pad(evict_ids[0].astype(jnp.float32), ((0, 0), (0, width - cap)))[:, None, :]
    blank = jnp.zeros((N_ALL, 8 - cap - 1, width), jnp.float32)
    packet = jnp.concatenate([evict_delta[0], numbers, blank], axis=1)
    got = lax.all_to_all(packet, ALL, split_axis=0, concat_axis=0, tiled=True)

    mine = lax.dynamic_slice_in_dim(w_first, core * half, half, axis=1)
    other = lax.dynamic_slice_in_dim(w_first, (1 - core) * half, half, axis=1)
    swapped = lax.ppermute(other, "core", SWAP)
    pair = jnp.where(
        core == 0, jnp.concatenate([mine, swapped], axis=0), jnp.concatenate([swapped, mine], axis=0)
    )
    weight = lax.all_gather(pair, CHIPS, axis=0, tiled=True)

    index, length = jnp.transpose(bag_index, (1, 2, 0)), bag_length.T
    fields = index.shape[0]
    first = count_call(index[: fields // 2], length[: fields // 2], cache_old)
    got, *first = lax.optimization_barrier((got, *first))
    got_delta = got[:, :cap].reshape(-1, width)
    got_ids = got[:, cap, :cap].astype(jnp.int32).reshape(-1)

    hot = hot_ids[0]
    hot_table, hot_accum = jnp.take(table, hot, axis=0), jnp.take(accum, hot, axis=0)
    match = (hot[:, None] == got_ids[None, :]).astype(jnp.float32)
    hot_sum = jnp.dot(match, got_delta, precision=lax.Precision.HIGHEST, preferred_element_type=jnp.float32)
    fresh = hot_table - 0.5 * hot_sum * lax.rsqrt(hot_accum + hot_sum * hot_sum)
    copies = jnp.broadcast_to(fresh.astype(jnp.bfloat16)[None], (N_ALL,) + fresh.shape)
    new_rows = lax.all_to_all(copies, ALL, split_axis=0, concat_axis=0, tiled=True).reshape(-1, width)

    second = count_call(index[fields // 2 :], length[fields // 2 :], cache_old)
    across, upright = [], []
    for words, part in (first, second):
        own = new_call(words, part, new_rows)
        for side, store in zip(own, (across, upright)):
            store += [side, lax.ppermute(side, "core", SWAP)]
    samples = labels.shape[0]
    marks = labels.astype(jnp.float32)
    marks = jnp.concatenate([marks, lax.ppermute(marks, "core", SWAP)])

    out_w = lax.dynamic_slice_in_dim(w_out, core * half, half)
    act, slope, logit = dense_call(*upright, weight, out_w.astype(jnp.float32))
    logit = logit[:, 0]
    swapped = lax.ppermute(logit, "core", SWAP)
    logit = logit + jnp.concatenate([swapped[samples:], swapped[:samples]])
    error = 0.125 * (jax.nn.sigmoid(logit) - marks)

    blocks = grad_call(*across, act, slope, error[:, None])
    terms = lax.all_to_all(blocks, ALL, split_axis=0, concat_axis=0, tiled=True)
    total = jnp.sum(terms.reshape((N_CHIPS, 2) + terms.shape[1:]).astype(jnp.float32), axis=0)
    grad_w1 = total[:, : half // 8].reshape(2, half // 128, rows, 128).transpose(2, 0, 1, 3).reshape(rows, 2 * half)
    grad_w2 = (total[:, half // 8 : half // 8 + 8] + total[:, half // 8 + 8 :]).reshape(-1)

    summed = jnp.zeros_like(table).at[got_ids].add(got_delta)
    accum_new = accum + summed * summed
    table_new = table - 0.5 * summed * lax.rsqrt(accum_new)
    return (table_new, accum_new, grad_w1, grad_w2)


def solution(mesh):
    fine = Mesh(mesh.devices.reshape(4, 4, 4, 2), ALL)
    placed = (
        P(ALL, None),
        P(ALL, None),
        P(ALL, None, None, None),
        P(ALL, None, None),
        P(ALL, None),
        P(),
        P(ALL, None, None),
        P(ALL, None),
        P(ALL),
        P(ALL, None),
        P(),
    )
    return jax.shard_map(
        per_device,
        mesh=fine,
        in_specs=placed,
        out_specs=(P(ALL, None), P(ALL, None), P(ALL, None), P()),
        check_vma=False,
    )
```

time: 237 us -> 207 us (0.87)
  waiting for transfers between devices: 96.8 us -> 55.1 us
  Pallas kernels: 47.5 us -> 72.2 us
  matrix products: 18.1 us -> 0.23 us
  other arithmetic: 16.8 us -> 19.5 us
    all_to_all x3 -> x2, waiting for transfers between devices: 79 us -> 50.7 us  [the longest x1 50.7 us: per_device(): terms = lax.all_to_all(blocks, ALL, split_axis=0, concat_axis=0, tiled=True)]
    pallas_call x2 -> x6, Pallas kernels: 47.5 us -> 72.2 us  [the longest x2 30.3 us: count_call(): pl.pallas_call(count_kernel, grid=(fields // GROUP,), in_specs=[pl.BlockS...]
    dot_general x4 -> x0, matrix products: 17.2 us -> none  [the longest x1 8.32 us: per_device(): lax.dot_general(pooled, weight, (((0,), (0,)), ((), ())), preferred_eleme...]
    all_to_all x1, waiting for transfers between devices: 12.1 us -> 0.01 us  [per_device(): lax.all_to_all(copies, ALL, split_axis=0, concat_axis=0, tiled=True)]
    all_to_all x1, starting transfers between devices: 4.76 us -> 9.75 us  [per_device(): lax.all_to_all(copies, ALL, split_axis=0, concat_axis=0, tiled=True)]
    ppermute x3 -> x5, starting transfers between devices: 4.79 us -> 3.05 us  [the longest x4 1.63 us: per_device(): store += [side, lax.ppermute(side, 'core', SWAP)]]
    all_to_all x3 -> x2, starting transfers between devices: 20.7 us -> 19.7 us  [the longest x1 10.4 us: per_device(): got = lax.all_to_all(packet, ALL, split_axis=0, concat_axis=0, tiled=True)]
    ppermute x3 -> x5, waiting for transfers between devices: 4.76 us -> 4.24 us  [the longest x4 3.38 us: per_device(): store += [side, lax.ppermute(side, 'core', SWAP)]]
  transfers between devices with their start and end apart: 10 -> 11, of which waited for: 8 -> 5; matrix products, arithmetic and copies ran while one was open for 8% -> 11% of each run, Pallas kernels for 20% -> 23%
where the time goes in v2:
time: 207 us; the launch traced here: 206 us
  Pallas kernels  72.2 us (35%)
  waiting for transfers between devices  55.1 us (27%)
  starting transfers between devices  33.1 us (16%)
  other arithmetic  19.5 us (9%)
  between operations  14.3 us (7%)
  local copies, waits for them, and re-layouts  11.9 us (6%)
    all_to_all x1, waiting for transfers between devices, per_device(): terms = lax.all_to_all(blocks, ALL, split_axis=0, concat_axis=0, tiled=True)  50.7 us
    pallas_call x2, Pallas kernels, count_call(): pl.pallas_call(count_kernel, grid=(fields // GROUP,), in_specs=[pl.BlockS...  30.3 us
    pallas_call x2, Pallas kernels, new_call(): pl.pallas_call(new_kernel, grid=(fields // GROUP,), in_specs=[pl.BlockSpe...  17.9 us
    pallas_call x1, Pallas kernels, grad_call(): pl.pallas_call(grad_kernel, grid=(2 * steps,), in_specs=[early, early, la...  12.4 us
    pallas_call x1, Pallas kernels, dense_call(): pl.pallas_call(dense_kernel, grid=(wide // 256,), in_specs=[whole, whole,...  11.6 us
    all_to_all x1, starting transfers between devices, per_device(): got = lax.all_to_all(packet, ALL, split_axis=0, concat_axis=0, tiled=True)  10.4 us
    all_to_all x1, starting transfers between devices, per_device(): lax.all_to_all(copies, ALL, split_axis=0, concat_axis=0, tiled=True)  9.75 us
    all_to_all x1, starting transfers between devices, per_device(): terms = lax.all_to_all(blocks, ALL, split_axis=0, concat_axis=0, tiled=True)  9.24 us
  transfers between devices with their start and end apart: 11, of which 5 were waited for; matrix products, arithmetic and copies ran while one was open for 11% of the time, Pallas kernels for 23%

profile of v2, /device:TPU:1, one launch (start us, length us, event | category | flops | bytes accessed | tf_op | source)
XLA Modules:
  0.0 206.3 jit_solution(12861546488326948476)
XLA Ops:
  7.2 0.0 copy-start.7
  7.2 0.0 all-gather.2.cloned.1.call-start
  7.3 0.8 constant_dynamic-slice_fusion.1
  8.1 1.4 collective-permute-start.4
  9.5 0.9 collective-permute-done.4
  10.4 0.6 maximum_select_fusion
  11.0 0.0 all-gather.2.cloned.1.call-update
  11.1 0.7 convert_bitcast_fusion
  11.8 0.1 copy.42
  11.9 0.1 pad.15.clone
  11.9 1.9 maximum_maximum_fusion
  13.8 10.4 %all-to-all-start = ((f32[128,8,128]{2,1,0:T(8,128)}), f32[128,8,128]{2,1,0:T(8,128)S(1)}, u32[]{:S(2)}, u32[]{:S(2)}) async-start(f32[128,8,128]{2,1,0:T(8,128)} %maximum_maximum_fusion), calls=%async_computation | async-start | bytes 1048576 | tf_op jit(solution)/shard_map/all_to_all | solution.py:294
  24.2 0.2 copy.43
  24.5 0.0 copy-done.7
  24.5 0.1 broadcast_bitcast_fusion
  24.6 0.6 copy.44.len_ref
  25.2 0.7 fusion.15
  25.9 1.0 fusion.2.told_ref
  26.9 2.2 %gather_fusion = f32[16,128]{1,0:T(8,128)S(1)} fusion(f32[4096,128]{1,0:T(8,128)} %param.15, s32[1024]{0:T(1024)S(1)} %pad_clamp_fusion), kind=kCustom, calls=%fused_computation.clone | custom fusion | bytes 16448 | tf_op jit(solution)/shard_map/jit(_take)/gather | solution.py:312
  29.0 2.2 %gather_fusion.1 = f32[16,128]{1,0:T(8,128)S(1)} fusion(f32[4096,128]{1,0:T(8,128)} %param.16, s32[1024]{0:T(1024)S(1)} %pad_clamp_fusion), kind=kCustom, calls=%fused_computation.1.clone | custom fusion | bytes 16448 | tf_op jit(solution)/shard_map/jit(_take)/gather | solution.py:312
  31.2 15.2 %count_bags.2 = (s32[8,256,512]{2,1,0:T(8,128)}, f32[8,128,512]{2,1,0:T(8,128)}) custom-call(s32[8,8,512]{2,1,0:T(8,128)} %get-tuple-element.36.idx_ref, s32[8,1,512]{2,1,0:T(1,128)} %copy.44.len_ref, bf16[128,2048]{1,0:T(8,128)(2,1)} %fusion.2.told_ref), custom_call_target="tpu_custom_call" | custom-call | flops 2147483648 | bytes 20971520 | tf_op jit(solution)/shard_map/count_bags/pallas_call | solution.py:96
  46.4 0.0 all-to-all-done
  46.4 0.1 slice_convert_fusion
  46.5 0.1 convert_element_type.64
  46.6 0.2 fusion.11
  46.8 0.9 broadcast_in_dim.36
  47.7 9.8 %all-to-all-start.1 = ((bf16[128,16,128]{2,1,0:T(8,128)(2,1)}), bf16[128,16,128]{2,1,0:T(8,128)(2,1)S(1)}, u32[]{:S(2)}, u32[]{:S(2)}) async-start(bf16[128,16,128]{2,1,0:T(8,128)(2,1)} %broadcast_in_dim.36), calls=%async_computation.1 | async-start | bytes 1048576 | tf_op jit(solution)/shard_map/all_to_all | solution.py:317
  57.5 0.6 reshape.82.len_ref
  58.1 15.1 %count_bags.3 = (s32[8,256,512]{2,1,0:T(8,128)}, f32[8,128,512]{2,1,0:T(8,128)}) custom-call(s32[8,8,512]{2,1,0:T(8,128)} %get-tuple-element.35.idx_ref, s32[8,1,512]{2,1,0:T(1,128)} %reshape.82.len_ref, bf16[128,2048]{1,0:T(8,128)(2,1)} %fusion.2.told_ref), custom_call_target="tpu_custom_call" | custom-call | flops 2147483648 | bytes 20971520 | tf_op jit(solution)/shard_map/count_bags/pallas_call | solution.py:96
  73.2 0.0 all-to-all-done.1
  73.2 0.8 copy-done.1
  74.0 9.0 %pool_new.2 = (bf16[1024,512]{1,0:T(8,128)(2,1)}, bf16[512,1024]{1,0:T(8,128)(2,1)}) custom-call(s32[8,256,512]{2,1,0:T(8,128)} %get-tuple-element.22.words_ref, f32[8,128,512]{2,1,0:T(8,128)} %get-tuple-element.23.part_ref, bf16[2048,128]{1,0:T(8,128)(2,1)} %bitcast.42), custom_call_target="tpu_custom_call" | custom-call | flops 2147483648 | bytes 20971520 | tf_op jit(solution)/shard_map/pool_new/pallas_call | solution.py:150
  83.0 1.1 collective-permute-start.2
  84.1 8.9 %pool_new.3 = (bf16[1024,512]{1,0:T(8,128)(2,1)}, bf16[512,1024]{1,0:T(8,128)(2,1)}) custom-call(s32[8,256,512]{2,1,0:T(8,128)} %get-tuple-element.25.words_ref, f32[8,128,512]{2,1,0:T(8,128)} %get-tuple-element.26.part_ref, bf16[2048,128]{1,0:T(8,128)(2,1)} %bitcast.43), custom_call_target="tpu_custom_call" | custom-call | flops 2147483648 | bytes 20971520 | tf_op jit(solution)/shard_map/pool_new/pallas_call | solution.py:150
  93.0 0.0 collective-permute-start.3
  93.0 0.6 dynamic-slice_convert_fusion
  93.6 0.0 collective-permute-done.2.peer_a
  93.6 2.3 %collective-permute-done.3.peer_b = bf16[512,1024]{1,0:T(8,128)(2,1)S(1)} collective-permute-done((bf16[512,1024]{1,0:T(8,128)(2,1)}, bf16[512,1024]{1,0:T(8,128)(2,1)S(1)}, u32[]{:S(2)}, u32[]{:S(2)}) %collective-permute-start.3) | collective-permute-done | bytes 1048608 | tf_op jit(solution)/shard_map/ppermute | solution.py:324
  95.8 1.0 copy-done.10
  96.8 11.6 %dense_forward.1 = (bf16[1024,1024]{1,0:T(8,128)(2,1)}, f32[1024,1024]{1,0:T(8,128)}, f32[1024,1]{1,0:T(8,128)}) custom-call(bf16[512,1024]{1,0:T(8,128)(2,1)} %get-tuple-element.28.own_a, bf16[512,1024]{1,0:T(8,128)(2,1)} %copy-done.9, bf16[512,1024]{1,0:T(8,128)(2,1)} %get-tuple-element.29.own_b, bf16[512,1024]{1,0:T(8,128)(2,1)} %copy-done.10, ...), custom_call_target="tpu_custom_call" | custom-call | flops 4294967296 | bytes 14680064 | tf_op jit(solution)/shard_map/dense_forward/pallas_call | solution.py:203
  108.4 1.2 reduce.2
  109.7 0.2 collective-permute-start.5
  109.9 0.4 collective-permute-start.6
  110.3 0.1 collective-permute-start
  110.4 0.4 collective-permute-start.1
  110.8 0.1 collective-permute-done.5
  110.9 0.2 copy.45
  111.2 1.2 add_divide_fusion
  112.4 0.2 copy.48
  112.6 0.0 collective-permute-done.6
  112.6 0.2 copy.49
  112.8 0.8 broadcast_multiply_fusion.error_ref
  113.7 0.0 collective-permute-done.peer_a
  113.7 1.1 collective-permute-done.1.peer_b
  114.8 12.4 %grad_terms.1 = bf16[128,144,128]{2,1,0:T(8,128)(2,1)} custom-call(bf16[1024,512]{1,0:T(8,128)(2,1)} %get-tuple-element.24.own_a, bf16[1024,512]{1,0:T(8,128)(2,1)} %collective-permute-done.peer_a, bf16[1024,512]{1,0:T(8,128)(2,1)} %get-tuple-element.27.own_b, bf16[1024,512]{1,0:T(8,128)(2,1)} %collective-permute-done.1.peer_b, ...), custom_call_target="tpu_custom_call" | custom-call | flops 4294967296 | bytes 14680064 | tf_op jit(solution)/shard_map/grad_terms/pallas_call | solution.py:269
  127.2 9.2 %all-to-all-start.2 = ((bf16[128,144,128]{2,1,0:T(8,128)(2,1)}), bf16[128,144,128]{2,1,0:T(8,128)(2,1)}, u32[]{:S(2)}, u32[]{:S(2)}) async-start(bf16[128,144,128]{2,1,0:T(8,128)(2,1)} %grad_terms.1), calls=%async_computation.2 | async-start | bytes 9437184 | tf_op jit(solution)/shard_map/all_to_all | solution.py:337
  136.5 0.2 fusion.14
  136.7 0.1 convert_element_type.63
  136.8 2.8 %scatter_custom_fusion = f32[4096,128]{1,0:T(8,128)S(1)} fusion(s32[512]{0:T(512)S(1)} %bitcast.56, f32[512,128]{1,0:T(8,128)S(1)} %bitcast.41, f32[]{:T(128)} %constant.19.clone.1), kind=kCustom, calls=%fused_computation.7 | custom fusion | flops 65536 | bytes 2097156 | tf_op jit(solution)/shard_map/scatter-add | solution.py:342
  139.6 4.7 %multiply_subtract_fusion = (f32[4096,128]{1,0:T(8,128)}, f32[4096,128]{1,0:T(8,128)}) fusion(f32[4096,128]{1,0:T(8,128)} %param.15, f32[4096,128]{1,0:T(8,128)S(1)} %scatter_custom_fusion, f32[4096,128]{1,0:T(8,128)} %param.16), kind=kLoop, calls=%fused_computation.4 | loop fusion | flops 2621440 | bytes 10485760 | tf_op jit(solution)/shard_map/sub | solution.py:344
  144.3 50.7 %all-to-all-done.2 = bf16[128,144,128]{2,1,0:T(8,128)(2,1)} async-done(((bf16[128,144,128]{2,1,0:T(8,128)(2,1)}), bf16[128,144,128]{2,1,0:T(8,128)(2,1)}, u32[]{:S(2)}, u32[]{:S(2)}) %all-to-all-start.2) | async-done | bytes 4718624 | tf_op jit(solution)/shard_map/all_to_all | solution.py:337
  195.0 3.0 %convert_reduce_fusion = f32[2,144,128]{2,1,0:T(8,128)S(1)} fusion(bf16[64,2,144,128]{3,2,1,0:T(8,128)(2,1)} %bitcast.20), kind=kLoop, calls=%fused_computation.3 | loop fusion | flops 4681728 | bytes 4866048 | tf_op jit(solution)/shard_map/reduce_sum | solution.py:338
  198.1 0.6 fusion.7
  198.7 0.7 copy.55
  (34 shorter events, 0.2 us)
Async XLA Ops:
  7.2 17.3 %copy-start.7 = (f32[8]{0:T(128)S(1)}, f32[8]{0:T(128)}, u32[]{:S(2)}) copy-start(f32[8]{0:T(128)} %constant.14.clone) | copy-start | bytes 100
  7.2 17.1 %copy-start = (bf16[2048,128]{1,0:T(8,128)(2,1)S(1)}, bf16[2048,128]{1,0:T(8,128)(2,1)}, u32[]{:S(2)}) copy-start(bf16[2048,128]{1,0:T(8,128)(2,1)} %param.20) | copy-start | bytes 1572868
  7.2 17.4 %copy-start.3 = (s32[512,16]{0,1:T(8,128)S(1)}, s32[512,16]{0,1:T(8,128)}, u32[]{:S(2)}) copy-start(s32[512,16]{0,1:T(8,128)} %param.22) | copy-start | bytes 98308
  7.2 18.0 %copy-start.6 = (s32[1,16]{1,0:T(1,128)S(1)}, s32[1,16]{1,0:T(1,128)}, u32[]{:S(2)}) copy-start(s32[1,16]{1,0:T(1,128)} %param.19) | copy-start | bytes 196
  7.2 18.0 %copy-start.2 = (s32[512,16,8]{0,2,1:T(8,128)S(1)}, s32[512,16,8]{0,2,1:T(8,128)}, u32[]{:S(2)}) copy-start(s32[512,16,8]{0,2,1:T(8,128)} %param.21) | copy-start | bytes 786436
  7.2 88.6 %all-gather.2.cloned.1.call-start = ((), (), s32[]{:S(2)}) async-start(), calls=%async_computation.3 | async-start | bytes 4259840 | tf_op jit(solution)/shard_map/all_gather | solution.py:302
  8.1 2.3 %collective-permute-start.4 = (bf16[16,1024]{1,0:T(8,128)(2,1)S(1)}, bf16[16,1024]{1,0:T(8,128)(2,1)S(1)}, u32[]{:S(2)}, u32[]{:S(2)}) collective-permute-start(bf16[16,1024]{1,0:T(8,128)(2,1)S(1)} %get-tuple-element.38), channel_id=1, source_target_pairs={{0,1},{1,0},{2,3},{3,2},{4,5},{5,4},{6,7},{7,6},{8,9},{9,8},{10,11... | collective-permute-start | bytes 98312 | tf_op jit(solution)/shard_map/ppermute | solution.py:298
  13.8 32.6 %all-to-all-start = ((f32[128,8,128]{2,1,0:T(8,128)}), f32[128,8,128]{2,1,0:T(8,128)S(1)}, u32[]{:S(2)}, u32[]{:S(2)}) async-start(f32[128,8,128]{2,1,0:T(8,128)} %maximum_maximum_fusion), calls=%async_computation | async-start | bytes 1048576 | tf_op jit(solution)/shard_map/all_to_all | solution.py:294
  47.7 25.5 %all-to-all-start.1 = ((bf16[128,16,128]{2,1,0:T(8,128)(2,1)}), bf16[128,16,128]{2,1,0:T(8,128)(2,1)S(1)}, u32[]{:S(2)}, u32[]{:S(2)}) async-start(bf16[128,16,128]{2,1,0:T(8,128)(2,1)} %broadcast_in_dim.36), calls=%async_computation.1 | async-start | bytes 1048576 | tf_op jit(solution)/shard_map/all_to_all | solution.py:317
  73.2 0.8 copy-start.1
  83.0 10.6 %collective-permute-start.2 = (bf16[512,1024]{1,0:T(8,128)(2,1)}, bf16[512,1024]{1,0:T(8,128)(2,1)S(1)}, u32[]{:S(2)}, u32[]{:S(2)}) collective-permute-start(bf16[512,1024]{1,0:T(8,128)(2,1)} %get-tuple-element.28.own_a), channel_id=1, source_target_pairs={{0,1},{1,0},{2,3},{3,2},{4,5},{5,4},{6,7},{7,6},{8,9},{9,8},{10,11... | collective-permute-start | bytes 3145736 | tf_op jit(solution)/shard_map/ppermute | solution.py:324
  84.1 8.9 %copy-start.5 = (bf16[2048]{0:T(1024)(128)(2,1)S(1)}, bf16[2048]{0:T(1024)(128)(2,1)}, u32[]{:S(2)}) copy-start(bf16[2048]{0:T(1024)(128)(2,1)} %param.25) | copy-start | bytes 12292
  93.0 2.9 %collective-permute-start.3 = (bf16[512,1024]{1,0:T(8,128)(2,1)}, bf16[512,1024]{1,0:T(8,128)(2,1)S(1)}, u32[]{:S(2)}, u32[]{:S(2)}) collective-permute-start(bf16[512,1024]{1,0:T(8,128)(2,1)} %get-tuple-element.29.own_b), channel_id=1, source_target_pairs={{0,1},{1,0},{2,3},{3,2},{4,5},{5,4},{6,7},{7,6},{8,9},{9,8},{10,11... | collective-permute-start | bytes 3145736 | tf_op jit(solution)/shard_map/ppermute | solution.py:324
  93.6 3.2 %copy-start.9 = (bf16[512,1024]{1,0:T(8,128)(2,1)}, bf16[512,1024]{1,0:T(8,128)(2,1)S(1)}, u32[]{:S(2)}) copy-start(bf16[512,1024]{1,0:T(8,128)(2,1)S(1)} %collective-permute-done.2.peer_a) | copy-start | bytes 3145732
  95.8 1.0 copy-start.10
  96.8 13.1 %copy-start.4 = (s32[512]{0:T(512)S(1)}, s32[512]{0:T(512)}, u32[]{:S(2)}) copy-start(s32[512]{0:T(512)} %param.23) | copy-start | bytes 6148
  96.8 13.5 %copy-start.8 = (bf16[1024,512]{1,0:T(8,128)(2,1)S(1)}, bf16[1024,512]{1,0:T(8,128)(2,1)}, u32[]{:S(2)}) copy-start(bf16[1024,512]{1,0:T(8,128)(2,1)} %get-tuple-element.24.own_a) | copy-start | bytes 3145732
  109.7 1.2 collective-permute-start.5
  109.9 2.7 %collective-permute-start.6 = (f32[512]{0:T(512)S(1)}, f32[512]{0:T(512)S(1)}, u32[]{:S(2)}, u32[]{:S(2)}) collective-permute-start(f32[512]{0:T(512)S(1)} %convert_element_type.68), channel_id=1, source_target_pairs={{0,1},{1,0},{2,3},{3,2},{4,5},{5,4},{6,7},{7,6},{8,9},{9,8},{10,11... | collective-permute-start | bytes 6152 | tf_op jit(solution)/shard_map/ppermute | solution.py:327
  110.3 3.4 %collective-permute-start = (bf16[1024,512]{1,0:T(8,128)(2,1)S(1)}, bf16[1024,512]{1,0:T(8,128)(2,1)}, u32[]{:S(2)}, u32[]{:S(2)}) collective-permute-start(bf16[1024,512]{1,0:T(8,128)(2,1)S(1)} %copy-done.8), channel_id=1, source_target_pairs={{0,1},{1,0},{2,3},{3,2},{4,5},{5,4},{6,7},{7,6},{8,9},{9,8},{10,11... | collective-permute-start | bytes 3145736 | tf_op jit(solution)/shard_map/ppermute | solution.py:324
  110.4 4.4 %collective-permute-start.1 = (bf16[1024,512]{1,0:T(8,128)(2,1)}, bf16[1024,512]{1,0:T(8,128)(2,1)}, u32[]{:S(2)}, u32[]{:S(2)}) collective-permute-start(bf16[1024,512]{1,0:T(8,128)(2,1)} %get-tuple-element.27.own_b), channel_id=1, source_target_pairs={{0,1},{1,0},{2,3},{3,2},{4,5},{5,4},{6,7},{7,6},{8,9},{9,8},{10,11... | collective-permute-start | bytes 3145736 | tf_op jit(solution)/shard_map/ppermute | solution.py:324
  127.2 67.8 %all-to-all-start.2 = ((bf16[128,144,128]{2,1,0:T(8,128)(2,1)}), bf16[128,144,128]{2,1,0:T(8,128)(2,1)}, u32[]{:S(2)}, u32[]{:S(2)}) async-start(bf16[128,144,128]{2,1,0:T(8,128)(2,1)} %grad_terms.1), calls=%async_computation.2 | async-start | bytes 9437184 | tf_op jit(solution)/shard_map/all_to_all | solution.py:337
Sparse Core Ops, SparseCore 0:
  11.2 73.8 all-gather.1

commit v3 on v2

v3 whole, which is shorter than its diff:
```python
import functools

import jax
import jax.numpy as jnp
from jax import lax
from jax.experimental import pallas as pl
from jax.experimental.pallas import tpu as pltpu
from jax.sharding import Mesh
from jax.sharding import PartitionSpec as P

ALL = ("x", "z", "y", "core")
CHIPS = ("x", "z", "y")
SWAP = ((0, 1), (1, 0))
N_ALL = 128
N_CHIPS = 64
ROOT = 0.7978845608028654
LO = 256
FIELDS = 8
SPAN = 32
SHIFT = 2.0 ** 24
MIB = 1024 * 1024
GROUP = 2


def level_of(k):
    return 2.0 ** (24 - 4 * k) if k < FIELDS - 1 else SHIFT


def scale_columns(rows_ref, columns_ref):
    for k in range(FIELDS):
        rows = rows_ref[LO * k : LO * k + LO].astype(jnp.float32) * level_of(k)
        columns_ref[:, LO * k : LO * k + LO] = rows.T.astype(jnp.bfloat16)


def field_counts(word, k):
    if k == FIELDS - 1:
        return lax.shift_right_logical(word, 28).astype(jnp.float32)
    return (word & (15 << (4 * k))).astype(jnp.float32)


def unpack(word, c_ref, base, lanes):
    for k in range(FIELDS):
        c_ref[LO * k + base : LO * k + base + SPAN, lanes] = field_counts(word, k).astype(jnp.bfloat16)


def overlapped(group, samples, fill, dot, c_a, c_b):
    bufs = (c_a, c_b)
    for g in range(group + 1):
        for lane in range(samples // 128):
            lanes = slice(128 * lane, 128 * lane + 128)
            if g > 0 and lane % 2 == 0:
                dot(g - 1, bufs[(g - 1) % 2], slice(128 * lane, 128 * lane + 256))
            if g < group:
                fill(g, bufs[g % 2], lanes)


def count_kernel(start, idx_ref, len_ref, rows_ref, words_ref, part_ref, told_ref, low_ref, old_ref, new_ref, c_a, c_b):
    most, samples = idx_ref.shape[1:]
    line = lax.broadcasted_iota(jnp.int32, (8, 128), 0)
    first = start + GROUP * pl.program_id(0)
    pl.when(pl.program_id(0) == 0)(lambda: scale_columns(rows_ref, told_ref))
    for g in range(GROUP):
        idx = idx_ref[g]
        live = lax.broadcasted_iota(jnp.int32, idx.shape, 0) < len_ref[pl.ds(first + g, 1)]
        high = idx >> 8
        unit = jnp.int32(1) << (4 * (high & 7))
        low = idx & (LO - 1)
        old = jnp.where(live & (high < 8), unit, 0)
        new = jnp.where(live & (high >= 8), unit, 0)
        for j in range(most):
            rows = slice(8 * j, 8 * j + 8)
            low_ref[g, rows] = jnp.broadcast_to(low[j : j + 1], (8, samples))
            old_ref[g, rows] = jnp.broadcast_to(old[j : j + 1], (8, samples))
            new_ref[g, rows] = jnp.broadcast_to(new[j : j + 1], (8, samples))

    def fill(g, c_ref, lanes):
        for base in range(0, LO, SPAN):
            a_old = [jnp.zeros((8, 128), jnp.int32) for _ in range(SPAN // 8)]
            a_new = [jnp.zeros((8, 128), jnp.int32) for _ in range(SPAN // 8)]
            for j in range(most):
                rows = slice(8 * j, 8 * j + 8)
                lo = low_ref[g, rows, lanes] - base
                v_old = old_ref[g, rows, lanes]
                v_new = new_ref[g, rows, lanes]
                for t in range(SPAN // 8):
                    hit = lo == line + 8 * t
                    a_old[t] = a_old[t] + jnp.where(hit, v_old, 0)
                    a_new[t] = a_new[t] + jnp.where(hit, v_new, 0)
            words_ref[g, base : base + SPAN, lanes] = jnp.concatenate(a_new, axis=0)
            unpack(jnp.concatenate(a_old, axis=0), c_ref, base, lanes)

    def dot(g, c_ref, lanes):
        part_ref[g, :, lanes] = jnp.dot(told_ref[...], c_ref[:, lanes], preferred_element_type=jnp.float32)

    overlapped(GROUP, samples, fill, dot, c_a, c_b)


def count_call(idx, length, rows, start, fields):
    _, most, samples = idx.shape
    width = rows.shape[1]
    return pl.pallas_call(
        functools.partial(count_kernel, start),
        grid=(fields // GROUP,),
        in_specs=[
            pl.BlockSpec((GROUP, most, samples), lambda f: (f + start // GROUP, 0, 0)),
            pl.BlockSpec(length.shape, lambda f: (0, 0)),
            pl.BlockSpec(rows.shape, lambda f: (0, 0)),
        ],
        out_specs=[
            pl.BlockSpec((GROUP, LO, samples), lambda f: (f, 0, 0)),
            pl.BlockSpec((GROUP, width, samples), lambda f: (f, 0, 0)),
        ],
        out_shape=[
            jax.ShapeDtypeStruct((fields, LO, samples), jnp.int32),
            jax.ShapeDtypeStruct((fields, width, samples), jnp.float32),
        ],
        scratch_shapes=[
            pltpu.VMEM((width, LO * FIELDS), jnp.bfloat16),
            pltpu.VMEM((GROUP, 8 * most, samples), jnp.int32),
            pltpu.VMEM((GROUP, 8 * most, samples), jnp.int32),
            pltpu.VMEM((GROUP, 8 * most, samples), jnp.int32),
            pltpu.VMEM((LO * FIELDS, samples), jnp.bfloat16),
            pltpu.VMEM((LO * FIELDS, samples), jnp.bfloat16),
        ],
        compiler_params=pltpu.CompilerParams(vmem_limit_bytes=56 * MIB),
        cost_estimate=pl.CostEstimate(flops=2 * fields * samples * 2048 * 128, bytes_accessed=20 << 20, transcendentals=0),
        name="count_bags",
    )(idx, length, rows)


def new_kernel(words_ref, part_ref, rows_ref, across_ref, pooled_ref, tnew_ref, c_a, c_b):
    width, samples = part_ref.shape[1:]

    pl.when(pl.program_id(0) == 0)(lambda: scale_columns(rows_ref, tnew_ref))

    def fill(g, c_ref, lanes):
        for base in range(0, LO, SPAN):
            unpack(words_ref[g, base : base + SPAN, lanes], c_ref, base, lanes)

    def dot(g, c_ref, lanes):
        new = jnp.dot(tnew_ref[...], c_ref[:, lanes], preferred_element_type=jnp.float32)
        both = (part_ref[g, :, lanes] + new) * (1.0 / SHIFT)
        across_ref[width * g : width * g + width, lanes] = both.astype(jnp.bfloat16)
        pooled_ref[lanes, width * g : width * g + width] = both.T.astype(jnp.bfloat16)

    overlapped(GROUP, samples, fill, dot, c_a, c_b)


def new_call(words, part, rows):
    fields, low, samples = words.shape
    width = part.shape[1]
    return pl.pallas_call(
        new_kernel,
        grid=(fields // GROUP,),
        in_specs=[
            pl.BlockSpec((GROUP, low, samples), lambda f: (f, 0, 0)),
            pl.BlockSpec((GROUP, width, samples), lambda f: (f, 0, 0)),
            pl.BlockSpec(rows.shape, lambda f: (0, 0)),
        ],
        out_specs=[
            pl.BlockSpec((width * GROUP, samples), lambda f: (f, 0)),
            pl.BlockSpec((samples, width * GROUP), lambda f: (0, f)),
        ],
        out_shape=[
            jax.ShapeDtypeStruct((fields * width, samples), jnp.bfloat16),
            jax.ShapeDtypeStruct((samples, fields * width), jnp.bfloat16),
        ],
        scratch_shapes=[
            pltpu.VMEM((width, LO * FIELDS), jnp.bfloat16),
            pltpu.VMEM((LO * FIELDS, samples), jnp.bfloat16),
            pltpu.VMEM((LO * FIELDS, samples), jnp.bfloat16),
        ],
        compiler_params=pltpu.CompilerParams(vmem_limit_bytes=56 * MIB),
        cost_estimate=pl.CostEstimate(flops=2 * fields * samples * 2048 * 128, bytes_accessed=20 << 20, transcendentals=0),
        name="pool_new",
    )(words, part, rows)


def hot_kernel(ids_ref, got_ref, hot_ref, table_ref, accum_ref, copies_ref, rows_ref, sems):
    count = ids_ref.shape[1]
    cap = 4
    fetches = []
    for k in range(count):
        row = pl.ds(ids_ref[0, k], 1)
        for which, ref in enumerate((table_ref, accum_ref)):
            fetch = pltpu.make_async_copy(ref.at[row], rows_ref.at[which, pl.ds(k, 1)], sems.at[which, k])
            fetch.start()
            fetches.append(fetch)
    got = got_ref[...]
    total = jnp.zeros((128, 128), jnp.float32)
    for c in range(cap):
        match = (got[:, cap, c : c + 1] == hot_ref[...]).astype(jnp.float32)
        total = total + lax.dot_general(
            match, got[:, c], (((0,), (0,)), ((), ())), precision=lax.Precision.HIGHEST, preferred_element_type=jnp.float32
        )
    total = total[:count]
    for fetch in fetches:
        fetch.wait()
    fresh = rows_ref[0] - 0.5 * total * lax.rsqrt(rows_ref[1] + total * total)
    fresh = fresh.astype(jnp.bfloat16)

    def place(d, carry):
        copies_ref[d] = fresh
        return carry

    lax.fori_loop(0, copies_ref.shape[0], place, 0)


def hot_call(got, ids, table, accum):
    count = ids.shape[1]
    hot = jnp.pad(ids.astype(jnp.float32), ((0, 0), (0, 128 - count)), constant_values=-1.0)
    inside = pl.BlockSpec(memory_space=pltpu.VMEM)
    return pl.pallas_call(
        hot_kernel,
        in_specs=[
            pl.BlockSpec(memory_space=pltpu.SMEM),
            inside,
            inside,
            pl.BlockSpec(memory_space=pltpu.HBM),
            pl.BlockSpec(memory_space=pltpu.HBM),
        ],
        out_specs=inside,
        out_shape=jax.ShapeDtypeStruct((N_ALL, count, 128), jnp.bfloat16),
        scratch_shapes=[pltpu.VMEM((2, count, 128), jnp.float32), pltpu.SemaphoreType.DMA((2, count))],
        compiler_params=pltpu.CompilerParams(vmem_limit_bytes=56 * MIB),
        cost_estimate=pl.CostEstimate(flops=4 * 128**3 * 12, bytes_accessed=1 << 20, transcendentals=count * 128),
        name="hot_rows",
    )(ids, got, hot, table, accum)


def dense_kernel(
    core_ref, own_a, peer_a, own_b, peer_b, weight_ref, out_ref, act_ref, slope_ref, logit_ref,
    sum_ref, side_ref, columns_ref, act_v, slope_v, sems, out_sems,
):
    samples, deep = own_a.shape
    steps = columns_ref.shape[0]
    fetch_columns = []
    for n in range(steps):
        columns = pl.ds(pl.multiple_of(core_ref[0] * (256 * steps) + 256 * n, 256), 256)
        fetch_columns.append(pltpu.make_async_copy(weight_ref.at[:, columns], columns_ref.at[n], sems.at[n]))
    fetch_sides = [
        pltpu.make_async_copy(side, side_ref.at[i], sems.at[steps + i])
        for i, side in enumerate((own_a, own_b, peer_a, peer_b))
    ]
    for fetch in fetch_columns[:1] + fetch_sides + fetch_columns[1:]:
        fetch.start()
    sent = []
    for n in range(steps):
        fetch_columns[n].wait()
        w = out_ref[:, 256 * n : 256 * n + 256]
        for m in range(2):
            if n == 0:
                fetch_sides[2 * m].wait()
                fetch_sides[2 * m + 1].wait()
            hidden = jnp.dot(side_ref[2 * m], columns_ref[n, :deep], preferred_element_type=jnp.float32)
            hidden = hidden + jnp.dot(side_ref[2 * m + 1], columns_ref[n, deep:], preferred_element_type=jnp.float32)
            square = hidden * hidden
            t = jnp.tanh(hidden * (ROOT + ROOT * 0.044715 * square))
            near = 0.5 + 0.5 * t
            act = (hidden * near).astype(jnp.bfloat16)
            slope = near + 0.5 * hidden * (1.0 - t * t) * (ROOT + 3.0 * ROOT * 0.044715 * square)
            here = slice(samples * m, samples * m + samples)
            act_v[n, here] = act
            slope_v[n, here] = slope * w
            term = act.astype(jnp.float32) * w
            term = term[:, :128] + term[:, 128:]
            sum_ref[here] = term if n == 0 else sum_ref[here] + term
        for i, (store, target) in enumerate(((act_v, act_ref), (slope_v, slope_ref))):
            send = pltpu.make_async_copy(store.at[n], target.at[n], out_sems.at[i, n])
            send.start()
            sent.append(send)
    ones = jnp.ones((8, 128), jnp.float32)
    for b in range(logit_ref.shape[0]):
        term = sum_ref[128 * b : 128 * b + 128]
        line = lax.dot_general(
            ones, term, (((1,), (1,)), ((), ())), precision=lax.Precision.HIGHEST, preferred_element_type=jnp.float32
        )
        logit_ref[b : b + 1] = line[:1]
    for send in sent:
        send.wait()


def dense_call(core, own_a, peer_a, own_b, peer_b, weight, out_w):
    samples, deep = own_a.shape
    wide = out_w.shape[0]
    steps = wide // 256
    far = pl.BlockSpec(memory_space=pltpu.HBM)
    inside = pl.BlockSpec(memory_space=pltpu.VMEM)
    return pl.pallas_call(
        dense_kernel,
        in_specs=[pl.BlockSpec(memory_space=pltpu.SMEM)] + [far] * 5 + [inside],
        out_specs=[far, far, inside],
        out_shape=[
            jax.ShapeDtypeStruct((steps, 2 * samples, 256), jnp.bfloat16),
            jax.ShapeDtypeStruct((steps, 2 * samples, 256), jnp.float32),
            jax.ShapeDtypeStruct((2 * samples // 128, 128), jnp.float32),
        ],
        scratch_shapes=[
            pltpu.VMEM((2 * samples, 128), jnp.float32),
            pltpu.VMEM((4, samples, deep), jnp.bfloat16),
            pltpu.VMEM((steps, 2 * deep, 256), jnp.bfloat16),
            pltpu.VMEM((steps, 2 * samples, 256), jnp.bfloat16),
            pltpu.VMEM((steps, 2 * samples, 256), jnp.float32),
            pltpu.SemaphoreType.DMA((steps + 4,)),
            pltpu.SemaphoreType.DMA((2, steps)),
        ],
        compiler_params=pltpu.CompilerParams(vmem_limit_bytes=56 * MIB),
        cost_estimate=pl.CostEstimate(flops=4 * samples * deep * 2 * wide, bytes_accessed=14 << 20, transcendentals=2 * samples * wide),
        name="dense_forward",
    )(core.reshape(1), own_a, peer_a, own_b, peer_b, weight, out_w.reshape(1, wide))


def grad_kernel(
    own_a, peer_a, own_b, peer_b, act_ref, slope_ref, logit_ref, swapped_ref, marks_ref, out_ref,
    side_ref, act_v, slope_v, dh_ref, blocks_ref, sems, out_sems,
):
    deep, samples = own_a.shape
    steps = act_ref.shape[0]
    tall = blocks_ref.shape[1]
    fetch_dense = [
        [pltpu.make_async_copy(act_ref.at[n], act_v.at[n], sems.at[2 * n]), pltpu.make_async_copy(slope_ref.at[n], slope_v.at[n], sems.at[2 * n + 1])]
        for n in range(steps)
    ]
    fetch_sides = [
        pltpu.make_async_copy(side, side_ref.at[i], sems.at[2 * steps + i])
        for i, side in enumerate((own_a, peer_a, own_b, peer_b))
    ]
    for fetch in fetch_dense[0] + fetch_sides + [f for pair in fetch_dense[1:] for f in pair]:
        fetch.start()
    own_rows = samples // 128
    logit = logit_ref[...] + jnp.concatenate([swapped_ref[own_rows:], swapped_ref[:own_rows]], axis=0)
    error = (0.125 * (jax.nn.sigmoid(logit) - marks_ref[...])).T
    sent = []
    lines = []
    for c in range(steps):
        for fetch in fetch_dense[c]:
            fetch.wait()
        total = jnp.zeros((8, 256), jnp.float32)
        for b in range(2 * own_rows):
            rows = slice(128 * b, 128 * b + 128)
            column = error[:, b : b + 1]
            dh_ref[c, rows] = (column * slope_v[c, rows]).astype(jnp.bfloat16)
            weighted = column * act_v[c, rows].astype(jnp.float32)
            total = total + jnp.sum(weighted.reshape(16, 8, 256), axis=0)
        total = jnp.sum(total, axis=0, keepdims=True)
        lines += [total[:, :128], total[:, 128:]]
        if c == steps - 1:
            total = jnp.concatenate(lines, axis=0)
            top = total.astype(jnp.bfloat16).astype(jnp.float32)
            extra = jnp.concatenate([top, total - top], axis=0).astype(jnp.bfloat16)

            def place(d, carry):
                blocks_ref[d, 32 * steps :] = extra
                return carry

            lax.fori_loop(0, blocks_ref.shape[0], place, 0)
        for side in range(2):
            if c == 0:
                fetch_sides[2 * side].wait()
                fetch_sides[2 * side + 1].wait()
            term = jnp.dot(side_ref[2 * side], dh_ref[c, :samples], preferred_element_type=jnp.float32)
            term = term + jnp.dot(side_ref[2 * side + 1], dh_ref[c, samples:], preferred_element_type=jnp.float32)
            term = term.astype(jnp.bfloat16)
            blocks = pl.ds(side * (deep // 16), deep // 16)
            for part in range(2):
                at = 32 * c + 16 * part
                blocks_ref[blocks, at : at + 16] = term[:, 128 * part : 128 * part + 128].reshape(-1, 16, 128)
            span = pl.ds(32 * c, (tall - 32 * c) if c == steps - 1 else 32)
            send = pltpu.make_async_copy(blocks_ref.at[blocks, span], out_ref.at[blocks, span], out_sems.at[side, c])
            send.start()
            sent.append(send)
    for send in sent:
        send.wait()


def grad_call(own_a, peer_a, own_b, peer_b, act, slope, logit, swapped, marks):
    deep, samples = own_a.shape
    steps = act.shape[0]
    far = pl.BlockSpec(memory_space=pltpu.HBM)
    inside = pl.BlockSpec(memory_space=pltpu.VMEM)
    shape = (2 * deep // 16, 32 * steps + 16, 128)
    return pl.pallas_call(
        grad_kernel,
        in_specs=[far] * 6 + [inside] * 3,
        out_specs=far,
        out_shape=jax.ShapeDtypeStruct(shape, jnp.bfloat16),
        scratch_shapes=[
            pltpu.VMEM((4, deep, samples), jnp.bfloat16),
            pltpu.VMEM(act.shape, jnp.bfloat16),
            pltpu.VMEM(slope.shape, jnp.float32),
            pltpu.VMEM(act.shape, jnp.bfloat16),
            pltpu.VMEM(shape, jnp.bfloat16),
            pltpu.SemaphoreType.DMA((2 * steps + 4,)),
            pltpu.SemaphoreType.DMA((2, steps)),
        ],
        compiler_params=pltpu.CompilerParams(vmem_limit_bytes=56 * MIB),
        cost_estimate=pl.CostEstimate(flops=8 * samples * deep * 256 * steps, bytes_accessed=14 << 20, transcendentals=0),
        name="grad_terms",
    )(own_a, peer_a, own_b, peer_b, act, slope, logit, swapped, marks)


def per_device(
    table, accum, evict_delta, evict_ids, hot_ids, cache_old, bag_index, bag_length, labels, w_first, w_out
):
    width = table.shape[1]
    cap = evict_ids.shape[2]
    core = lax.axis_index("core")
    half = w_first.shape[1] // 2
    rows = w_first.shape[0]

    numbers = jnp.pad(evict_ids[0].astype(jnp.float32), ((0, 0), (0, width - cap)))[:, None, :]
    blank = jnp.zeros((N_ALL, 8 - cap - 1, width), jnp.float32)
    packet = jnp.concatenate([evict_delta[0], numbers, blank], axis=1)
    got = lax.all_to_all(packet, ALL, split_axis=0, concat_axis=0, tiled=True)

    weight = lax.all_gather(w_first, ALL, axis=0, tiled=True)

    index, length = jnp.transpose(bag_index, (1, 2, 0)), bag_length.T
    fields = index.shape[0]
    first = count_call(index, length, cache_old, 0, fields // 2)
    got, *first = lax.optimization_barrier((got, *first))
    got_delta = got[:, :cap].reshape(-1, width)
    got_ids = got[:, cap, :cap].astype(jnp.int32).reshape(-1)

    copies = hot_call(got, hot_ids, table, accum)
    new_rows = lax.all_to_all(copies, ALL, split_axis=0, concat_axis=0, tiled=True).reshape(-1, width)

    second = count_call(index, length, cache_old, fields // 2, fields // 2)
    across, upright = [], []
    for words, part in (first, second):
        own = new_call(words, part, new_rows)
        for side, store in zip(own, (across, upright)):
            store += [side, lax.ppermute(side, "core", SWAP)]
    marks = labels.astype(jnp.float32).reshape(-1, 128)
    marks = jnp.concatenate([marks, lax.ppermute(marks, "core", SWAP)], axis=0)

    out_w = lax.dynamic_slice_in_dim(w_out, core * half, half)
    act, slope, logit = dense_call(core, *upright, weight, out_w.astype(jnp.float32))
    swapped = lax.ppermute(logit, "core", SWAP)

    blocks = grad_call(*across, act, slope, logit, swapped, marks)
    terms = lax.all_to_all(blocks, ALL, split_axis=0, concat_axis=0, tiled=True)
    total = jnp.sum(terms.reshape((N_CHIPS, 2) + terms.shape[1:]).astype(jnp.float32), axis=0)
    grad_w1 = total[:, : half // 8].reshape(2, half // 128, rows, 128).transpose(2, 0, 1, 3).reshape(rows, 2 * half)
    grad_w2 = (total[:, half // 8 : half // 8 + 8] + total[:, half // 8 + 8 :]).reshape(-1)

    summed = jnp.zeros_like(table).at[got_ids].add(got_delta)
    accum_new = accum + summed * summed
    table_new = table - 0.5 * summed * lax.rsqrt(accum_new)
    return (table_new, accum_new, grad_w1, grad_w2)


def solution(mesh):
    fine = Mesh(mesh.devices.reshape(4, 4, 4, 2), ALL)
    placed = (
        P(ALL, None),
        P(ALL, None),
        P(ALL, None, None, None),
        P(ALL, None, None),
        P(ALL, None),
        P(),
        P(ALL, None, None),
        P(ALL, None),
        P(ALL),
        P(ALL, None),
        P(),
    )
    return jax.shard_map(
        per_device,
        mesh=fine,
        in_specs=placed,
        out_specs=(P(ALL, None), P(ALL, None), P(ALL, None), P()),
        check_vma=False,
    )
```

time: 207 us -> 198 us (0.957)
  local copies, waits for them, and re-layouts: 11.9 us -> 4.57 us
  Pallas kernels: 72.2 us -> 77.6 us
  other arithmetic: 19.5 us -> 15.2 us
    pallas_call x4 -> x5, Pallas kernels: 54.3 us -> 59.2 us  [the longest x2 30.8 us: count_call(): pl.pallas_call(functools.partial(count_kernel, start), grid=(fields // GR...]
    gather x2 -> x0, local copies, waits for them, and re-layouts: 4.32 us -> none  [the longest x1 2.17 us: per_device(): jnp.take(accum, hot, axis=0)]
  transfers between devices with their start and end apart: 11 -> 10, of which waited for: 5 -> 3; matrix products, arithmetic and copies ran while one was open for 11% -> 7% of each run, Pallas kernels for 23% -> 33%
where the time goes in v3:
time: 198 us; the launch traced here: 197 us
  Pallas kernels  77.6 us (39%)
  waiting for transfers between devices  54.1 us (27%)
  starting transfers between devices  31.8 us (16%)
  other arithmetic  15.2 us (8%)
  between operations  14.2 us (7%)
  local copies, waits for them, and re-layouts  4.57 us (2%)
    all_to_all x1, waiting for transfers between devices, per_device(): terms = lax.all_to_all(blocks, ALL, split_axis=0, concat_axis=0, tiled=True)  49.9 us
    pallas_call x2, Pallas kernels, count_call(): pl.pallas_call(functools.partial(count_kernel, start), grid=(fields // GR...  30.8 us
    pallas_call x2, Pallas kernels, new_call(): pl.pallas_call(new_kernel, grid=(fields // GROUP,), in_specs=[pl.BlockSpe...  18.4 us
    pallas_call x1, Pallas kernels, dense_call(): pl.pallas_call(dense_kernel, in_specs=[pl.BlockSpec(memory_space=pltpu.SM...  12.9 us
    all_to_all x1, starting transfers between devices, per_device(): got = lax.all_to_all(packet, ALL, split_axis=0, concat_axis=0, tiled=True)  11.5 us
    pallas_call x1, Pallas kernels, grad_call(): pl.pallas_call(grad_kernel, in_specs=[far] * 6 + [inside] * 3, out_specs=...  11.5 us
    all_to_all x1, starting transfers between devices, per_device(): lax.all_to_all(copies, ALL, split_axis=0, concat_axis=0, tiled=True)  9.77 us
    all_to_all x1, starting transfers between devices, per_device(): terms = lax.all_to_all(blocks, ALL, split_axis=0, concat_axis=0, tiled=True)  8.42 us
  transfers between devices with their start and end apart: 10, of which 3 were waited for; matrix products, arithmetic and copies ran while one was open for 7% of the time, Pallas kernels for 33%

profile of v3, /device:TPU:1, one launch (start us, length us, event | category | flops | bytes accessed | tf_op | source)
XLA Modules:
  0.0 197.4 jit_solution(2367162574506866209)
XLA Ops:
  7.2 0.0 copy-start.6
  7.2 0.0 all-gather.2.cloned.1.call-start
  7.2 0.7 all-gather.2.cloned.1.call-update
  7.9 0.8 copy.17
  8.7 0.1 pad.14.clone
  8.8 1.9 maximum_maximum_fusion
  10.7 11.5 %all-to-all-start = ((f32[128,8,128]{2,1,0:T(8,128)}), f32[128,8,128]{2,1,0:T(8,128)S(1)}, u32[]{:S(2)}, u32[]{:S(2)}) async-start(f32[128,8,128]{2,1,0:T(8,128)} %maximum_maximum_fusion), calls=%async_computation | async-start | bytes 1048576 | tf_op jit(solution)/shard_map/all_to_all | solution.py:414
  22.2 0.0 copy-done.6
  22.2 0.5 pad.9.hot_ref
  22.7 15.4 %count_bags.2 = (s32[8,256,512]{2,1,0:T(8,128)}, f32[8,128,512]{2,1,0:T(8,128)}) custom-call(s32[16,8,512]{2,1,0:T(8,128)} %bitcast.35, s32[16,512]{1,0:T(8,128)} %bitcast.37, bf16[2048,128]{1,0:T(8,128)(2,1)} %rows_ref.3), custom_call_target="tpu_custom_call" | custom-call | flops 2147483648 | bytes 20971520 | tf_op jit(solution)/shard_map/count_bags/pallas_call | solution.py:101
  38.1 0.0 all-to-all-done.got_ref
  38.1 0.0 copy-start.1
  38.1 0.8 copy-done.1
  38.9 4.0 %hot_rows.1 = bf16[128,16,128]{2,1,0:T(8,128)(2,1)} custom-call(s32[1,16]{1,0:T(1,128)} %ids_ref.1, f32[128,8,128]{2,1,0:T(8,128)} %copy-done.1, f32[1,128]{1,0:T(1,128)} %pad.9.hot_ref, f32[4096,128]{1,0:T(8,128)} %table_ref.1, f32[4096,128]{1,0:T(8,128)} %accum_ref.1), custom_call_target="tpu_custom_call" | custom-call | flops 100663296 | bytes 1048576 | tf_op jit(solution)/shard_map/hot_rows/pallas_call | solution.py:213
  42.9 9.8 %all-to-all-start.1 = ((bf16[128,16,128]{2,1,0:T(8,128)(2,1)}), bf16[128,16,128]{2,1,0:T(8,128)(2,1)S(1)}, u32[]{:S(2)}, u32[]{:S(2)}) async-start(bf16[128,16,128]{2,1,0:T(8,128)(2,1)} %hot_rows.1), calls=%async_computation.1 | async-start | bytes 1048576 | tf_op jit(solution)/shard_map/all_to_all | solution.py:426
  52.7 15.4 %count_bags.3 = (s32[8,256,512]{2,1,0:T(8,128)}, f32[8,128,512]{2,1,0:T(8,128)}) custom-call(s32[16,8,512]{2,1,0:T(8,128)} %bitcast.36, s32[16,512]{1,0:T(8,128)} %bitcast.38, bf16[2048,128]{1,0:T(8,128)(2,1)} %rows_ref.3), custom_call_target="tpu_custom_call" | custom-call | flops 2147483648 | bytes 20971520 | tf_op jit(solution)/shard_map/count_bags/pallas_call | solution.py:101
  68.1 0.0 all-to-all-done.1
  68.1 0.0 copy-start.3
  68.1 0.8 copy-done.3
  68.9 9.4 %pool_new.2 = (bf16[1024,512]{1,0:T(8,128)(2,1)}, bf16[512,1024]{1,0:T(8,128)(2,1)}) custom-call(s32[8,256,512]{2,1,0:T(8,128)} %get-tuple-element.21.words_ref, f32[8,128,512]{2,1,0:T(8,128)} %get-tuple-element.22.part_ref, bf16[2048,128]{1,0:T(8,128)(2,1)} %bitcast.26), custom_call_target="tpu_custom_call" | custom-call | flops 2147483648 | bytes 20971520 | tf_op jit(solution)/shard_map/pool_new/pallas_call | solution.py:152
  78.3 0.6 collective-permute-start.2
  78.9 0.0 copy-start.7
  78.9 0.0 copy-start.4
  78.9 0.0 copy-start.5
  78.9 9.0 %pool_new.3 = (bf16[1024,512]{1,0:T(8,128)(2,1)}, bf16[512,1024]{1,0:T(8,128)(2,1)}) custom-call(s32[8,256,512]{2,1,0:T(8,128)} %get-tuple-element.24.words_ref, f32[8,128,512]{2,1,0:T(8,128)} %get-tuple-element.25.part_ref, bf16[2048,128]{1,0:T(8,128)(2,1)} %bitcast.27), custom_call_target="tpu_custom_call" | custom-call | flops 2147483648 | bytes 20971520 | tf_op jit(solution)/shard_map/pool_new/pallas_call | solution.py:152
  87.9 0.0 collective-permute-start.3
  87.9 0.0 copy-done.7
  87.9 0.5 collective-permute-start
  88.4 0.1 collective-permute-start.1
  88.5 0.0 copy-done.4
  88.5 0.4 collective-permute-start.5
  88.9 0.0 copy-done.5
  88.9 0.6 dynamic-slice_convert_fusion
  89.5 0.0 collective-permute-done.2.peer_a
  89.5 2.9 %collective-permute-done.3.peer_b = bf16[512,1024]{1,0:T(8,128)(2,1)} collective-permute-done((bf16[512,1024]{1,0:T(8,128)(2,1)}, bf16[512,1024]{1,0:T(8,128)(2,1)}, u32[]{:S(2)}, u32[]{:S(2)}) %collective-permute-start.3) | collective-permute-done | bytes 1048608 | tf_op jit(solution)/shard_map/ppermute | solution.py:433
  92.4 0.0 all-gather.2.cloned.1.call-done.weight_ref
  92.4 12.9 %dense_forward.1 = (bf16[4,1024,256]{2,1,0:T(8,128)(2,1)}, f32[4,1024,256]{2,1,0:T(8,128)}, f32[8,128]{1,0:T(8,128)}) custom-call(s32[1]{0:T(128)} %bitcast.8.core_ref, bf16[512,1024]{1,0:T(8,128)(2,1)} %get-tuple-element.27.own_a, bf16[512,1024]{1,0:T(8,128)(2,1)} %collective-permute-done.2.peer_a, bf16[512,1024]{1,0:T(8,128)(2,1)} %get-tuple-element.28.own_b, ...), custom_call_target="tpu_custom_call" | custom-call | flops 4294967296 | bytes 14680064 | tf_op jit(solution)/shard_map/dense_forward/pallas_call | solution.py:289
  105.3 0.5 collective-permute-start.4
  105.8 0.0 collective-permute-done.5
  105.8 0.6 pad_maximum_fusion.marks_ref
  106.4 0.0 collective-permute-done.peer_a
  106.4 0.0 copy-start.8
  106.4 0.0 collective-permute-done.1.peer_b
  106.4 0.0 copy-start.9
  106.4 0.6 collective-permute-done.4.swapped_ref
  107.0 0.3 copy-done.8
  107.4 0.4 copy-done.9
  107.7 0.0 copy-done.10
  107.7 11.5 %grad_terms.1 = bf16[128,144,128]{2,1,0:T(8,128)(2,1)} custom-call(bf16[1024,512]{1,0:T(8,128)(2,1)} %get-tuple-element.23.own_a, bf16[1024,512]{1,0:T(8,128)(2,1)} %copy-done.8, bf16[1024,512]{1,0:T(8,128)(2,1)} %get-tuple-element.26.own_b, bf16[1024,512]{1,0:T(8,128)(2,1)} %copy-done.9, bf16[4,1024,256]{2,1,0:T(8,128)(2,1)} %get-tuple-element.29.act_ref, ...), custom_call_target="tpu_custom_call" | custom-call | flops 4294967296 | bytes 14680064 | tf_op jit(solution)/shard_map/grad_terms/pallas_call | solution.py:382
  119.2 0.0 copy-start.2
  119.2 0.0 slice-start
  119.2 8.4 %all-to-all-start.2 = ((bf16[128,144,128]{2,1,0:T(8,128)(2,1)}), bf16[128,144,128]{2,1,0:T(8,128)(2,1)}, u32[]{:S(2)}, u32[]{:S(2)}) async-start(bf16[128,144,128]{2,1,0:T(8,128)(2,1)} %grad_terms.1), calls=%async_computation.2 | async-start | bytes 9437184 | tf_op jit(solution)/shard_map/all_to_all | solution.py:442
  127.6 0.0 copy-start
  127.7 0.0 copy-done.2
  127.7 0.2 convert_reduce_fusion.1
  127.9 0.1 convert_element_type.38
  128.0 0.0 slice-done
  128.0 3.6 %scatter_custom_fusion = f32[4096,128]{1,0:T(8,128)} fusion(s32[512]{0:T(512)S(1)} %bitcast.34, f32[512,128]{1,0:T(8,128)S(1)} %bitcast.25, f32[]{:T(128)} %constant.8.clone.1), kind=kCustom, calls=%fused_computation.4 | custom fusion | flops 65536 | bytes 2097156 | tf_op jit(solution)/shard_map/scatter-add | solution.py:447
  131.7 0.0 copy-done
  131.7 4.6 %multiply_subtract_fusion = (f32[4096,128]{1,0:T(8,128)}, f32[4096,128]{1,0:T(8,128)}) fusion(f32[4096,128]{1,0:T(8,128)S(1)} %copy-done, f32[4096,128]{1,0:T(8,128)} %scatter_custom_fusion, f32[4096,128]{1,0:T(8,128)} %accum_ref.1), kind=kLoop, calls=%fused_computation.2 | loop fusion | flops 2621440 | bytes 10485760 | tf_op jit(solution)/shard_map/sub | solution.py:449
  136.3 49.9 %all-to-all-done.2 = bf16[128,144,128]{2,1,0:T(8,128)(2,1)} async-done(((bf16[128,144,128]{2,1,0:T(8,128)(2,1)}), bf16[128,144,128]{2,1,0:T(8,128)(2,1)}, u32[]{:S(2)}, u32[]{:S(2)}) %all-to-all-start.2) | async-done | bytes 4718624 | tf_op jit(solution)/shard_map/all_to_all | solution.py:442
  186.2 3.0 %convert_reduce_fusion = f32[2,144,128]{2,1,0:T(8,128)S(1)} fusion(bf16[64,2,144,128]{3,2,1,0:T(8,128)(2,1)} %bitcast.15), kind=kLoop, calls=%fused_computation.1 | loop fusion | flops 4681728 | bytes 4866048 | tf_op jit(solution)/shard_map/reduce_sum | solution.py:443
  189.2 0.6 fusion.2
  189.9 0.7 copy.21
  (9 shorter events, 0.1 us)
Async XLA Ops:
  7.2 15.0 %copy-start.6 = (s32[1,16]{1,0:T(1,128)S(1)}, s32[1,16]{1,0:T(1,128)}, u32[]{:S(2)}) copy-start(s32[1,16]{1,0:T(1,128)} %ids_ref.1) | copy-start | bytes 196
  7.2 85.2 %all-gather.2.cloned.1.call-start = ((), (), s32[]{:S(2)}) async-start(), calls=%async_computation.3 | async-start | bytes 8454144 | tf_op jit(solution)/shard_map/all_gather | solution.py:416
  10.7 27.4 %all-to-all-start = ((f32[128,8,128]{2,1,0:T(8,128)}), f32[128,8,128]{2,1,0:T(8,128)S(1)}, u32[]{:S(2)}, u32[]{:S(2)}) async-start(f32[128,8,128]{2,1,0:T(8,128)} %maximum_maximum_fusion), calls=%async_computation | async-start | bytes 1048576 | tf_op jit(solution)/shard_map/all_to_all | solution.py:414
  38.1 0.8 copy-start.1
  42.9 25.2 %all-to-all-start.1 = ((bf16[128,16,128]{2,1,0:T(8,128)(2,1)}), bf16[128,16,128]{2,1,0:T(8,128)(2,1)S(1)}, u32[]{:S(2)}, u32[]{:S(2)}) async-start(bf16[128,16,128]{2,1,0:T(8,128)(2,1)} %hot_rows.1), calls=%async_computation.1 | async-start | bytes 1048576 | tf_op jit(solution)/shard_map/all_to_all | solution.py:426
  68.1 0.8 copy-start.3
  78.3 11.2 %collective-permute-start.2 = (bf16[512,1024]{1,0:T(8,128)(2,1)}, bf16[512,1024]{1,0:T(8,128)(2,1)}, u32[]{:S(2)}, u32[]{:S(2)}) collective-permute-start(bf16[512,1024]{1,0:T(8,128)(2,1)} %get-tuple-element.27.own_a), channel_id=1, source_target_pairs={{0,1},{1,0},{2,3},{3,2},{4,5},{5,4},{6,7},{7,6},{8,9},{9,8},{10,11... | collective-permute-start | bytes 3145736 | tf_op jit(solution)/shard_map/ppermute | solution.py:433
  78.9 9.0 %copy-start.7 = (bf16[1024,512]{1,0:T(8,128)(2,1)S(1)}, bf16[1024,512]{1,0:T(8,128)(2,1)}, u32[]{:S(2)}) copy-start(bf16[1024,512]{1,0:T(8,128)(2,1)} %get-tuple-element.23.own_a) | copy-start | bytes 3145732
  78.9 9.6 %copy-start.4 = (s32[512]{0:T(512)S(1)}, s32[512]{0:T(512)}, u32[]{:S(2)}) copy-start(s32[512]{0:T(512)} %param.19) | copy-start | bytes 6148
  78.9 10.0 %copy-start.5 = (bf16[2048]{0:T(1024)(128)(2,1)S(1)}, bf16[2048]{0:T(1024)(128)(2,1)}, u32[]{:S(2)}) copy-start(bf16[2048]{0:T(1024)(128)(2,1)} %param.21) | copy-start | bytes 12292
  87.9 4.5 %collective-permute-start.3 = (bf16[512,1024]{1,0:T(8,128)(2,1)}, bf16[512,1024]{1,0:T(8,128)(2,1)}, u32[]{:S(2)}, u32[]{:S(2)}) collective-permute-start(bf16[512,1024]{1,0:T(8,128)(2,1)} %get-tuple-element.28.own_b), channel_id=1, source_target_pairs={{0,1},{1,0},{2,3},{3,2},{4,5},{5,4},{6,7},{7,6},{8,9},{9,8},{10,11... | collective-permute-start | bytes 3145736 | tf_op jit(solution)/shard_map/ppermute | solution.py:433
  87.9 18.4 %collective-permute-start = (bf16[1024,512]{1,0:T(8,128)(2,1)S(1)}, bf16[1024,512]{1,0:T(8,128)(2,1)S(1)}, u32[]{:S(2)}, u32[]{:S(2)}) collective-permute-start(bf16[1024,512]{1,0:T(8,128)(2,1)S(1)} %copy-done.7), channel_id=1, source_target_pairs={{0,1},{1,0},{2,3},{3,2},{4,5},{5,4},{6,7},{7,6},{8,9},{9,8},{10,11... | collective-permute-start | bytes 3145736 | tf_op jit(solution)/shard_map/ppermute | solution.py:433
  88.4 18.0 %collective-permute-start.1 = (bf16[1024,512]{1,0:T(8,128)(2,1)}, bf16[1024,512]{1,0:T(8,128)(2,1)S(1)}, u32[]{:S(2)}, u32[]{:S(2)}) collective-permute-start(bf16[1024,512]{1,0:T(8,128)(2,1)} %get-tuple-element.26.own_b), channel_id=1, source_target_pairs={{0,1},{1,0},{2,3},{3,2},{4,5},{5,4},{6,7},{7,6},{8,9},{9,8},{10,11... | collective-permute-start | bytes 3145736 | tf_op jit(solution)/shard_map/ppermute | solution.py:433
  88.5 17.3 %collective-permute-start.5 = (f32[4,128]{1,0:T(4,128)S(1)}, f32[4,128]{1,0:T(4,128)S(1)}, u32[]{:S(2)}, u32[]{:S(2)}) collective-permute-start(f32[4,128]{1,0:T(4,128)S(1)} %convert_bitcast_fusion.1), channel_id=1, source_target_pairs={{0,1},{1,0},{2,3},{3,2},{4,5},{5,4},{6,7},{7,6},{8,9},{9,8},{10,11... | collective-permute-start | bytes 6152 | tf_op jit(solution)/shard_map/ppermute | solution.py:435
  105.3 1.7 collective-permute-start.4
  106.4 1.0 copy-start.8
  106.4 1.3 copy-start.9
  107.0 0.7 copy-start.10
  119.2 8.5 %copy-start.2 = (f32[128,8,128]{2,1,0:T(8,128)S(1)}, f32[128,8,128]{2,1,0:T(8,128)}, u32[]{:S(2)}) copy-start(f32[128,8,128]{2,1,0:T(8,128)} %copy-done.1) | copy-start | bytes 1572868
  119.2 8.8 %slice-start = ((f32[128,8,128]{2,1,0:T(8,128)}), f32[128,4,128]{2,1,0:T(4,128)S(1)}, s32[]{:S(2)}) async-start(f32[128,8,128]{2,1,0:T(8,128)} %copy-done.1), calls=%async_computation.4 | async-start | bytes 524288 | tf_op jit(solution)/shard_map/slice | solution.py:422
  119.2 67.0 %all-to-all-start.2 = ((bf16[128,144,128]{2,1,0:T(8,128)(2,1)}), bf16[128,144,128]{2,1,0:T(8,128)(2,1)}, u32[]{:S(2)}, u32[]{:S(2)}) async-start(bf16[128,144,128]{2,1,0:T(8,128)(2,1)} %grad_terms.1), calls=%async_computation.2 | async-start | bytes 9437184 | tf_op jit(solution)/shard_map/all_to_all | solution.py:442
  127.6 4.0 %copy-start = (f32[4096,128]{1,0:T(8,128)S(1)}, f32[4096,128]{1,0:T(8,128)}, u32[]{:S(2)}) copy-start(f32[4096,128]{1,0:T(8,128)} %table_ref.1) | copy-start | bytes 6291460
Sparse Core Ops, SparseCore 0:
  11.0 78.3 all-gather.1

commit v4 on v3

--- a/solution.py
+++ b/solution.py
@@ -19,7 +19,16 @@
 SPAN = 32
 SHIFT = 2.0 ** 24
 MIB = 1024 * 1024
+ROW = 256
 GROUP = 2
+
+
+def in_hbm(*arrays):
+    return [pltpu.with_memory_space_constraint(a, pltpu.HBM) for a in arrays]
+
+
+def in_vmem(*arrays):
+    return [pltpu.with_memory_space_constraint(a, pltpu.VMEM) for a in arrays]
 
 
 def level_of(k):
@@ -111,8 +120,8 @@
             pl.BlockSpec((GROUP, width, samples), lambda f: (f, 0, 0)),
         ],
         out_shape=[
-            jax.ShapeDtypeStruct((fields, LO, samples), jnp.int32),
-            jax.ShapeDtypeStruct((fields, width, samples), jnp.float32),
+            pltpu.HBM((fields, LO, samples), jnp.int32),
+            pltpu.HBM((fields, width, samples), jnp.float32),
         ],
         scratch_shapes=[
             pltpu.VMEM((width, LO * FIELDS), jnp.bfloat16),
@@ -122,7 +131,7 @@
             pltpu.VMEM((LO * FIELDS, samples), jnp.bfloat16),
             pltpu.VMEM((LO * FIELDS, samples), jnp.bfloat16),
         ],
-        compiler_params=pltpu.CompilerParams(vmem_limit_bytes=56 * MIB),
+        compiler_params=pltpu.CompilerParams(vmem_limit_bytes=16 * MIB),
         cost_estimate=pl.CostEstimate(flops=2 * fields * samples * 2048 * 128, bytes_accessed=20 << 20, transcendentals=0),
         name="count_bags",
     )(idx, length, rows)
@@ -162,18 +171,18 @@
             pl.BlockSpec((samples, width * GROUP), lambda f: (0, f)),
         ],
         out_shape=[
-            jax.ShapeDtypeStruct((fields * width, samples), jnp.bfloat16),
-            jax.ShapeDtypeStruct((samples, fields * width), jnp.bfloat16),
+            pltpu.VMEM((fields * width, samples), jnp.bfloat16),
+            pltpu.VMEM((samples, fields * width), jnp.bfloat16),
         ],
         scratch_shapes=[
             pltpu.VMEM((width, LO * FIELDS), jnp.bfloat16),
             pltpu.VMEM((LO * FIELDS, samples), jnp.bfloat16),
             pltpu.VMEM((LO * FIELDS, samples), jnp.bfloat16),
         ],
-        compiler_params=pltpu.CompilerParams(vmem_limit_bytes=56 * MIB),
+        compiler_params=pltpu.CompilerParams(vmem_limit_bytes=16 * MIB),
         cost_estimate=pl.CostEstimate(flops=2 * fields * samples * 2048 * 128, bytes_accessed=20 << 20, transcendentals=0),
         name="pool_new",
-    )(words, part, rows)
+    )(*in_hbm(words, part), rows)
 
 
 def hot_kernel(ids_ref, got_ref, hot_ref, table_ref, accum_ref, copies_ref, rows_ref, sems):
@@ -222,15 +231,15 @@
         out_specs=inside,
         out_shape=jax.ShapeDtypeStruct((N_ALL, count, 128), jnp.bfloat16),
         scratch_shapes=[pltpu.VMEM((2, count, 128), jnp.float32), pltpu.SemaphoreType.DMA((2, count))],
-        compiler_params=pltpu.CompilerParams(vmem_limit_bytes=56 * MIB),
+        compiler_params=pltpu.CompilerParams(vmem_limit_bytes=8 * MIB),
         cost_estimate=pl.CostEstimate(flops=4 * 128**3 * 12, bytes_accessed=1 << 20, transcendentals=count * 128),
         name="hot_rows",
-    )(ids, got, hot, table, accum)
+    )(ids, got, hot, *in_hbm(table, accum))
 
 
 def dense_kernel(
     core_ref, own_a, peer_a, own_b, peer_b, weight_ref, out_ref, act_ref, slope_ref, logit_ref,
-    sum_ref, side_ref, columns_ref, act_v, slope_v, sems, out_sems,
+    sum_ref, columns_ref, sems,
 ):
     samples, deep = own_a.shape
     steps = columns_ref.shape[0]
@@ -238,37 +247,38 @@
     for n in range(steps):
         columns = pl.ds(pl.multiple_of(core_ref[0] * (256 * steps) + 256 * n, 256), 256)
         fetch_columns.append(pltpu.make_async_copy(weight_ref.at[:, columns], columns_ref.at[n], sems.at[n]))
-    fetch_sides = [
-        pltpu.make_async_copy(side, side_ref.at[i], sems.at[steps + i])
-        for i, side in enumerate((own_a, own_b, peer_a, peer_b))
-    ]
-    for fetch in fetch_columns[:1] + fetch_sides + fetch_columns[1:]:
+    for fetch in fetch_columns:
         fetch.start()
-    sent = []
+
+    def product(n, m):
+        left, right = ((own_a, own_b), (peer_a, peer_b))[m // 2]
+        rows = slice(ROW * (m % 2), ROW * (m % 2) + ROW)
+        hidden = jnp.dot(left[rows], columns_ref[n, :deep], preferred_element_type=jnp.float32)
+        return hidden + jnp.dot(right[rows], columns_ref[n, deep:], preferred_element_type=jnp.float32)
+
+    def finish(n, m, hidden):
+        w = out_ref[:, 256 * n : 256 * n + 256]
+        square = hidden * hidden
+        t = jnp.tanh(hidden * (ROOT + ROOT * 0.044715 * square))
+        near = 0.5 + 0.5 * t
+        act = (hidden * near).astype(jnp.bfloat16)
+        slope = near + 0.5 * hidden * (1.0 - t * t) * (ROOT + 3.0 * ROOT * 0.044715 * square)
+        here = slice(ROW * m, ROW * m + ROW)
+        act_ref[n, here] = act
+        slope_ref[n, here] = slope * w
+        term = act.astype(jnp.float32) * w
+        term = term[:, :128] + term[:, 128:]
+        sum_ref[here] = term if n == 0 else sum_ref[here] + term
+
+    before = None
     for n in range(steps):
         fetch_columns[n].wait()
-        w = out_ref[:, 256 * n : 256 * n + 256]
-        for m in range(2):
-            if n == 0:
-                fetch_sides[2 * m].wait()
-                fetch_sides[2 * m + 1].wait()
-            hidden = jnp.dot(side_ref[2 * m], columns_ref[n, :deep], preferred_element_type=jnp.float32)
-            hidden = hidden + jnp.dot(side_ref[2 * m + 1], columns_ref[n, deep:], preferred_element_type=jnp.float32)
-            square = hidden * hidden
-            t = jnp.tanh(hidden * (ROOT + ROOT * 0.044715 * square))
-            near = 0.5 + 0.5 * t
-            act = (hidden * near).astype(jnp.bfloat16)
-            slope = near + 0.5 * hidden * (1.0 - t * t) * (ROOT + 3.0 * ROOT * 0.044715 * square)
-            here = slice(samples * m, samples * m + samples)
-            act_v[n, here] = act
-            slope_v[n, here] = slope * w
-            term = act.astype(jnp.float32) * w
-            term = term[:, :128] + term[:, 128:]
-            sum_ref[here] = term if n == 0 else sum_ref[here] + term
-        for i, (store, target) in enumerate(((act_v, act_ref), (slope_v, slope_ref))):
-            send = pltpu.make_async_copy(store.at[n], target.at[n], out_sems.at[i, n])
-            send.start()
-            sent.append(send)
+        for m in range(4):
+            hidden = product(n, m)
+            if before is not None:
+                finish(*before)
+            before = (n, m, hidden)
+    finish(*before)
     ones = jnp.ones((8, 128), jnp.float32)
     for b in range(logit_ref.shape[0]):
         term = sum_ref[128 * b : 128 * b + 128]
@@ -276,8 +286,6 @@
             ones, term, (((1,), (1,)), ((), ())), precision=lax.Precision.HIGHEST, preferred_element_type=jnp.float32
         )
         logit_ref[b : b + 1] = line[:1]
-    for send in sent:
-        send.wait()
 
 
 def dense_call(core, own_a, peer_a, own_b, peer_b, weight, out_w):
@@ -288,59 +296,43 @@
     inside = pl.BlockSpec(memory_space=pltpu.VMEM)
     return pl.pallas_call(
         dense_kernel,
-        in_specs=[pl.BlockSpec(memory_space=pltpu.SMEM)] + [far] * 5 + [inside],
-        out_specs=[far, far, inside],
+        in_specs=[pl.BlockSpec(memory_space=pltpu.SMEM)] + [inside] * 4 + [far] + [inside],
+        out_specs=[inside] * 3,
         out_shape=[
-            jax.ShapeDtypeStruct((steps, 2 * samples, 256), jnp.bfloat16),
-            jax.ShapeDtypeStruct((steps, 2 * samples, 256), jnp.float32),
+            pltpu.VMEM((steps, 2 * samples, 256), jnp.bfloat16),
+            pltpu.VMEM((steps, 2 * samples, 256), jnp.float32),
             jax.ShapeDtypeStruct((2 * samples // 128, 128), jnp.float32),
         ],
         scratch_shapes=[
             pltpu.VMEM((2 * samples, 128), jnp.float32),
-            pltpu.VMEM((4, samples, deep), jnp.bfloat16),
             pltpu.VMEM((steps, 2 * deep, 256), jnp.bfloat16),
-            pltpu.VMEM((steps, 2 * samples, 256), jnp.bfloat16),
-            pltpu.VMEM((steps, 2 * samples, 256), jnp.float32),
-            pltpu.SemaphoreType.DMA((steps + 4,)),
-            pltpu.SemaphoreType.DMA((2, steps)),
-        ],
-        compiler_params=pltpu.CompilerParams(vmem_limit_bytes=56 * MIB),
+            pltpu.SemaphoreType.DMA((steps,)),
+        ],
+        compiler_params=pltpu.CompilerParams(vmem_limit_bytes=16 * MIB),
         cost_estimate=pl.CostEstimate(flops=4 * samples * deep * 2 * wide, bytes_accessed=14 << 20, transcendentals=2 * samples * wide),
         name="dense_forward",
-    )(core.reshape(1), own_a, peer_a, own_b, peer_b, weight, out_w.reshape(1, wide))
+    )(core.reshape(1), *in_vmem(own_a, peer_a, own_b, peer_b), *in_hbm(weight), out_w.reshape(1, wide))
 
 
 def grad_kernel(
     own_a, peer_a, own_b, peer_b, act_ref, slope_ref, logit_ref, swapped_ref, marks_ref, out_ref,
-    side_ref, act_v, slope_v, dh_ref, blocks_ref, sems, out_sems,
+    dh_ref, blocks_ref, out_sems,
 ):
     deep, samples = own_a.shape
     steps = act_ref.shape[0]
     tall = blocks_ref.shape[1]
-    fetch_dense = [
-        [pltpu.make_async_copy(act_ref.at[n], act_v.at[n], sems.at[2 * n]), pltpu.make_async_copy(slope_ref.at[n], slope_v.at[n], sems.at[2 * n + 1])]
-        for n in range(steps)
-    ]
-    fetch_sides = [
-        pltpu.make_async_copy(side, side_ref.at[i], sems.at[2 * steps + i])
-        for i, side in enumerate((own_a, peer_a, own_b, peer_b))
-    ]
-    for fetch in fetch_dense[0] + fetch_sides + [f for pair in fetch_dense[1:] for f in pair]:
-        fetch.start()
     own_rows = samples // 128
     logit = logit_ref[...] + jnp.concatenate([swapped_ref[own_rows:], swapped_ref[:own_rows]], axis=0)
     error = (0.125 * (jax.nn.sigmoid(logit) - marks_ref[...])).T
     sent = []
     lines = []
     for c in range(steps):
-        for fetch in fetch_dense[c]:
-            fetch.wait()
         total = jnp.zeros((8, 256), jnp.float32)
         for b in range(2 * own_rows):
             rows = slice(128 * b, 128 * b + 128)
             column = error[:, b : b + 1]
-            dh_ref[c, rows] = (column * slope_v[c, rows]).astype(jnp.bfloat16)
-            weighted = column * act_v[c, rows].astype(jnp.float32)
+            dh_ref[c, rows] = (column * slope_ref[c, rows]).astype(jnp.bfloat16)
+            weighted = column * act_ref[c, rows].astype(jnp.float32)
             total = total + jnp.sum(weighted.reshape(16, 8, 256), axis=0)
         total = jnp.sum(total, axis=0, keepdims=True)
         lines += [total[:, :128], total[:, 128:]]
@@ -355,11 +347,9 @@
 
             lax.fori_loop(0, blocks_ref.shape[0], place, 0)
         for side in range(2):
-            if c == 0:
-                fetch_sides[2 * side].wait()
-                fetch_sides[2 * side + 1].wait()
-            term = jnp.dot(side_ref[2 * side], dh_ref[c, :samples], preferred_element_type=jnp.float32)
-            term = term + jnp.dot(side_ref[2 * side + 1], dh_ref[c, samples:], preferred_element_type=jnp.float32)
+            own, peer = ((own_a, peer_a), (own_b, peer_b))[side]
+            term = jnp.dot(own[...], dh_ref[c, :samples], preferred_element_type=jnp.float32)
+            term = term + jnp.dot(peer[...], dh_ref[c, samples:], preferred_element_type=jnp.float32)
             term = term.astype(jnp.bfloat16)
             blocks = pl.ds(side * (deep // 16), deep // 16)
             for part in range(2):
@@ -381,22 +371,18 @@
     shape = (2 * deep // 16, 32 * steps + 16, 128)
     return pl.pallas_call(
         grad_kernel,
-        in_specs=[far] * 6 + [inside] * 3,
+        in_specs=[inside] * 9,
         out_specs=far,
-        out_shape=jax.ShapeDtypeStruct(shape, jnp.bfloat16),
+        out_shape=pltpu.HBM(shape, jnp.bfloat16),
         scratch_shapes=[
-            pltpu.VMEM((4, deep, samples), jnp.bfloat16),
-            pltpu.VMEM(act.shape, jnp.bfloat16),
-            pltpu.VMEM(slope.shape, jnp.float32),
             pltpu.VMEM(act.shape, jnp.bfloat16),
             pltpu.VMEM(shape, jnp.bfloat16),
-            pltpu.SemaphoreType.DMA((2 * steps + 4,)),
             pltpu.SemaphoreType.DMA((2, steps)),
         ],
-        compiler_params=pltpu.CompilerParams(vmem_limit_bytes=56 * MIB),
+        compiler_params=pltpu.CompilerParams(vmem_limit_bytes=16 * MIB),
         cost_estimate=pl.CostEstimate(flops=8 * samples * deep * 256 * steps, bytes_accessed=14 << 20, transcendentals=0),
         name="grad_terms",
-    )(own_a, peer_a, own_b, peer_b, act, slope, logit, swapped, marks)
+    )(*in_vmem(own_a, peer_a, own_b, peer_b, act, slope), logit, swapped, marks)
 
 
 def per_device(

time: 198 us -> 190 us (0.960)
  Pallas kernels: 77.6 us -> 70.5 us
  waiting for transfers between devices: 54.1 us -> 57.8 us
  local copies, waits for them, and re-layouts: 4.57 us -> 1.8 us
    pallas_call x1, Pallas kernels: 11.5 us -> 8.88 us  [grad_call(): pl.pallas_call(grad_kernel, in_specs=[inside] * 9, out_specs=far, out_sha...]
    all_gather x1, waiting for transfers between devices: 0.01 us -> 2.3 us  [per_device(): weight = lax.all_gather(w_first, ALL, axis=0, tiled=True)]
    unnamed x24 -> x16, local copies, waits for them, and re-layouts: 3.81 us -> 1.52 us
    pallas_call x2, Pallas kernels: 30.8 us -> 28.6 us  [count_call(): pl.pallas_call(functools.partial(count_kernel, start), grid=(fields // GR...]
  transfers between devices with their start and end apart: 10 -> 10, of which waited for: 3 -> 5; matrix products, arithmetic and copies ran while one was open for 7% -> 6% of each run, Pallas kernels for 33% -> 32%
where the time goes in v4:
time: 190 us
  Pallas kernels  70.5 us (37%)
  waiting for transfers between devices  57.8 us (30%)
  starting transfers between devices  31.4 us (17%)
  between operations  14.2 us (7%)
  other arithmetic  14 us (7%)
    all_to_all x1, waiting for transfers between devices, per_device(): terms = lax.all_to_all(blocks, ALL, split_axis=0, concat_axis=0, tiled=True)  49.9 us
    pallas_call x2, Pallas kernels, count_call(): pl.pallas_call(functools.partial(count_kernel, start), grid=(fields // GR...  28.6 us
    pallas_call x2, Pallas kernels, new_call(): pl.pallas_call(new_kernel, grid=(fields // GROUP,), in_specs=[pl.BlockSpe...  17.7 us
    all_to_all x1, starting transfers between devices, per_device(): got = lax.all_to_all(packet, ALL, split_axis=0, concat_axis=0, tiled=True)  11.5 us
    pallas_call x1, Pallas kernels, dense_call(): pl.pallas_call(dense_kernel, in_specs=[pl.BlockSpec(memory_space=pltpu.SM...  11.3 us
    all_to_all x1, starting transfers between devices, per_device(): lax.all_to_all(copies, ALL, split_axis=0, concat_axis=0, tiled=True)  9.76 us
    pallas_call x1, Pallas kernels, grad_call(): pl.pallas_call(grad_kernel, in_specs=[inside] * 9, out_specs=far, out_sha...  8.88 us
    all_to_all x1, starting transfers between devices, per_device(): terms = lax.all_to_all(blocks, ALL, split_axis=0, concat_axis=0, tiled=True)  7.71 us
  transfers between devices with their start and end apart: 10, of which 5 were waited for; matrix products, arithmetic and copies ran while one was open for 6% of the time, Pallas kernels for 32%

profile of v4, /device:TPU:1, one launch (start us, length us, event | category | flops | bytes accessed | tf_op | source)
XLA Modules:
  0.0 189.8 jit_solution(5437444640965972240)
XLA Ops:
  7.2 0.0 copy-start
  7.2 0.0 copy-start.2
  7.2 0.0 copy-start.3
  7.2 0.0 copy-start.1
  7.2 0.0 all-gather.2.cloned.1.call-start
  7.3 0.7 all-gather.2.cloned.1.call-update
  7.9 0.8 copy.17
  8.8 0.1 pad.14.clone
  8.8 1.9 maximum_maximum_fusion
  10.7 11.5 %all-to-all-start = ((f32[128,8,128]{2,1,0:T(8,128)}), f32[128,8,128]{2,1,0:T(8,128)S(1)}, u32[]{:S(2)}, u32[]{:S(2)}) async-start(f32[128,8,128]{2,1,0:T(8,128)} %maximum_maximum_fusion), calls=%async_computation | async-start | bytes 1048576 | tf_op jit(solution)/shard_map/all_to_all | solution.py:400
  22.2 0.0 copy-done
  22.2 0.0 copy-done.2
  22.3 0.0 copy-done.3
  22.3 0.0 copy-done.1
  22.3 14.3 %count_bags.2 = (s32[8,256,512]{2,1,0:T(8,128)}, f32[8,128,512]{2,1,0:T(8,128)}) custom-call(s32[16,8,512]{2,1,0:T(8,128)S(1)} %bitcast.28, s32[16,512]{1,0:T(8,128)S(1)} %bitcast.30, bf16[2048,128]{1,0:T(8,128)(2,1)S(1)} %copy-done.1), custom_call_target="tpu_custom_call" | custom-call | flops 2147483648 | bytes 20971520 | tf_op jit(solution)/shard_map/count_bags/pallas_call | solution.py:110
  36.6 0.0 all-to-all-done.got_ref
  36.6 4.0 %hot_rows.1 = bf16[128,16,128]{2,1,0:T(8,128)(2,1)} custom-call(s32[1,16]{1,0:T(1,128)S(1)} %copy-done, f32[128,8,128]{2,1,0:T(8,128)S(1)} %all-to-all-done.got_ref, f32[1,128]{1,0:T(1,128)S(1)} %pad.9.hot_ref, f32[4096,128]{1,0:T(8,128)} %table_ref.1, f32[4096,128]{1,0:T(8,128)} %accum_ref.1), custom_call_target="tpu_custom_call" | custom-call | flops 100663296 | bytes 1048576 | tf_op jit(solution)/shard_map/hot_rows/pallas_call | solution.py:222
  40.6 9.8 %all-to-all-start.1 = ((bf16[128,16,128]{2,1,0:T(8,128)(2,1)}), bf16[128,16,128]{2,1,0:T(8,128)(2,1)S(1)}, u32[]{:S(2)}, u32[]{:S(2)}) async-start(bf16[128,16,128]{2,1,0:T(8,128)(2,1)} %hot_rows.1), calls=%async_computation.1 | async-start | bytes 1048576 | tf_op jit(solution)/shard_map/all_to_all | solution.py:412
  50.4 14.3 %count_bags.3 = (s32[8,256,512]{2,1,0:T(8,128)}, f32[8,128,512]{2,1,0:T(8,128)}) custom-call(s32[16,8,512]{2,1,0:T(8,128)S(1)} %bitcast.29, s32[16,512]{1,0:T(8,128)S(1)} %bitcast.31, bf16[2048,128]{1,0:T(8,128)(2,1)S(1)} %copy-done.1), custom_call_target="tpu_custom_call" | custom-call | flops 2147483648 | bytes 20971520 | tf_op jit(solution)/shard_map/count_bags/pallas_call | solution.py:110
  64.7 0.1 all-to-all-done.1
  64.8 8.8 %pool_new.2 = (bf16[1024,512]{1,0:T(8,128)(2,1)S(1)}, bf16[512,1024]{1,0:T(8,128)(2,1)}) custom-call(s32[8,256,512]{2,1,0:T(8,128)} %get-tuple-element.21.words_ref, f32[8,128,512]{2,1,0:T(8,128)} %get-tuple-element.22.part_ref, bf16[2048,128]{1,0:T(8,128)(2,1)S(1)} %bitcast.25), custom_call_target="tpu_custom_call" | custom-call | flops 2147483648 | bytes 20971520 | tf_op jit(solution)/shard_map/pool_new/pallas_call | solution.py:161
  73.6 0.8 collective-permute-start.2
  74.5 0.0 copy-start.5
  74.5 0.0 copy-start.6
  74.5 8.8 %pool_new.3 = (bf16[1024,512]{1,0:T(8,128)(2,1)S(1)}, bf16[512,1024]{1,0:T(8,128)(2,1)}) custom-call(s32[8,256,512]{2,1,0:T(8,128)} %get-tuple-element.24.words_ref, f32[8,128,512]{2,1,0:T(8,128)} %get-tuple-element.25.part_ref, bf16[2048,128]{1,0:T(8,128)(2,1)S(1)} %bitcast.26), custom_call_target="tpu_custom_call" | custom-call | flops 2147483648 | bytes 20971520 | tf_op jit(solution)/shard_map/pool_new/pallas_call | solution.py:161
  83.3 0.0 collective-permute-start.3
  83.3 0.5 collective-permute-start
  83.8 0.0 collective-permute-start.1
  83.8 0.0 copy-done.5
  83.8 0.5 collective-permute-start.5
  84.3 0.0 copy-done.6
  84.3 0.0 collective-permute-done.2.peer_a
  84.3 3.9 %collective-permute-done.3.peer_b = bf16[512,1024]{1,0:T(8,128)(2,1)} collective-permute-done((bf16[512,1024]{1,0:T(8,128)(2,1)}, bf16[512,1024]{1,0:T(8,128)(2,1)}, u32[]{:S(2)}, u32[]{:S(2)}) %collective-permute-start.3) | collective-permute-done | bytes 1048608 | tf_op jit(solution)/shard_map/ppermute | solution.py:419
  88.3 2.3 %all-gather.2.cloned.1.call-done.weight_ref = bf16[2048,2048]{1,0:T(8,128)(2,1)} async-done(((bf16[16,2048]{1,0:T(8,128)(2,1)}), bf16[2048,2048]{1,0:T(8,128)(2,1)}) %all-gather.2.cloned.1.call-update) | async-done | bytes 8388624 | tf_op jit(solution)/shard_map/all_gather | solution.py:402
  90.6 11.3 %dense_forward.1 = (bf16[4,1024,256]{2,1,0:T(8,128)(2,1)S(1)}, f32[4,1024,256]{2,1,0:T(8,128)S(1)}, f32[8,128]{1,0:T(8,128)S(1)}) custom-call(s32[1]{0:T(128)} %bitcast.8.core_ref, bf16[512,1024]{1,0:T(8,128)(2,1)} %get-tuple-element.27.own_a, bf16[512,1024]{1,0:T(8,128)(2,1)} %collective-permute-done.2.peer_a, bf16[512,1024]{1,0:T(8,128)(2,1)} %get-tuple-element.28.own_b, ...), custom_call_target="tpu_custom_call" | custom-call | flops 4294967296 | bytes 14680064 | tf_op jit(solution)/shard_map/dense_forward/pallas_call | solution.py:297
  101.9 0.5 collective-permute-start.4
  102.5 0.0 collective-permute-done.5
  102.5 0.0 collective-permute-done.peer_a
  102.5 0.0 collective-permute-done.1.peer_b
  102.5 0.9 collective-permute-done.4.swapped_ref
  103.4 8.9 %grad_terms.1 = bf16[128,144,128]{2,1,0:T(8,128)(2,1)} custom-call(bf16[1024,512]{1,0:T(8,128)(2,1)S(1)} %get-tuple-element.23.own_a, bf16[1024,512]{1,0:T(8,128)(2,1)} %collective-permute-done.peer_a, bf16[1024,512]{1,0:T(8,128)(2,1)S(1)} %get-tuple-element.26.own_b, bf16[1024,512]{1,0:T(8,128)(2,1)} %collective-permute-done.1.peer_b, ...), custom_call_target="tpu_custom_call" | custom-call | flops 4294967296 | bytes 14680064 | tf_op jit(solution)/shard_map/grad_terms/pallas_call | solution.py:372
  112.3 7.7 %all-to-all-start.2 = ((bf16[128,144,128]{2,1,0:T(8,128)(2,1)}), bf16[128,144,128]{2,1,0:T(8,128)(2,1)}, u32[]{:S(2)}, u32[]{:S(2)}) async-start(bf16[128,144,128]{2,1,0:T(8,128)(2,1)} %grad_terms.1), calls=%async_computation.2 | async-start | bytes 9437184 | tf_op jit(solution)/shard_map/all_to_all | solution.py:428
  120.0 0.0 copy-start.4
  120.1 0.2 convert_reduce_fusion.1
  120.3 0.1 convert_element_type.38
  120.4 3.6 %scatter_custom_fusion = f32[4096,128]{1,0:T(8,128)} fusion(s32[512]{0:T(512)S(1)} %bitcast.38, f32[512,128]{1,0:T(8,128)S(1)} %bitcast.36, f32[]{:T(128)} %constant.8.clone.1), kind=kCustom, calls=%fused_computation.4 | custom fusion | flops 65536 | bytes 2097156 | tf_op jit(solution)/shard_map/scatter-add | solution.py:433
  124.1 0.0 copy-done.4
  124.1 4.6 %multiply_subtract_fusion = (f32[4096,128]{1,0:T(8,128)}, f32[4096,128]{1,0:T(8,128)}) fusion(f32[4096,128]{1,0:T(8,128)S(1)} %copy-done.4, f32[4096,128]{1,0:T(8,128)} %scatter_custom_fusion, f32[4096,128]{1,0:T(8,128)} %accum_ref.1), kind=kLoop, calls=%fused_computation.2 | loop fusion | flops 2621440 | bytes 10485760 | tf_op jit(solution)/shard_map/sub | solution.py:435
  128.7 49.9 %all-to-all-done.2 = bf16[128,144,128]{2,1,0:T(8,128)(2,1)} async-done(((bf16[128,144,128]{2,1,0:T(8,128)(2,1)}), bf16[128,144,128]{2,1,0:T(8,128)(2,1)}, u32[]{:S(2)}, u32[]{:S(2)}) %all-to-all-start.2) | async-done | bytes 4718624 | tf_op jit(solution)/shard_map/all_to_all | solution.py:428
  178.6 3.0 %convert_reduce_fusion = f32[2,144,128]{2,1,0:T(8,128)S(1)} fusion(bf16[64,2,144,128]{3,2,1,0:T(8,128)(2,1)} %bitcast.15), kind=kLoop, calls=%fused_computation.1 | loop fusion | flops 4681728 | bytes 4866048 | tf_op jit(solution)/shard_map/reduce_sum | solution.py:429
  181.6 0.6 fusion.2
  182.2 0.7 copy.21
  (12 shorter events, 0.1 us)
Async XLA Ops:
  7.2 15.0 %copy-start = (s32[1,16]{1,0:T(1,128)S(1)}, s32[1,16]{1,0:T(1,128)}, u32[]{:S(2)}) copy-start(s32[1,16]{1,0:T(1,128)} %ids_ref.1) | copy-start | bytes 196
  7.2 15.1 %copy-start.2 = (s32[512,16,8]{0,2,1:T(8,128)S(1)}, s32[512,16,8]{0,2,1:T(8,128)}, u32[]{:S(2)}) copy-start(s32[512,16,8]{0,2,1:T(8,128)} %param.17) | copy-start | bytes 786436
  7.2 15.1 %copy-start.3 = (s32[512,16]{0,1:T(8,128)S(1)}, s32[512,16]{0,1:T(8,128)}, u32[]{:S(2)}) copy-start(s32[512,16]{0,1:T(8,128)} %param.18) | copy-start | bytes 98308
  7.2 15.1 %copy-start.1 = (bf16[2048,128]{1,0:T(8,128)(2,1)S(1)}, bf16[2048,128]{1,0:T(8,128)(2,1)}, u32[]{:S(2)}) copy-start(bf16[2048,128]{1,0:T(8,128)(2,1)} %rows_ref.3) | copy-start | bytes 1572868
  7.2 83.4 %all-gather.2.cloned.1.call-start = ((), (), s32[]{:S(2)}) async-start(), calls=%async_computation.3 | async-start | bytes 8454144 | tf_op jit(solution)/shard_map/all_gather | solution.py:402
  10.7 25.9 %all-to-all-start = ((f32[128,8,128]{2,1,0:T(8,128)}), f32[128,8,128]{2,1,0:T(8,128)S(1)}, u32[]{:S(2)}, u32[]{:S(2)}) async-start(f32[128,8,128]{2,1,0:T(8,128)} %maximum_maximum_fusion), calls=%async_computation | async-start | bytes 1048576 | tf_op jit(solution)/shard_map/all_to_all | solution.py:400
  40.6 24.2 %all-to-all-start.1 = ((bf16[128,16,128]{2,1,0:T(8,128)(2,1)}), bf16[128,16,128]{2,1,0:T(8,128)(2,1)S(1)}, u32[]{:S(2)}, u32[]{:S(2)}) async-start(bf16[128,16,128]{2,1,0:T(8,128)(2,1)} %hot_rows.1), calls=%async_computation.1 | async-start | bytes 1048576 | tf_op jit(solution)/shard_map/all_to_all | solution.py:412
  73.6 10.7 %collective-permute-start.2 = (bf16[512,1024]{1,0:T(8,128)(2,1)}, bf16[512,1024]{1,0:T(8,128)(2,1)}, u32[]{:S(2)}, u32[]{:S(2)}) collective-permute-start(bf16[512,1024]{1,0:T(8,128)(2,1)} %get-tuple-element.27.own_a), channel_id=1, source_target_pairs={{0,1},{1,0},{2,3},{3,2},{4,5},{5,4},{6,7},{7,6},{8,9},{9,8},{10,11... | collective-permute-start | bytes 3145736 | tf_op jit(solution)/shard_map/ppermute | solution.py:419
  74.5 9.4 %copy-start.5 = (s32[512]{0:T(512)S(1)}, s32[512]{0:T(512)}, u32[]{:S(2)}) copy-start(s32[512]{0:T(512)} %param.19) | copy-start | bytes 6148
  74.5 9.9 %copy-start.6 = (bf16[2048]{0:T(1024)(128)(2,1)S(1)}, bf16[2048]{0:T(1024)(128)(2,1)}, u32[]{:S(2)}) copy-start(bf16[2048]{0:T(1024)(128)(2,1)} %param.21) | copy-start | bytes 12292
  83.3 5.0 %collective-permute-start.3 = (bf16[512,1024]{1,0:T(8,128)(2,1)}, bf16[512,1024]{1,0:T(8,128)(2,1)}, u32[]{:S(2)}, u32[]{:S(2)}) collective-permute-start(bf16[512,1024]{1,0:T(8,128)(2,1)} %get-tuple-element.28.own_b), channel_id=1, source_target_pairs={{0,1},{1,0},{2,3},{3,2},{4,5},{5,4},{6,7},{7,6},{8,9},{9,8},{10,11... | collective-permute-start | bytes 3145736 | tf_op jit(solution)/shard_map/ppermute | solution.py:419
  83.3 19.2 %collective-permute-start = (bf16[1024,512]{1,0:T(8,128)(2,1)S(1)}, bf16[1024,512]{1,0:T(8,128)(2,1)}, u32[]{:S(2)}, u32[]{:S(2)}) collective-permute-start(bf16[1024,512]{1,0:T(8,128)(2,1)S(1)} %get-tuple-element.23.own_a), channel_id=1, source_target_pairs={{0,1},{1,0},{2,3},{3,2},{4,5},{5,4},{6,7},{7,6},{8,9},{9,8},{10,11... | collective-permute-start | bytes 3145736 | tf_op jit(solution)/shard_map/ppermute | solution.py:419
  83.8 18.7 %collective-permute-start.1 = (bf16[1024,512]{1,0:T(8,128)(2,1)S(1)}, bf16[1024,512]{1,0:T(8,128)(2,1)}, u32[]{:S(2)}, u32[]{:S(2)}) collective-permute-start(bf16[1024,512]{1,0:T(8,128)(2,1)S(1)} %get-tuple-element.26.own_b), channel_id=1, source_target_pairs={{0,1},{1,0},{2,3},{3,2},{4,5},{5,4},{6,7},{7,6},{8,9},{9,8},{10,11... | collective-permute-start | bytes 3145736 | tf_op jit(solution)/shard_map/ppermute | solution.py:419
  83.8 18.6 %collective-permute-start.5 = (f32[4,128]{1,0:T(4,128)S(1)}, f32[4,128]{1,0:T(4,128)S(1)}, u32[]{:S(2)}, u32[]{:S(2)}) collective-permute-start(f32[4,128]{1,0:T(4,128)S(1)} %convert_bitcast_fusion.1), channel_id=1, source_target_pairs={{0,1},{1,0},{2,3},{3,2},{4,5},{5,4},{6,7},{7,6},{8,9},{9,8},{10,11... | collective-permute-start | bytes 6152 | tf_op jit(solution)/shard_map/ppermute | solution.py:421
  101.9 1.5 collective-permute-start.4
  112.3 66.3 %all-to-all-start.2 = ((bf16[128,144,128]{2,1,0:T(8,128)(2,1)}), bf16[128,144,128]{2,1,0:T(8,128)(2,1)}, u32[]{:S(2)}, u32[]{:S(2)}) async-start(bf16[128,144,128]{2,1,0:T(8,128)(2,1)} %grad_terms.1), calls=%async_computation.2 | async-start | bytes 9437184 | tf_op jit(solution)/shard_map/all_to_all | solution.py:428
  120.0 4.1 %copy-start.4 = (f32[4096,128]{1,0:T(8,128)S(1)}, f32[4096,128]{1,0:T(8,128)}, u32[]{:S(2)}) copy-start(f32[4096,128]{1,0:T(8,128)} %table_ref.1) | copy-start | bytes 6291460
Sparse Core Ops, SparseCore 0:
  11.0 79.5 all-gather.1

commit v5 on v4

--- a/solution.py
+++ b/solution.py
@@ -261,8 +261,9 @@
         square = hidden * hidden
         t = jnp.tanh(hidden * (ROOT + ROOT * 0.044715 * square))
         near = 0.5 + 0.5 * t
-        act = (hidden * near).astype(jnp.bfloat16)
-        slope = near + 0.5 * hidden * (1.0 - t * t) * (ROOT + 3.0 * ROOT * 0.044715 * square)
+        value = hidden * near
+        act = value.astype(jnp.bfloat16)
+        slope = near + value * (1.0 - near) * (2.0 * ROOT + 6.0 * ROOT * 0.044715 * square)
         here = slice(ROW * m, ROW * m + ROW)
         act_ref[n, here] = act
         slope_ref[n, here] = slope * w
@@ -337,9 +338,7 @@
         total = jnp.sum(total, axis=0, keepdims=True)
         lines += [total[:, :128], total[:, 128:]]
         if c == steps - 1:
-            total = jnp.concatenate(lines, axis=0)
-            top = total.astype(jnp.bfloat16).astype(jnp.float32)
-            extra = jnp.concatenate([top, total - top], axis=0).astype(jnp.bfloat16)
+            extra = jnp.concatenate(lines, axis=0).astype(jnp.bfloat16)
 
             def place(d, carry):
                 blocks_ref[d, 32 * steps :] = extra
@@ -368,7 +367,7 @@
     steps = act.shape[0]
     far = pl.BlockSpec(memory_space=pltpu.HBM)
     inside = pl.BlockSpec(memory_space=pltpu.VMEM)
-    shape = (2 * deep // 16, 32 * steps + 16, 128)
+    shape = (2 * deep // 16, 32 * steps + 8, 128)
     return pl.pallas_call(
         grad_kernel,
         in_specs=[inside] * 9,
@@ -385,6 +384,45 @@
     )(*in_vmem(own_a, peer_a, own_b, peer_b, act, slope), logit, swapped, marks)
 
 
+def sum_kernel(terms_ref, grad_ref, out_ref, total_ref):
+    step = pl.program_id(0)
+    chips = terms_ref.shape[0] // 2
+    tall = terms_ref.shape[1]
+    rows = grad_ref.shape[0]
+    half = grad_ref.shape[1] // 2
+    for core in range(2):
+        for top in range(0, tall, 8):
+            part = jnp.zeros((8, 128), jnp.float32)
+            for chip in range(chips):
+                part = part + terms_ref[2 * chip + core, top : top + 8].astype(jnp.float32)
+            span = slice(top, top + 8)
+            total_ref[core, span] = jnp.where(step == 0, part, total_ref[core, span] + part)
+
+    @pl.when(step == pl.num_programs(0) - 1)
+    def _():
+        for core in range(2):
+            for c in range(half // 128):
+                at = half * core + 128 * c
+                grad_ref[:, at : at + 128] = total_ref[core, rows * c : rows * c + rows]
+            out_ref[8 * core : 8 * core + 8] = total_ref[core, tall - 8 :]
+
+
+def sum_call(terms, rows, wide):
+    devices, tall, _ = terms.shape
+    steps = 4
+    return pl.pallas_call(
+        sum_kernel,
+        grid=(steps,),
+        in_specs=[pl.BlockSpec((devices // steps, tall, 128), lambda n: (n, 0, 0))],
+        out_specs=[pl.BlockSpec((rows, wide), lambda n: (0, 0)), pl.BlockSpec((16, 128), lambda n: (0, 0))],
+        out_shape=[jax.ShapeDtypeStruct((rows, wide), jnp.float32), jax.ShapeDtypeStruct((16, 128), jnp.float32)],
+        scratch_shapes=[pltpu.VMEM((2, tall, 128), jnp.float32)],
+        compiler_params=pltpu.CompilerParams(vmem_limit_bytes=56 * MIB),
+        cost_estimate=pl.CostEstimate(flops=devices * tall * 128, bytes_accessed=5 << 20, transcendentals=0),
+        name="sum_terms",
+    )(terms)
+
+
 def per_device(
     table, accum, evict_delta, evict_ids, hot_ids, cache_old, bag_index, bag_length, labels, w_first, w_out
 ):
@@ -426,9 +464,8 @@
 
     blocks = grad_call(*across, act, slope, logit, swapped, marks)
     terms = lax.all_to_all(blocks, ALL, split_axis=0, concat_axis=0, tiled=True)
-    total = jnp.sum(terms.reshape((N_CHIPS, 2) + terms.shape[1:]).astype(jnp.float32), axis=0)
-    grad_w1 = total[:, : half // 8].reshape(2, half // 128, rows, 128).transpose(2, 0, 1, 3).reshape(rows, 2 * half)
-    grad_w2 = (total[:, half // 8 : half // 8 + 8] + total[:, half // 8 + 8 :]).reshape(-1)
+    grad_w1, out_lines = sum_call(terms, rows, 2 * half)
+    grad_w2 = out_lines.reshape(-1)
 
     summed = jnp.zeros_like(table).at[got_ids].add(got_delta)
     accum_new = accum + summed * summed

time: 190 us -> 186 us (0.979)
  other arithmetic: 14 us -> 10.4 us
  Pallas kernels: 70.5 us -> 74.1 us
  waiting for transfers between devices: 57.8 us -> 54.8 us
    pallas_call x0 -> x1, Pallas kernels: none -> 3.89 us  [sum_call(): pl.pallas_call(sum_kernel, grid=(steps,), in_specs=[pl.BlockSpec((devices...]
    all_to_all x1, waiting for transfers between devices: 49.9 us -> 46.8 us  [per_device(): terms = lax.all_to_all(blocks, ALL, split_axis=0, concat_axis=0, tiled=True)]
    reduce_sum x1 -> x0, other arithmetic: 3.02 us -> none  [per_device(): jnp.sum(terms.reshape((N_CHIPS, 2) + terms.shape[1:]).astype(jnp.float32)...]
  transfers between devices with their start and end apart: 10 -> 10, of which waited for: 5 -> 5; matrix products, arithmetic and copies ran while one was open for 6% -> 6% of each run, Pallas kernels for 32% -> 33%
where the time goes in v5:
time: 186 us
  Pallas kernels  74.1 us (40%)
  waiting for transfers between devices  54.8 us (29%)
  starting transfers between devices  31.3 us (17%)
  between operations  14.2 us (8%)
  other arithmetic  10.4 us (6%)
    all_to_all x1, waiting for transfers between devices, per_device(): terms = lax.all_to_all(blocks, ALL, split_axis=0, concat_axis=0, tiled=True)  46.8 us
    pallas_call x2, Pallas kernels, count_call(): pl.pallas_call(functools.partial(count_kernel, start), grid=(fields // GR...  28.6 us
    pallas_call x2, Pallas kernels, new_call(): pl.pallas_call(new_kernel, grid=(fields // GROUP,), in_specs=[pl.BlockSpe...  17.6 us
    all_to_all x1, starting transfers between devices, per_device(): got = lax.all_to_all(packet, ALL, split_axis=0, concat_axis=0, tiled=True)  11.5 us
    pallas_call x1, Pallas kernels, dense_call(): pl.pallas_call(dense_kernel, in_specs=[pl.BlockSpec(memory_space=pltpu.SM...  11 us
    all_to_all x1, starting transfers between devices, per_device(): lax.all_to_all(copies, ALL, split_axis=0, concat_axis=0, tiled=True)  9.76 us
    pallas_call x1, Pallas kernels, grad_call(): pl.pallas_call(grad_kernel, in_specs=[inside] * 9, out_specs=far, out_sha...  8.96 us
    all_to_all x1, starting transfers between devices, per_device(): terms = lax.all_to_all(blocks, ALL, split_axis=0, concat_axis=0, tiled=True)  7.56 us
  transfers between devices with their start and end apart: 10, of which 5 were waited for; matrix products, arithmetic and copies ran while one was open for 6% of the time, Pallas kernels for 33%

profile of v5, /device:TPU:1, one launch (start us, length us, event | category | flops | bytes accessed | tf_op | source)
XLA Modules:
  0.0 185.9 jit_solution(18210274259850228676)
XLA Ops:
  7.2 0.0 copy-start
  7.2 0.0 copy-start.2
  7.2 0.0 copy-start.3
  7.2 0.0 copy-start.1
  7.2 0.0 all-gather.2.cloned.1.call-start
  7.3 0.7 all-gather.2.cloned.1.call-update
  7.9 0.8 copy.16
  8.8 0.1 pad.14.clone
  8.8 1.9 %maximum_maximum_fusion = f32[128,8,128]{2,1,0:T(8,128)} fusion(f32[128,1,128]{2,1,0:T(1,128)S(1)} %bitcast.22, f32[128,4,128]{2,1,0:T(4,128)} %bitcast.21, f32[8]{0:T(128)S(1)} %pad.14.clone), kind=kLoop, calls=%fused_computation.5 | loop fusion | flops 262144 | bytes 852000 | tf_op jit(solution)/shard_map/concatenate | solution.py:437
  10.7 11.5 %all-to-all-start = ((f32[128,8,128]{2,1,0:T(8,128)}), f32[128,8,128]{2,1,0:T(8,128)S(1)}, u32[]{:S(2)}, u32[]{:S(2)}) async-start(f32[128,8,128]{2,1,0:T(8,128)} %maximum_maximum_fusion), calls=%async_computation | async-start | bytes 1048576 | tf_op jit(solution)/shard_map/all_to_all | solution.py:438
  22.2 0.0 copy-done
  22.2 0.0 copy-done.2
  22.3 0.0 copy-done.3
  22.3 0.0 copy-done.1
  22.3 14.3 %count_bags.2 = (s32[8,256,512]{2,1,0:T(8,128)}, f32[8,128,512]{2,1,0:T(8,128)}) custom-call(s32[16,8,512]{2,1,0:T(8,128)S(1)} %bitcast.17, s32[16,512]{1,0:T(8,128)S(1)} %bitcast.19, bf16[2048,128]{1,0:T(8,128)(2,1)S(1)} %copy-done.1), custom_call_target="tpu_custom_call" | custom-call | flops 2147483648 | bytes 20971520 | tf_op jit(solution)/shard_map/count_bags/pallas_call | solution.py:110
  36.6 0.0 all-to-all-done.got_ref
  36.6 4.0 %hot_rows.1 = bf16[128,16,128]{2,1,0:T(8,128)(2,1)} custom-call(s32[1,16]{1,0:T(1,128)S(1)} %copy-done, f32[128,8,128]{2,1,0:T(8,128)S(1)} %all-to-all-done.got_ref, f32[1,128]{1,0:T(1,128)S(1)} %pad.9.hot_ref, f32[4096,128]{1,0:T(8,128)} %table_ref.1, f32[4096,128]{1,0:T(8,128)} %accum_ref.1), custom_call_target="tpu_custom_call" | custom-call | flops 100663296 | bytes 1048576 | tf_op jit(solution)/shard_map/hot_rows/pallas_call | solution.py:222
  40.6 9.8 %all-to-all-start.1 = ((bf16[128,16,128]{2,1,0:T(8,128)(2,1)}), bf16[128,16,128]{2,1,0:T(8,128)(2,1)S(1)}, u32[]{:S(2)}, u32[]{:S(2)}) async-start(bf16[128,16,128]{2,1,0:T(8,128)(2,1)} %hot_rows.1), calls=%async_computation.1 | async-start | bytes 1048576 | tf_op jit(solution)/shard_map/all_to_all | solution.py:450
  50.4 14.3 %count_bags.3 = (s32[8,256,512]{2,1,0:T(8,128)}, f32[8,128,512]{2,1,0:T(8,128)}) custom-call(s32[16,8,512]{2,1,0:T(8,128)S(1)} %bitcast.18, s32[16,512]{1,0:T(8,128)S(1)} %bitcast.20, bf16[2048,128]{1,0:T(8,128)(2,1)S(1)} %copy-done.1), custom_call_target="tpu_custom_call" | custom-call | flops 2147483648 | bytes 20971520 | tf_op jit(solution)/shard_map/count_bags/pallas_call | solution.py:110
  64.7 0.1 all-to-all-done.1
  64.8 8.8 %pool_new.2 = (bf16[1024,512]{1,0:T(8,128)(2,1)S(1)}, bf16[512,1024]{1,0:T(8,128)(2,1)}) custom-call(s32[8,256,512]{2,1,0:T(8,128)} %get-tuple-element.23.words_ref, f32[8,128,512]{2,1,0:T(8,128)} %get-tuple-element.24.part_ref, bf16[2048,128]{1,0:T(8,128)(2,1)S(1)} %bitcast.14), custom_call_target="tpu_custom_call" | custom-call | flops 2147483648 | bytes 20971520 | tf_op jit(solution)/shard_map/pool_new/pallas_call | solution.py:161
  73.5 0.9 collective-permute-start.2
  74.4 0.0 copy-start.5
  74.4 0.0 copy-start.6
  74.5 8.9 %pool_new.3 = (bf16[1024,512]{1,0:T(8,128)(2,1)S(1)}, bf16[512,1024]{1,0:T(8,128)(2,1)}) custom-call(s32[8,256,512]{2,1,0:T(8,128)} %get-tuple-element.26.words_ref, f32[8,128,512]{2,1,0:T(8,128)} %get-tuple-element.27.part_ref, bf16[2048,128]{1,0:T(8,128)(2,1)S(1)} %bitcast.15), custom_call_target="tpu_custom_call" | custom-call | flops 2147483648 | bytes 20971520 | tf_op jit(solution)/shard_map/pool_new/pallas_call | solution.py:161
  83.3 0.0 collective-permute-start.3
  83.3 0.5 collective-permute-start
  83.8 0.0 collective-permute-start.1
  83.8 0.0 copy-done.5
  83.8 0.5 collective-permute-start.5
  84.3 0.0 copy-done.6
  84.3 0.0 collective-permute-done.2.peer_a
  84.3 3.7 %collective-permute-done.3.peer_b = bf16[512,1024]{1,0:T(8,128)(2,1)} collective-permute-done((bf16[512,1024]{1,0:T(8,128)(2,1)}, bf16[512,1024]{1,0:T(8,128)(2,1)}, u32[]{:S(2)}, u32[]{:S(2)}) %collective-permute-start.3) | collective-permute-done | bytes 1048608 | tf_op jit(solution)/shard_map/ppermute | solution.py:457
  88.1 2.6 %all-gather.2.cloned.1.call-done.weight_ref = bf16[2048,2048]{1,0:T(8,128)(2,1)} async-done(((bf16[16,2048]{1,0:T(8,128)(2,1)}), bf16[2048,2048]{1,0:T(8,128)(2,1)}) %all-gather.2.cloned.1.call-update) | async-done | bytes 8388624 | tf_op jit(solution)/shard_map/all_gather | solution.py:440
  90.7 11.0 %dense_forward.1 = (bf16[4,1024,256]{2,1,0:T(8,128)(2,1)S(1)}, f32[4,1024,256]{2,1,0:T(8,128)S(1)}, f32[8,128]{1,0:T(8,128)S(1)}) custom-call(s32[1]{0:T(128)} %bitcast.8.core_ref, bf16[512,1024]{1,0:T(8,128)(2,1)} %get-tuple-element.29.own_a, bf16[512,1024]{1,0:T(8,128)(2,1)} %collective-permute-done.2.peer_a, bf16[512,1024]{1,0:T(8,128)(2,1)} %get-tuple-element.30.own_b, ...), custom_call_target="tpu_custom_call" | custom-call | flops 4294967296 | bytes 14680064 | tf_op jit(solution)/shard_map/dense_forward/pallas_call | solution.py:298
  101.7 0.6 collective-permute-start.4
  102.2 0.0 collective-permute-done.5
  102.3 0.0 collective-permute-done.peer_a
  102.3 0.0 collective-permute-done.1.peer_b
  102.3 0.9 collective-permute-done.4.swapped_ref
  103.2 9.0 %grad_terms.1 = bf16[128,136,128]{2,1,0:T(8,128)(2,1)} custom-call(bf16[1024,512]{1,0:T(8,128)(2,1)S(1)} %get-tuple-element.25.own_a, bf16[1024,512]{1,0:T(8,128)(2,1)} %collective-permute-done.peer_a, bf16[1024,512]{1,0:T(8,128)(2,1)S(1)} %get-tuple-element.28.own_b, bf16[1024,512]{1,0:T(8,128)(2,1)} %collective-permute-done.1.peer_b, ...), custom_call_target="tpu_custom_call" | custom-call | flops 4294967296 | bytes 14680064 | tf_op jit(solution)/shard_map/grad_terms/pallas_call | solution.py:371
  112.1 7.6 %all-to-all-start.2 = ((bf16[128,136,128]{2,1,0:T(8,128)(2,1)}), bf16[128,136,128]{2,1,0:T(8,128)(2,1)}, u32[]{:S(2)}, u32[]{:S(2)}) async-start(bf16[128,136,128]{2,1,0:T(8,128)(2,1)} %grad_terms.1), calls=%async_computation.2 | async-start | bytes 8912896 | tf_op jit(solution)/shard_map/all_to_all | solution.py:466
  119.7 0.0 copy-start.4
  119.8 0.2 convert_reduce_fusion
  120.0 0.1 convert_element_type.32
  120.1 3.6 %scatter_custom_fusion = f32[4096,128]{1,0:T(8,128)} fusion(s32[512]{0:T(512)S(1)} %bitcast.24, f32[512,128]{1,0:T(8,128)S(1)} %bitcast.23, f32[]{:T(128)} %constant.8.clone.1), kind=kCustom, calls=%fused_computation.3 | custom fusion | flops 65536 | bytes 2097156 | tf_op jit(solution)/shard_map/scatter-add | solution.py:470
  123.8 0.0 copy-done.4
  123.8 4.6 %multiply_subtract_fusion = (f32[4096,128]{1,0:T(8,128)}, f32[4096,128]{1,0:T(8,128)}) fusion(f32[4096,128]{1,0:T(8,128)S(1)} %copy-done.4, f32[4096,128]{1,0:T(8,128)} %scatter_custom_fusion, f32[4096,128]{1,0:T(8,128)} %accum_ref.1), kind=kLoop, calls=%fused_computation.1 | loop fusion | flops 2621440 | bytes 10485760 | tf_op jit(solution)/shard_map/sub | solution.py:472
  128.4 46.8 %all-to-all-done.2.terms_ref = bf16[128,136,128]{2,1,0:T(8,128)(2,1)} async-done(((bf16[128,136,128]{2,1,0:T(8,128)(2,1)}), bf16[128,136,128]{2,1,0:T(8,128)(2,1)}, u32[]{:S(2)}, u32[]{:S(2)}) %all-to-all-start.2) | async-done | bytes 4456480 | tf_op jit(solution)/shard_map/all_to_all | solution.py:466
  175.2 3.9 %sum_terms.1 = (f32[16,2048]{1,0:T(8,128)}, f32[16,128]{1,0:T(8,128)}) custom-call(bf16[128,136,128]{2,1,0:T(8,128)(2,1)} %all-to-all-done.2.terms_ref), custom_call_target="tpu_custom_call" | custom-call | flops 2228224 | bytes 5242880 | tf_op jit(solution)/shard_map/sum_terms/pallas_call | solution.py:413
  (10 shorter events, 0.1 us)
Async XLA Ops:
  7.2 15.0 %copy-start = (s32[1,16]{1,0:T(1,128)S(1)}, s32[1,16]{1,0:T(1,128)}, u32[]{:S(2)}) copy-start(s32[1,16]{1,0:T(1,128)} %ids_ref.1) | copy-start | bytes 196
  7.2 15.1 %copy-start.2 = (s32[512,16,8]{0,2,1:T(8,128)S(1)}, s32[512,16,8]{0,2,1:T(8,128)}, u32[]{:S(2)}) copy-start(s32[512,16,8]{0,2,1:T(8,128)} %param.17) | copy-start | bytes 786436
  7.2 15.1 %copy-start.3 = (s32[512,16]{0,1:T(8,128)S(1)}, s32[512,16]{0,1:T(8,128)}, u32[]{:S(2)}) copy-start(s32[512,16]{0,1:T(8,128)} %param.18) | copy-start | bytes 98308
  7.2 15.1 %copy-start.1 = (bf16[2048,128]{1,0:T(8,128)(2,1)S(1)}, bf16[2048,128]{1,0:T(8,128)(2,1)}, u32[]{:S(2)}) copy-start(bf16[2048,128]{1,0:T(8,128)(2,1)} %rows_ref.3) | copy-start | bytes 1572868
  7.2 83.5 %all-gather.2.cloned.1.call-start = ((), (), s32[]{:S(2)}) async-start(), calls=%async_computation.3 | async-start | bytes 8454144 | tf_op jit(solution)/shard_map/all_gather | solution.py:440
  10.7 25.9 %all-to-all-start = ((f32[128,8,128]{2,1,0:T(8,128)}), f32[128,8,128]{2,1,0:T(8,128)S(1)}, u32[]{:S(2)}, u32[]{:S(2)}) async-start(f32[128,8,128]{2,1,0:T(8,128)} %maximum_maximum_fusion), calls=%async_computation | async-start | bytes 1048576 | tf_op jit(solution)/shard_map/all_to_all | solution.py:438
  40.6 24.2 %all-to-all-start.1 = ((bf16[128,16,128]{2,1,0:T(8,128)(2,1)}), bf16[128,16,128]{2,1,0:T(8,128)(2,1)S(1)}, u32[]{:S(2)}, u32[]{:S(2)}) async-start(bf16[128,16,128]{2,1,0:T(8,128)(2,1)} %hot_rows.1), calls=%async_computation.1 | async-start | bytes 1048576 | tf_op jit(solution)/shard_map/all_to_all | solution.py:450
  73.5 10.8 %collective-permute-start.2 = (bf16[512,1024]{1,0:T(8,128)(2,1)}, bf16[512,1024]{1,0:T(8,128)(2,1)}, u32[]{:S(2)}, u32[]{:S(2)}) collective-permute-start(bf16[512,1024]{1,0:T(8,128)(2,1)} %get-tuple-element.29.own_a), channel_id=1, source_target_pairs={{0,1},{1,0},{2,3},{3,2},{4,5},{5,4},{6,7},{7,6},{8,9},{9,8},{10,11... | collective-permute-start | bytes 3145736 | tf_op jit(solution)/shard_map/ppermute | solution.py:457
  74.4 9.4 %copy-start.5 = (s32[512]{0:T(512)S(1)}, s32[512]{0:T(512)}, u32[]{:S(2)}) copy-start(s32[512]{0:T(512)} %param.19) | copy-start | bytes 6148
  74.4 9.9 %copy-start.6 = (bf16[2048]{0:T(1024)(128)(2,1)S(1)}, bf16[2048]{0:T(1024)(128)(2,1)}, u32[]{:S(2)}) copy-start(bf16[2048]{0:T(1024)(128)(2,1)} %param.21) | copy-start | bytes 12292
  83.3 4.8 %collective-permute-start.3 = (bf16[512,1024]{1,0:T(8,128)(2,1)}, bf16[512,1024]{1,0:T(8,128)(2,1)}, u32[]{:S(2)}, u32[]{:S(2)}) collective-permute-start(bf16[512,1024]{1,0:T(8,128)(2,1)} %get-tuple-element.30.own_b), channel_id=1, source_target_pairs={{0,1},{1,0},{2,3},{3,2},{4,5},{5,4},{6,7},{7,6},{8,9},{9,8},{10,11... | collective-permute-start | bytes 3145736 | tf_op jit(solution)/shard_map/ppermute | solution.py:457
  83.3 19.0 %collective-permute-start = (bf16[1024,512]{1,0:T(8,128)(2,1)S(1)}, bf16[1024,512]{1,0:T(8,128)(2,1)}, u32[]{:S(2)}, u32[]{:S(2)}) collective-permute-start(bf16[1024,512]{1,0:T(8,128)(2,1)S(1)} %get-tuple-element.25.own_a), channel_id=1, source_target_pairs={{0,1},{1,0},{2,3},{3,2},{4,5},{5,4},{6,7},{7,6},{8,9},{9,8},{10,11... | collective-permute-start | bytes 3145736 | tf_op jit(solution)/shard_map/ppermute | solution.py:457
  83.8 18.5 %collective-permute-start.1 = (bf16[1024,512]{1,0:T(8,128)(2,1)S(1)}, bf16[1024,512]{1,0:T(8,128)(2,1)}, u32[]{:S(2)}, u32[]{:S(2)}) collective-permute-start(bf16[1024,512]{1,0:T(8,128)(2,1)S(1)} %get-tuple-element.28.own_b), channel_id=1, source_target_pairs={{0,1},{1,0},{2,3},{3,2},{4,5},{5,4},{6,7},{7,6},{8,9},{9,8},{10,11... | collective-permute-start | bytes 3145736 | tf_op jit(solution)/shard_map/ppermute | solution.py:457
  83.8 18.4 %collective-permute-start.5 = (f32[4,128]{1,0:T(4,128)S(1)}, f32[4,128]{1,0:T(4,128)S(1)}, u32[]{:S(2)}, u32[]{:S(2)}) collective-permute-start(f32[4,128]{1,0:T(4,128)S(1)} %convert_bitcast_fusion.1), channel_id=1, source_target_pairs={{0,1},{1,0},{2,3},{3,2},{4,5},{5,4},{6,7},{7,6},{8,9},{9,8},{10,11... | collective-permute-start | bytes 6152 | tf_op jit(solution)/shard_map/ppermute | solution.py:459
  101.7 1.5 collective-permute-start.4
  112.1 63.0 %all-to-all-start.2 = ((bf16[128,136,128]{2,1,0:T(8,128)(2,1)}), bf16[128,136,128]{2,1,0:T(8,128)(2,1)}, u32[]{:S(2)}, u32[]{:S(2)}) async-start(bf16[128,136,128]{2,1,0:T(8,128)(2,1)} %grad_terms.1), calls=%async_computation.2 | async-start | bytes 8912896 | tf_op jit(solution)/shard_map/all_to_all | solution.py:466
  119.7 4.1 %copy-start.4 = (f32[4096,128]{1,0:T(8,128)S(1)}, f32[4096,128]{1,0:T(8,128)}, u32[]{:S(2)}) copy-start(f32[4096,128]{1,0:T(8,128)} %table_ref.1) | copy-start | bytes 6291460
Sparse Core Ops, SparseCore 0:
  11.0 79.6 all-gather.1

commit v6 on v5

--- a/solution.py
+++ b/solution.py
@@ -391,11 +391,12 @@
     rows = grad_ref.shape[0]
     half = grad_ref.shape[1] // 2
     for core in range(2):
-        for top in range(0, tall, 8):
-            part = jnp.zeros((8, 128), jnp.float32)
+        for top in range(0, tall, 16):
+            size = min(16, tall - top)
+            part = jnp.zeros((size, 128), jnp.float32)
             for chip in range(chips):
-                part = part + terms_ref[2 * chip + core, top : top + 8].astype(jnp.float32)
-            span = slice(top, top + 8)
+                part = part + terms_ref[2 * chip + core, top : top + size].astype(jnp.float32)
+            span = slice(top, top + size)
             total_ref[core, span] = jnp.where(step == 0, part, total_ref[core, span] + part)
 
     @pl.when(step == pl.num_programs(0) - 1)
@@ -409,7 +410,7 @@
 
 def sum_call(terms, rows, wide):
     devices, tall, _ = terms.shape
-    steps = 4
+    steps = 2
     return pl.pallas_call(
         sum_kernel,
         grid=(steps,),

time: 186 us -> 186 us (level)
  no operation moved by 1% of the time
where the time goes in v6:
time: 186 us; the launch traced here: 185 us
  Pallas kernels  73.5 us (40%)
  waiting for transfers between devices  54.8 us (29%)
  starting transfers between devices  31.3 us (17%)
  between operations  14.2 us (8%)
  other arithmetic  10.4 us (6%)
    all_to_all x1, waiting for transfers between devices, per_device(): terms = lax.all_to_all(blocks, ALL, split_axis=0, concat_axis=0, tiled=True)  46.8 us
    pallas_call x2, Pallas kernels, count_call(): pl.pallas_call(functools.partial(count_kernel, start), grid=(fields // GR...  28.6 us
    pallas_call x2, Pallas kernels, new_call(): pl.pallas_call(new_kernel, grid=(fields // GROUP,), in_specs=[pl.BlockSpe...  17.6 us
    all_to_all x1, starting transfers between devices, per_device(): got = lax.all_to_all(packet, ALL, split_axis=0, concat_axis=0, tiled=True)  11.5 us
    pallas_call x1, Pallas kernels, dense_call(): pl.pallas_call(dense_kernel, in_specs=[pl.BlockSpec(memory_space=pltpu.SM...  11 us
    all_to_all x1, starting transfers between devices, per_device(): lax.all_to_all(copies, ALL, split_axis=0, concat_axis=0, tiled=True)  9.76 us
    pallas_call x1, Pallas kernels, grad_call(): pl.pallas_call(grad_kernel, in_specs=[inside] * 9, out_specs=far, out_sha...  8.96 us
    all_to_all x1, starting transfers between devices, per_device(): terms = lax.all_to_all(blocks, ALL, split_axis=0, concat_axis=0, tiled=True)  7.56 us
  transfers between devices with their start and end apart: 10, of which 5 were waited for; matrix products, arithmetic and copies ran while one was open for 6% of the time, Pallas kernels for 33%

profile of v6, /device:TPU:1, one launch (start us, length us, event | category | flops | bytes accessed | tf_op | source)
XLA Modules:
  0.0 185.3 jit_solution(7081969172884224493)
XLA Ops:
  7.2 0.0 copy-start
  7.2 0.0 copy-start.2
  7.2 0.0 copy-start.3
  7.2 0.0 copy-start.1
  7.2 0.0 all-gather.2.cloned.1.call-start
  7.3 0.7 all-gather.2.cloned.1.call-update
  7.9 0.8 copy.16
  8.8 0.1 pad.14.clone
  8.8 1.9 %maximum_maximum_fusion = f32[128,8,128]{2,1,0:T(8,128)} fusion(f32[128,1,128]{2,1,0:T(1,128)S(1)} %bitcast.22, f32[128,4,128]{2,1,0:T(4,128)} %bitcast.21, f32[8]{0:T(128)S(1)} %pad.14.clone), kind=kLoop, calls=%fused_computation.5 | loop fusion | flops 262144 | bytes 852000 | tf_op jit(solution)/shard_map/concatenate | solution.py:438
  10.7 11.5 %all-to-all-start = ((f32[128,8,128]{2,1,0:T(8,128)}), f32[128,8,128]{2,1,0:T(8,128)S(1)}, u32[]{:S(2)}, u32[]{:S(2)}) async-start(f32[128,8,128]{2,1,0:T(8,128)} %maximum_maximum_fusion), calls=%async_computation | async-start | bytes 1048576 | tf_op jit(solution)/shard_map/all_to_all | solution.py:439
  22.2 0.0 copy-done
  22.2 0.0 copy-done.2
  22.3 0.0 copy-done.3
  22.3 0.0 copy-done.1
  22.3 14.3 %count_bags.2 = (s32[8,256,512]{2,1,0:T(8,128)}, f32[8,128,512]{2,1,0:T(8,128)}) custom-call(s32[16,8,512]{2,1,0:T(8,128)S(1)} %bitcast.17, s32[16,512]{1,0:T(8,128)S(1)} %bitcast.19, bf16[2048,128]{1,0:T(8,128)(2,1)S(1)} %copy-done.1), custom_call_target="tpu_custom_call" | custom-call | flops 2147483648 | bytes 20971520 | tf_op jit(solution)/shard_map/count_bags/pallas_call | solution.py:110
  36.6 0.0 all-to-all-done.got_ref
  36.6 4.0 %hot_rows.1 = bf16[128,16,128]{2,1,0:T(8,128)(2,1)} custom-call(s32[1,16]{1,0:T(1,128)S(1)} %copy-done, f32[128,8,128]{2,1,0:T(8,128)S(1)} %all-to-all-done.got_ref, f32[1,128]{1,0:T(1,128)S(1)} %pad.9.hot_ref, f32[4096,128]{1,0:T(8,128)} %table_ref.1, f32[4096,128]{1,0:T(8,128)} %accum_ref.1), custom_call_target="tpu_custom_call" | custom-call | flops 100663296 | bytes 1048576 | tf_op jit(solution)/shard_map/hot_rows/pallas_call | solution.py:222
  40.6 9.8 %all-to-all-start.1 = ((bf16[128,16,128]{2,1,0:T(8,128)(2,1)}), bf16[128,16,128]{2,1,0:T(8,128)(2,1)S(1)}, u32[]{:S(2)}, u32[]{:S(2)}) async-start(bf16[128,16,128]{2,1,0:T(8,128)(2,1)} %hot_rows.1), calls=%async_computation.1 | async-start | bytes 1048576 | tf_op jit(solution)/shard_map/all_to_all | solution.py:451
  50.4 14.3 %count_bags.3 = (s32[8,256,512]{2,1,0:T(8,128)}, f32[8,128,512]{2,1,0:T(8,128)}) custom-call(s32[16,8,512]{2,1,0:T(8,128)S(1)} %bitcast.18, s32[16,512]{1,0:T(8,128)S(1)} %bitcast.20, bf16[2048,128]{1,0:T(8,128)(2,1)S(1)} %copy-done.1), custom_call_target="tpu_custom_call" | custom-call | flops 2147483648 | bytes 20971520 | tf_op jit(solution)/shard_map/count_bags/pallas_call | solution.py:110
  64.7 0.1 all-to-all-done.1
  64.8 8.8 %pool_new.2 = (bf16[1024,512]{1,0:T(8,128)(2,1)S(1)}, bf16[512,1024]{1,0:T(8,128)(2,1)}) custom-call(s32[8,256,512]{2,1,0:T(8,128)} %get-tuple-element.23.words_ref, f32[8,128,512]{2,1,0:T(8,128)} %get-tuple-element.24.part_ref, bf16[2048,128]{1,0:T(8,128)(2,1)S(1)} %bitcast.14), custom_call_target="tpu_custom_call" | custom-call | flops 2147483648 | bytes 20971520 | tf_op jit(solution)/shard_map/pool_new/pallas_call | solution.py:161
  73.5 0.9 collective-permute-start.2
  74.4 0.0 copy-start.5
  74.4 0.0 copy-start.6
  74.5 8.9 %pool_new.3 = (bf16[1024,512]{1,0:T(8,128)(2,1)S(1)}, bf16[512,1024]{1,0:T(8,128)(2,1)}) custom-call(s32[8,256,512]{2,1,0:T(8,128)} %get-tuple-element.26.words_ref, f32[8,128,512]{2,1,0:T(8,128)} %get-tuple-element.27.part_ref, bf16[2048,128]{1,0:T(8,128)(2,1)S(1)} %bitcast.15), custom_call_target="tpu_custom_call" | custom-call | flops 2147483648 | bytes 20971520 | tf_op jit(solution)/shard_map/pool_new/pallas_call | solution.py:161
  83.3 0.0 collective-permute-start.3
  83.3 0.5 collective-permute-start
  83.8 0.0 collective-permute-start.1
  83.8 0.0 copy-done.5
  83.8 0.5 collective-permute-start.5
  84.3 0.0 copy-done.6
  84.3 0.0 collective-permute-done.2.peer_a
  84.3 3.7 %collective-permute-done.3.peer_b = bf16[512,1024]{1,0:T(8,128)(2,1)} collective-permute-done((bf16[512,1024]{1,0:T(8,128)(2,1)}, bf16[512,1024]{1,0:T(8,128)(2,1)}, u32[]{:S(2)}, u32[]{:S(2)}) %collective-permute-start.3) | collective-permute-done | bytes 1048608 | tf_op jit(solution)/shard_map/ppermute | solution.py:458
  88.1 2.6 %all-gather.2.cloned.1.call-done.weight_ref = bf16[2048,2048]{1,0:T(8,128)(2,1)} async-done(((bf16[16,2048]{1,0:T(8,128)(2,1)}), bf16[2048,2048]{1,0:T(8,128)(2,1)}) %all-gather.2.cloned.1.call-update) | async-done | bytes 8388624 | tf_op jit(solution)/shard_map/all_gather | solution.py:441
  90.7 11.0 %dense_forward.1 = (bf16[4,1024,256]{2,1,0:T(8,128)(2,1)S(1)}, f32[4,1024,256]{2,1,0:T(8,128)S(1)}, f32[8,128]{1,0:T(8,128)S(1)}) custom-call(s32[1]{0:T(128)} %bitcast.8.core_ref, bf16[512,1024]{1,0:T(8,128)(2,1)} %get-tuple-element.29.own_a, bf16[512,1024]{1,0:T(8,128)(2,1)} %collective-permute-done.2.peer_a, bf16[512,1024]{1,0:T(8,128)(2,1)} %get-tuple-element.30.own_b, ...), custom_call_target="tpu_custom_call" | custom-call | flops 4294967296 | bytes 14680064 | tf_op jit(solution)/shard_map/dense_forward/pallas_call | solution.py:298
  101.7 0.6 collective-permute-start.4
  102.2 0.0 collective-permute-done.5
  102.3 0.0 collective-permute-done.peer_a
  102.3 0.0 collective-permute-done.1.peer_b
  102.3 0.9 collective-permute-done.4.swapped_ref
  103.2 9.0 %grad_terms.1 = bf16[128,136,128]{2,1,0:T(8,128)(2,1)} custom-call(bf16[1024,512]{1,0:T(8,128)(2,1)S(1)} %get-tuple-element.25.own_a, bf16[1024,512]{1,0:T(8,128)(2,1)} %collective-permute-done.peer_a, bf16[1024,512]{1,0:T(8,128)(2,1)S(1)} %get-tuple-element.28.own_b, bf16[1024,512]{1,0:T(8,128)(2,1)} %collective-permute-done.1.peer_b, ...), custom_call_target="tpu_custom_call" | custom-call | flops 4294967296 | bytes 14680064 | tf_op jit(solution)/shard_map/grad_terms/pallas_call | solution.py:371
  112.1 7.6 %all-to-all-start.2 = ((bf16[128,136,128]{2,1,0:T(8,128)(2,1)}), bf16[128,136,128]{2,1,0:T(8,128)(2,1)}, u32[]{:S(2)}, u32[]{:S(2)}) async-start(bf16[128,136,128]{2,1,0:T(8,128)(2,1)} %grad_terms.1), calls=%async_computation.2 | async-start | bytes 8912896 | tf_op jit(solution)/shard_map/all_to_all | solution.py:467
  119.7 0.0 copy-start.4
  119.8 0.2 convert_reduce_fusion
  120.0 0.1 convert_element_type.32
  120.1 3.6 %scatter_custom_fusion = f32[4096,128]{1,0:T(8,128)} fusion(s32[512]{0:T(512)S(1)} %bitcast.24, f32[512,128]{1,0:T(8,128)S(1)} %bitcast.23, f32[]{:T(128)} %constant.8.clone.1), kind=kCustom, calls=%fused_computation.3 | custom fusion | flops 65536 | bytes 2097156 | tf_op jit(solution)/shard_map/scatter-add | solution.py:471
  123.8 0.0 copy-done.4
  123.8 4.6 %multiply_subtract_fusion = (f32[4096,128]{1,0:T(8,128)}, f32[4096,128]{1,0:T(8,128)}) fusion(f32[4096,128]{1,0:T(8,128)S(1)} %copy-done.4, f32[4096,128]{1,0:T(8,128)} %scatter_custom_fusion, f32[4096,128]{1,0:T(8,128)} %accum_ref.1), kind=kLoop, calls=%fused_computation.1 | loop fusion | flops 2621440 | bytes 10485760 | tf_op jit(solution)/shard_map/sub | solution.py:473
  128.4 46.8 %all-to-all-done.2.terms_ref = bf16[128,136,128]{2,1,0:T(8,128)(2,1)} async-done(((bf16[128,136,128]{2,1,0:T(8,128)(2,1)}), bf16[128,136,128]{2,1,0:T(8,128)(2,1)}, u32[]{:S(2)}, u32[]{:S(2)}) %all-to-all-start.2) | async-done | bytes 4456480 | tf_op jit(solution)/shard_map/all_to_all | solution.py:467
  175.2 3.3 %sum_terms.1 = (f32[16,2048]{1,0:T(8,128)}, f32[16,128]{1,0:T(8,128)}) custom-call(bf16[128,136,128]{2,1,0:T(8,128)(2,1)} %all-to-all-done.2.terms_ref), custom_call_target="tpu_custom_call" | custom-call | flops 2228224 | bytes 5242880 | tf_op jit(solution)/shard_map/sum_terms/pallas_call | solution.py:414
  (10 shorter events, 0.1 us)
Async XLA Ops:
  7.2 15.0 %copy-start = (s32[1,16]{1,0:T(1,128)S(1)}, s32[1,16]{1,0:T(1,128)}, u32[]{:S(2)}) copy-start(s32[1,16]{1,0:T(1,128)} %ids_ref.1) | copy-start | bytes 196
  7.2 15.1 %copy-start.2 = (s32[512,16,8]{0,2,1:T(8,128)S(1)}, s32[512,16,8]{0,2,1:T(8,128)}, u32[]{:S(2)}) copy-start(s32[512,16,8]{0,2,1:T(8,128)} %param.17) | copy-start | bytes 786436
  7.2 15.1 %copy-start.3 = (s32[512,16]{0,1:T(8,128)S(1)}, s32[512,16]{0,1:T(8,128)}, u32[]{:S(2)}) copy-start(s32[512,16]{0,1:T(8,128)} %param.18) | copy-start | bytes 98308
  7.2 15.1 %copy-start.1 = (bf16[2048,128]{1,0:T(8,128)(2,1)S(1)}, bf16[2048,128]{1,0:T(8,128)(2,1)}, u32[]{:S(2)}) copy-start(bf16[2048,128]{1,0:T(8,128)(2,1)} %rows_ref.3) | copy-start | bytes 1572868
  7.2 83.5 %all-gather.2.cloned.1.call-start = ((), (), s32[]{:S(2)}) async-start(), calls=%async_computation.3 | async-start | bytes 8454144 | tf_op jit(solution)/shard_map/all_gather | solution.py:441
  10.7 25.9 %all-to-all-start = ((f32[128,8,128]{2,1,0:T(8,128)}), f32[128,8,128]{2,1,0:T(8,128)S(1)}, u32[]{:S(2)}, u32[]{:S(2)}) async-start(f32[128,8,128]{2,1,0:T(8,128)} %maximum_maximum_fusion), calls=%async_computation | async-start | bytes 1048576 | tf_op jit(solution)/shard_map/all_to_all | solution.py:439
  40.6 24.2 %all-to-all-start.1 = ((bf16[128,16,128]{2,1,0:T(8,128)(2,1)}), bf16[128,16,128]{2,1,0:T(8,128)(2,1)S(1)}, u32[]{:S(2)}, u32[]{:S(2)}) async-start(bf16[128,16,128]{2,1,0:T(8,128)(2,1)} %hot_rows.1), calls=%async_computation.1 | async-start | bytes 1048576 | tf_op jit(solution)/shard_map/all_to_all | solution.py:451
  73.5 10.8 %collective-permute-start.2 = (bf16[512,1024]{1,0:T(8,128)(2,1)}, bf16[512,1024]{1,0:T(8,128)(2,1)}, u32[]{:S(2)}, u32[]{:S(2)}) collective-permute-start(bf16[512,1024]{1,0:T(8,128)(2,1)} %get-tuple-element.29.own_a), channel_id=1, source_target_pairs={{0,1},{1,0},{2,3},{3,2},{4,5},{5,4},{6,7},{7,6},{8,9},{9,8},{10,11... | collective-permute-start | bytes 3145736 | tf_op jit(solution)/shard_map/ppermute | solution.py:458
  74.4 9.4 %copy-start.5 = (s32[512]{0:T(512)S(1)}, s32[512]{0:T(512)}, u32[]{:S(2)}) copy-start(s32[512]{0:T(512)} %param.19) | copy-start | bytes 6148
  74.4 9.9 %copy-start.6 = (bf16[2048]{0:T(1024)(128)(2,1)S(1)}, bf16[2048]{0:T(1024)(128)(2,1)}, u32[]{:S(2)}) copy-start(bf16[2048]{0:T(1024)(128)(2,1)} %param.21) | copy-start | bytes 12292
  83.3 4.8 %collective-permute-start.3 = (bf16[512,1024]{1,0:T(8,128)(2,1)}, bf16[512,1024]{1,0:T(8,128)(2,1)}, u32[]{:S(2)}, u32[]{:S(2)}) collective-permute-start(bf16[512,1024]{1,0:T(8,128)(2,1)} %get-tuple-element.30.own_b), channel_id=1, source_target_pairs={{0,1},{1,0},{2,3},{3,2},{4,5},{5,4},{6,7},{7,6},{8,9},{9,8},{10,11... | collective-permute-start | bytes 3145736 | tf_op jit(solution)/shard_map/ppermute | solution.py:458
  83.3 19.0 %collective-permute-start = (bf16[1024,512]{1,0:T(8,128)(2,1)S(1)}, bf16[1024,512]{1,0:T(8,128)(2,1)}, u32[]{:S(2)}, u32[]{:S(2)}) collective-permute-start(bf16[1024,512]{1,0:T(8,128)(2,1)S(1)} %get-tuple-element.25.own_a), channel_id=1, source_target_pairs={{0,1},{1,0},{2,3},{3,2},{4,5},{5,4},{6,7},{7,6},{8,9},{9,8},{10,11... | collective-permute-start | bytes 3145736 | tf_op jit(solution)/shard_map/ppermute | solution.py:458
  83.8 18.5 %collective-permute-start.1 = (bf16[1024,512]{1,0:T(8,128)(2,1)S(1)}, bf16[1024,512]{1,0:T(8,128)(2,1)}, u32[]{:S(2)}, u32[]{:S(2)}) collective-permute-start(bf16[1024,512]{1,0:T(8,128)(2,1)S(1)} %get-tuple-element.28.own_b), channel_id=1, source_target_pairs={{0,1},{1,0},{2,3},{3,2},{4,5},{5,4},{6,7},{7,6},{8,9},{9,8},{10,11... | collective-permute-start | bytes 3145736 | tf_op jit(solution)/shard_map/ppermute | solution.py:458
  83.8 18.4 %collective-permute-start.5 = (f32[4,128]{1,0:T(4,128)S(1)}, f32[4,128]{1,0:T(4,128)S(1)}, u32[]{:S(2)}, u32[]{:S(2)}) collective-permute-start(f32[4,128]{1,0:T(4,128)S(1)} %convert_bitcast_fusion.1), channel_id=1, source_target_pairs={{0,1},{1,0},{2,3},{3,2},{4,5},{5,4},{6,7},{7,6},{8,9},{9,8},{10,11... | collective-permute-start | bytes 6152 | tf_op jit(solution)/shard_map/ppermute | solution.py:460
  101.7 1.5 collective-permute-start.4
  112.1 63.0 %all-to-all-start.2 = ((bf16[128,136,128]{2,1,0:T(8,128)(2,1)}), bf16[128,136,128]{2,1,0:T(8,128)(2,1)}, u32[]{:S(2)}, u32[]{:S(2)}) async-start(bf16[128,136,128]{2,1,0:T(8,128)(2,1)} %grad_terms.1), calls=%async_computation.2 | async-start | bytes 8912896 | tf_op jit(solution)/shard_map/all_to_all | solution.py:467
  119.7 4.1 %copy-start.4 = (f32[4096,128]{1,0:T(8,128)S(1)}, f32[4096,128]{1,0:T(8,128)}, u32[]{:S(2)}) copy-start(f32[4096,128]{1,0:T(8,128)} %table_ref.1) | copy-start | bytes 6291460
Sparse Core Ops, SparseCore 0:
  11.0 79.6 all-gather.1

commit v7 on v6

--- a/solution.py
+++ b/solution.py
@@ -237,11 +237,35 @@
     )(ids, got, hot, *in_hbm(table, accum))
 
 
+def stage_kernel(own_a, peer_a, own_b, peer_b, sides_ref, sems):
+    fetches = [
+        pltpu.make_async_copy(side, sides_ref.at[i], sems.at[i]) for i, side in enumerate((own_a, peer_a, own_b, peer_b))
+    ]
+    for fetch in fetches:
+        fetch.start()
+    for fetch in fetches:
+        fetch.wait()
+
+
+def stage_call(*sides):
+    samples, deep = sides[0].shape
+    return pl.pallas_call(
+        stage_kernel,
+        in_specs=[pl.BlockSpec(memory_space=pltpu.HBM)] * 4,
+        out_specs=pl.BlockSpec(memory_space=pltpu.VMEM),
+        out_shape=pltpu.VMEM((4, samples, deep), jnp.bfloat16),
+        scratch_shapes=[pltpu.SemaphoreType.DMA((4,))],
+        compiler_params=pltpu.CompilerParams(vmem_limit_bytes=8 * MIB),
+        cost_estimate=pl.CostEstimate(flops=0, bytes_accessed=8 << 20, transcendentals=0),
+        name="stage_rows",
+    )(*in_hbm(*sides))
+
+
 def dense_kernel(
-    core_ref, own_a, peer_a, own_b, peer_b, weight_ref, out_ref, act_ref, slope_ref, logit_ref,
+    core_ref, sides_ref, weight_ref, out_ref, act_ref, slope_ref, logit_ref,
     sum_ref, columns_ref, sems,
 ):
-    samples, deep = own_a.shape
+    _, samples, deep = sides_ref.shape
     steps = columns_ref.shape[0]
     fetch_columns = []
     for n in range(steps):
@@ -251,7 +275,7 @@
         fetch.start()
 
     def product(n, m):
-        left, right = ((own_a, own_b), (peer_a, peer_b))[m // 2]
+        left, right = sides_ref.at[m // 2], sides_ref.at[2 + m // 2]
         rows = slice(ROW * (m % 2), ROW * (m % 2) + ROW)
         hidden = jnp.dot(left[rows], columns_ref[n, :deep], preferred_element_type=jnp.float32)
         return hidden + jnp.dot(right[rows], columns_ref[n, deep:], preferred_element_type=jnp.float32)
@@ -297,7 +321,7 @@
     inside = pl.BlockSpec(memory_space=pltpu.VMEM)
     return pl.pallas_call(
         dense_kernel,
-        in_specs=[pl.BlockSpec(memory_space=pltpu.SMEM)] + [inside] * 4 + [far] + [inside],
+        in_specs=[pl.BlockSpec(memory_space=pltpu.SMEM)] + [inside] + [far] + [inside],
         out_specs=[inside] * 3,
         out_shape=[
             pltpu.VMEM((steps, 2 * samples, 256), jnp.bfloat16),
@@ -312,7 +336,7 @@
         compiler_params=pltpu.CompilerParams(vmem_limit_bytes=16 * MIB),
         cost_estimate=pl.CostEstimate(flops=4 * samples * deep * 2 * wide, bytes_accessed=14 << 20, transcendentals=2 * samples * wide),
         name="dense_forward",
-    )(core.reshape(1), *in_vmem(own_a, peer_a, own_b, peer_b), *in_hbm(weight), out_w.reshape(1, wide))
+    )(core.reshape(1), *in_vmem(stage_call(own_a, peer_a, own_b, peer_b)), *in_hbm(weight), out_w.reshape(1, wide))
 
 
 def grad_kernel(

time: 186 us -> 190 us (1.022)
  local copies, waits for them, and re-layouts: 1.05 us -> 5.21 us
  waiting for transfers between devices: 54.8 us -> 51.8 us
  starting transfers between devices: 31.3 us -> 33.9 us
    unnamed x15 -> x23, local copies, waits for them, and re-layouts: 0.82 us -> 4.98 us
    all_gather x1, waiting for transfers between devices: 2.58 us -> 0.01 us  [per_device(): weight = lax.all_gather(w_first, ALL, axis=0, tiled=True)]
    all_to_all x1, starting transfers between devices: 7.56 us -> 9.98 us  [per_device(): terms = lax.all_to_all(blocks, ALL, split_axis=0, concat_axis=0, tiled=True)]
    pallas_call x0 -> x1, Pallas kernels: none -> 2.21 us  [stage_call(): pl.pallas_call(stage_kernel, in_specs=[pl.BlockSpec(memory_space=pltpu.HB...]
    pallas_call x1, Pallas kernels: 11 us -> 8.92 us  [dense_call(): pl.pallas_call(dense_kernel, in_specs=[pl.BlockSpec(memory_space=pltpu.SM...]
  transfers between devices with their start and end apart: 10 -> 10, of which waited for: 5 -> 4; matrix products, arithmetic and copies ran while one was open for 6% -> 6% of each run, Pallas kernels for 33% -> 32%
where the time goes in v7:
time: 190 us
  Pallas kernels  74 us (39%)
  waiting for transfers between devices  51.8 us (27%)
  starting transfers between devices  33.9 us (18%)
  between operations  14.3 us (8%)
  other arithmetic  10.4 us (5%)
  local copies, waits for them, and re-layouts  5.21 us (3%)
    all_to_all x1, waiting for transfers between devices, per_device(): terms = lax.all_to_all(blocks, ALL, split_axis=0, concat_axis=0, tiled=True)  46.8 us
    pallas_call x2, Pallas kernels, count_call(): pl.pallas_call(functools.partial(count_kernel, start), grid=(fields // GR...  28.6 us
    pallas_call x2, Pallas kernels, new_call(): pl.pallas_call(new_kernel, grid=(fields // GROUP,), in_specs=[pl.BlockSpe...  17.5 us
    all_to_all x1, starting transfers between devices, per_device(): got = lax.all_to_all(packet, ALL, split_axis=0, concat_axis=0, tiled=True)  11.5 us
    all_to_all x1, starting transfers between devices, per_device(): terms = lax.all_to_all(blocks, ALL, split_axis=0, concat_axis=0, tiled=True)  9.98 us
    all_to_all x1, starting transfers between devices, per_device(): lax.all_to_all(copies, ALL, split_axis=0, concat_axis=0, tiled=True)  9.77 us
    pallas_call x1, Pallas kernels, grad_call(): pl.pallas_call(grad_kernel, in_specs=[inside] * 9, out_specs=far, out_sha...  9.51 us
    pallas_call x1, Pallas kernels, dense_call(): pl.pallas_call(dense_kernel, in_specs=[pl.BlockSpec(memory_space=pltpu.SM...  8.92 us
  transfers between devices with their start and end apart: 10, of which 4 were waited for; matrix products, arithmetic and copies ran while one was open for 6% of the time, Pallas kernels for 32%

profile of v7, /device:TPU:1, one launch (start us, length us, event | category | flops | bytes accessed | tf_op | source)
XLA Modules:
  0.0 189.5 jit_solution(3762168484629930409)
XLA Ops:
  7.2 0.0 copy-start.4
  7.2 0.0 copy-start.6
  7.2 0.0 copy-start.7
  7.2 0.0 copy-start.5
  7.2 0.0 all-gather.2.cloned.1.call-start
  7.3 0.7 all-gather.2.cloned.1.call-update
  7.9 0.8 copy.16
  8.8 0.1 pad.14.clone
  8.8 1.9 maximum_maximum_fusion
  10.7 11.5 %all-to-all-start = ((f32[128,8,128]{2,1,0:T(8,128)}), f32[128,8,128]{2,1,0:T(8,128)S(1)}, u32[]{:S(2)}, u32[]{:S(2)}) async-start(f32[128,8,128]{2,1,0:T(8,128)} %maximum_maximum_fusion), calls=%async_computation | async-start | bytes 1048576 | tf_op jit(solution)/shard_map/all_to_all | solution.py:463
  22.2 0.0 copy-done.4
  22.2 0.0 copy-done.6
  22.3 0.0 copy-done.7
  22.3 0.0 copy-done.5
  22.3 14.3 %count_bags.2 = (s32[8,256,512]{2,1,0:T(8,128)}, f32[8,128,512]{2,1,0:T(8,128)}) custom-call(s32[16,8,512]{2,1,0:T(8,128)S(1)} %bitcast.17, s32[16,512]{1,0:T(8,128)S(1)} %bitcast.19, bf16[2048,128]{1,0:T(8,128)(2,1)S(1)} %copy-done.5), custom_call_target="tpu_custom_call" | custom-call | flops 2147483648 | bytes 20971520 | tf_op jit(solution)/shard_map/count_bags/pallas_call | solution.py:110
  36.6 0.0 all-to-all-done.got_ref
  36.6 4.0 %hot_rows.1 = bf16[128,16,128]{2,1,0:T(8,128)(2,1)} custom-call(s32[1,16]{1,0:T(1,128)S(1)} %copy-done.4, f32[128,8,128]{2,1,0:T(8,128)S(1)} %all-to-all-done.got_ref, f32[1,128]{1,0:T(1,128)S(1)} %pad.9.hot_ref, f32[4096,128]{1,0:T(8,128)} %table_ref.1, f32[4096,128]{1,0:T(8,128)} %accum_ref.1), custom_call_target="tpu_custom_call" | custom-call | flops 100663296 | bytes 1048576 | tf_op jit(solution)/shard_map/hot_rows/pallas_call | solution.py:222
  40.6 9.8 %all-to-all-start.1 = ((bf16[128,16,128]{2,1,0:T(8,128)(2,1)}), bf16[128,16,128]{2,1,0:T(8,128)(2,1)S(1)}, u32[]{:S(2)}, u32[]{:S(2)}) async-start(bf16[128,16,128]{2,1,0:T(8,128)(2,1)} %hot_rows.1), calls=%async_computation.1 | async-start | bytes 1048576 | tf_op jit(solution)/shard_map/all_to_all | solution.py:475
  50.4 14.3 %count_bags.3 = (s32[8,256,512]{2,1,0:T(8,128)}, f32[8,128,512]{2,1,0:T(8,128)}) custom-call(s32[16,8,512]{2,1,0:T(8,128)S(1)} %bitcast.18, s32[16,512]{1,0:T(8,128)S(1)} %bitcast.20, bf16[2048,128]{1,0:T(8,128)(2,1)S(1)} %copy-done.5), custom_call_target="tpu_custom_call" | custom-call | flops 2147483648 | bytes 20971520 | tf_op jit(solution)/shard_map/count_bags/pallas_call | solution.py:110
  64.7 0.1 all-to-all-done.1
  64.8 8.6 %pool_new.2 = (bf16[1024,512]{1,0:T(8,128)(2,1)}, bf16[512,1024]{1,0:T(8,128)(2,1)S(1)}) custom-call(s32[8,256,512]{2,1,0:T(8,128)} %get-tuple-element.23.words_ref, f32[8,128,512]{2,1,0:T(8,128)} %get-tuple-element.24.part_ref, bf16[2048,128]{1,0:T(8,128)(2,1)S(1)} %bitcast.14), custom_call_target="tpu_custom_call" | custom-call | flops 2147483648 | bytes 20971520 | tf_op jit(solution)/shard_map/pool_new/pallas_call | solution.py:161
  73.4 0.0 copy-start.2
  73.4 1.0 collective-permute-start.2
  74.4 0.0 copy-start.9
  74.4 0.0 copy-start.10
  74.5 8.8 %pool_new.3 = (bf16[1024,512]{1,0:T(8,128)(2,1)}, bf16[512,1024]{1,0:T(8,128)(2,1)S(1)}) custom-call(s32[8,256,512]{2,1,0:T(8,128)} %get-tuple-element.26.words_ref, f32[8,128,512]{2,1,0:T(8,128)} %get-tuple-element.27.part_ref, bf16[2048,128]{1,0:T(8,128)(2,1)S(1)} %bitcast.15), custom_call_target="tpu_custom_call" | custom-call | flops 2147483648 | bytes 20971520 | tf_op jit(solution)/shard_map/pool_new/pallas_call | solution.py:161
  83.3 0.0 copy-done.2
  83.3 0.0 copy-start.3
  83.3 0.2 collective-permute-start.3
  83.5 0.3 collective-permute-start
  83.8 0.2 collective-permute-start.1
  84.0 0.0 copy-done.9
  84.0 0.3 collective-permute-start.5
  84.3 0.0 copy-done.10
  84.3 0.0 collective-permute-done.2.peer_a
  84.3 3.3 %collective-permute-done.3.peer_b = bf16[512,1024]{1,0:T(8,128)(2,1)} collective-permute-done((bf16[512,1024]{1,0:T(8,128)(2,1)S(1)}, bf16[512,1024]{1,0:T(8,128)(2,1)}, u32[]{:S(2)}, u32[]{:S(2)}) %collective-permute-start.3) | collective-permute-done | bytes 1048608 | tf_op jit(solution)/shard_map/ppermute | solution.py:482
  87.7 0.0 copy-done.3
  87.7 2.2 %stage_rows.1.sides_ref = bf16[4,512,1024]{2,1,0:T(8,128)(2,1)S(1)} custom-call(bf16[512,1024]{1,0:T(8,128)(2,1)} %copy-done.2, bf16[512,1024]{1,0:T(8,128)(2,1)} %collective-permute-done.2.peer_a, bf16[512,1024]{1,0:T(8,128)(2,1)} %copy-done.3, bf16[512,1024]{1,0:T(8,128)(2,1)} %collective-permute-done.3.peer_b), custom_call_target="tpu_custom_call" | custom-call | bytes 8388608 | tf_op jit(solution)/shard_map/stage_rows/pallas_call | solution.py:252
  89.9 0.0 copy-start
  89.9 2.0 %copy-done = bf16[4,512,1024]{2,1,0:T(8,128)(2,1)} copy-done((bf16[4,512,1024]{2,1,0:T(8,128)(2,1)}, bf16[4,512,1024]{2,1,0:T(8,128)(2,1)S(1)}, u32[]{:S(2)}) %copy-start) | copy-done | bytes 4194328
  91.9 0.0 all-gather.2.cloned.1.call-done.weight_ref
  91.9 0.0 copy-start.1
  91.9 2.2 %copy-done.1 = bf16[4,512,1024]{2,1,0:T(8,128)(2,1)S(1)} copy-done((bf16[4,512,1024]{2,1,0:T(8,128)(2,1)S(1)}, bf16[4,512,1024]{2,1,0:T(8,128)(2,1)}, u32[]{:S(2)}) %copy-start.1) | copy-done | bytes 4194328
  94.1 8.9 %dense_forward.1 = (bf16[4,1024,256]{2,1,0:T(8,128)(2,1)S(1)}, f32[4,1024,256]{2,1,0:T(8,128)S(1)}, f32[8,128]{1,0:T(8,128)S(1)}) custom-call(s32[1]{0:T(128)} %bitcast.8.core_ref, bf16[4,512,1024]{2,1,0:T(8,128)(2,1)S(1)} %copy-done.1, bf16[2048,2048]{1,0:T(8,128)(2,1)} %all-gather.2.cloned.1.call-done.weight_ref, f32[1,1024]{1,0:T(1,128)S(1)} %bitcast.16), custom_call_target="tpu_custom_call" | custom-call | flops 4294967296 | bytes 14680064 | tf_op jit(solution)/shard_map/dense_forward/pallas_call | solution.py:322
  103.0 0.6 collective-permute-start.4
  103.5 0.0 collective-permute-done.5
  103.5 0.0 collective-permute-done.peer_a
  103.6 0.0 collective-permute-done.1.peer_b
  103.6 0.9 collective-permute-done.4.swapped_ref
  104.4 9.5 %grad_terms.1 = bf16[128,136,128]{2,1,0:T(8,128)(2,1)} custom-call(bf16[1024,512]{1,0:T(8,128)(2,1)} %get-tuple-element.25.own_a, bf16[1024,512]{1,0:T(8,128)(2,1)} %collective-permute-done.peer_a, bf16[1024,512]{1,0:T(8,128)(2,1)} %get-tuple-element.28.own_b, bf16[1024,512]{1,0:T(8,128)(2,1)} %collective-permute-done.1.peer_b, ...), custom_call_target="tpu_custom_call" | custom-call | flops 4294967296 | bytes 14680064 | tf_op jit(solution)/shard_map/grad_terms/pallas_call | solution.py:395
  114.0 10.0 %all-to-all-start.2 = ((bf16[128,136,128]{2,1,0:T(8,128)(2,1)}), bf16[128,136,128]{2,1,0:T(8,128)(2,1)}, u32[]{:S(2)}, u32[]{:S(2)}) async-start(bf16[128,136,128]{2,1,0:T(8,128)(2,1)} %grad_terms.1), calls=%async_computation.2 | async-start | bytes 8912896 | tf_op jit(solution)/shard_map/all_to_all | solution.py:491
  124.0 0.0 copy-start.8
  124.0 0.2 convert_reduce_fusion
  124.2 0.1 convert_element_type.32
  124.4 3.6 %scatter_custom_fusion = f32[4096,128]{1,0:T(8,128)} fusion(s32[512]{0:T(512)S(1)} %bitcast.24, f32[512,128]{1,0:T(8,128)S(1)} %bitcast.23, f32[]{:T(128)} %constant.8.clone.1), kind=kCustom, calls=%fused_computation.3 | custom fusion | flops 65536 | bytes 2097156 | tf_op jit(solution)/shard_map/scatter-add | solution.py:495
  128.0 0.0 copy-done.8
  128.0 4.6 %multiply_subtract_fusion = (f32[4096,128]{1,0:T(8,128)}, f32[4096,128]{1,0:T(8,128)}) fusion(f32[4096,128]{1,0:T(8,128)S(1)} %copy-done.8, f32[4096,128]{1,0:T(8,128)} %scatter_custom_fusion, f32[4096,128]{1,0:T(8,128)} %accum_ref.1), kind=kLoop, calls=%fused_computation.1 | loop fusion | flops 2621440 | bytes 10485760 | tf_op jit(solution)/shard_map/sub | solution.py:497
  132.7 46.8 %all-to-all-done.2.terms_ref = bf16[128,136,128]{2,1,0:T(8,128)(2,1)} async-done(((bf16[128,136,128]{2,1,0:T(8,128)(2,1)}), bf16[128,136,128]{2,1,0:T(8,128)(2,1)}, u32[]{:S(2)}, u32[]{:S(2)}) %all-to-all-start.2) | async-done | bytes 4456480 | tf_op jit(solution)/shard_map/all_to_all | solution.py:491
  179.4 3.3 %sum_terms.1 = (f32[16,2048]{1,0:T(8,128)}, f32[16,128]{1,0:T(8,128)}) custom-call(bf16[128,136,128]{2,1,0:T(8,128)(2,1)} %all-to-all-done.2.terms_ref), custom_call_target="tpu_custom_call" | custom-call | flops 2228224 | bytes 5242880 | tf_op jit(solution)/shard_map/sum_terms/pallas_call | solution.py:438
  (10 shorter events, 0.1 us)
Async XLA Ops:
  7.2 15.0 %copy-start.4 = (s32[1,16]{1,0:T(1,128)S(1)}, s32[1,16]{1,0:T(1,128)}, u32[]{:S(2)}) copy-start(s32[1,16]{1,0:T(1,128)} %ids_ref.1) | copy-start | bytes 196
  7.2 15.1 %copy-start.6 = (s32[512,16,8]{0,2,1:T(8,128)S(1)}, s32[512,16,8]{0,2,1:T(8,128)}, u32[]{:S(2)}) copy-start(s32[512,16,8]{0,2,1:T(8,128)} %param.17) | copy-start | bytes 786436
  7.2 15.1 %copy-start.7 = (s32[512,16]{0,1:T(8,128)S(1)}, s32[512,16]{0,1:T(8,128)}, u32[]{:S(2)}) copy-start(s32[512,16]{0,1:T(8,128)} %param.18) | copy-start | bytes 98308
  7.2 15.1 %copy-start.5 = (bf16[2048,128]{1,0:T(8,128)(2,1)S(1)}, bf16[2048,128]{1,0:T(8,128)(2,1)}, u32[]{:S(2)}) copy-start(bf16[2048,128]{1,0:T(8,128)(2,1)} %rows_ref.3) | copy-start | bytes 1572868
  7.2 84.7 %all-gather.2.cloned.1.call-start = ((), (), s32[]{:S(2)}) async-start(), calls=%async_computation.3 | async-start | bytes 8454144 | tf_op jit(solution)/shard_map/all_gather | solution.py:465
  10.7 25.9 %all-to-all-start = ((f32[128,8,128]{2,1,0:T(8,128)}), f32[128,8,128]{2,1,0:T(8,128)S(1)}, u32[]{:S(2)}, u32[]{:S(2)}) async-start(f32[128,8,128]{2,1,0:T(8,128)} %maximum_maximum_fusion), calls=%async_computation | async-start | bytes 1048576 | tf_op jit(solution)/shard_map/all_to_all | solution.py:463
  40.6 24.2 %all-to-all-start.1 = ((bf16[128,16,128]{2,1,0:T(8,128)(2,1)}), bf16[128,16,128]{2,1,0:T(8,128)(2,1)S(1)}, u32[]{:S(2)}, u32[]{:S(2)}) async-start(bf16[128,16,128]{2,1,0:T(8,128)(2,1)} %hot_rows.1), calls=%async_computation.1 | async-start | bytes 1048576 | tf_op jit(solution)/shard_map/all_to_all | solution.py:475
  73.4 9.9 %copy-start.2 = (bf16[512,1024]{1,0:T(8,128)(2,1)}, bf16[512,1024]{1,0:T(8,128)(2,1)S(1)}, u32[]{:S(2)}) copy-start(bf16[512,1024]{1,0:T(8,128)(2,1)S(1)} %get-tuple-element.29.own_a) | copy-start | bytes 3145732
  73.4 10.9 %collective-permute-start.2 = (bf16[512,1024]{1,0:T(8,128)(2,1)S(1)}, bf16[512,1024]{1,0:T(8,128)(2,1)}, u32[]{:S(2)}, u32[]{:S(2)}) collective-permute-start(bf16[512,1024]{1,0:T(8,128)(2,1)S(1)} %get-tuple-element.29.own_a), channel_id=1, source_target_pairs={{0,1},{1,0},{2,3},{3,2},{4,5},{5,4},{6,7},{7,6},{8,9},{9,8},{10,11... | collective-permute-start | bytes 3145736 | tf_op jit(solution)/shard_map/ppermute | solution.py:482
  74.4 9.6 %copy-start.9 = (s32[512]{0:T(512)S(1)}, s32[512]{0:T(512)}, u32[]{:S(2)}) copy-start(s32[512]{0:T(512)} %param.19) | copy-start | bytes 6148
  74.4 9.9 %copy-start.10 = (bf16[2048]{0:T(1024)(128)(2,1)S(1)}, bf16[2048]{0:T(1024)(128)(2,1)}, u32[]{:S(2)}) copy-start(bf16[2048]{0:T(1024)(128)(2,1)} %param.21) | copy-start | bytes 12292
  83.3 4.4 %copy-start.3 = (bf16[512,1024]{1,0:T(8,128)(2,1)}, bf16[512,1024]{1,0:T(8,128)(2,1)S(1)}, u32[]{:S(2)}) copy-start(bf16[512,1024]{1,0:T(8,128)(2,1)S(1)} %get-tuple-element.30.own_b) | copy-start | bytes 3145732
  83.3 4.4 %collective-permute-start.3 = (bf16[512,1024]{1,0:T(8,128)(2,1)S(1)}, bf16[512,1024]{1,0:T(8,128)(2,1)}, u32[]{:S(2)}, u32[]{:S(2)}) collective-permute-start(bf16[512,1024]{1,0:T(8,128)(2,1)S(1)} %get-tuple-element.30.own_b), channel_id=1, source_target_pairs={{0,1},{1,0},{2,3},{3,2},{4,5},{5,4},{6,7},{7,6},{8,9},{9,8},{10,11... | collective-permute-start | bytes 3145736 | tf_op jit(solution)/shard_map/ppermute | solution.py:482
  83.5 20.0 %collective-permute-start = (bf16[1024,512]{1,0:T(8,128)(2,1)}, bf16[1024,512]{1,0:T(8,128)(2,1)}, u32[]{:S(2)}, u32[]{:S(2)}) collective-permute-start(bf16[1024,512]{1,0:T(8,128)(2,1)} %get-tuple-element.25.own_a), channel_id=1, source_target_pairs={{0,1},{1,0},{2,3},{3,2},{4,5},{5,4},{6,7},{7,6},{8,9},{9,8},{10,11... | collective-permute-start | bytes 3145736 | tf_op jit(solution)/shard_map/ppermute | solution.py:482
  83.8 19.8 %collective-permute-start.1 = (bf16[1024,512]{1,0:T(8,128)(2,1)}, bf16[1024,512]{1,0:T(8,128)(2,1)}, u32[]{:S(2)}, u32[]{:S(2)}) collective-permute-start(bf16[1024,512]{1,0:T(8,128)(2,1)} %get-tuple-element.28.own_b), channel_id=1, source_target_pairs={{0,1},{1,0},{2,3},{3,2},{4,5},{5,4},{6,7},{7,6},{8,9},{9,8},{10,11... | collective-permute-start | bytes 3145736 | tf_op jit(solution)/shard_map/ppermute | solution.py:482
  84.0 19.5 %collective-permute-start.5 = (f32[4,128]{1,0:T(4,128)S(1)}, f32[4,128]{1,0:T(4,128)S(1)}, u32[]{:S(2)}, u32[]{:S(2)}) collective-permute-start(f32[4,128]{1,0:T(4,128)S(1)} %convert_bitcast_fusion.1), channel_id=1, source_target_pairs={{0,1},{1,0},{2,3},{3,2},{4,5},{5,4},{6,7},{7,6},{8,9},{9,8},{10,11... | collective-permute-start | bytes 6152 | tf_op jit(solution)/shard_map/ppermute | solution.py:484
  89.9 2.0 %copy-start = (bf16[4,512,1024]{2,1,0:T(8,128)(2,1)}, bf16[4,512,1024]{2,1,0:T(8,128)(2,1)S(1)}, u32[]{:S(2)}) copy-start(bf16[4,512,1024]{2,1,0:T(8,128)(2,1)S(1)} %stage_rows.1.sides_ref) | copy-start | bytes 12582916
  91.9 2.2 %copy-start.1 = (bf16[4,512,1024]{2,1,0:T(8,128)(2,1)S(1)}, bf16[4,512,1024]{2,1,0:T(8,128)(2,1)}, u32[]{:S(2)}) copy-start(bf16[4,512,1024]{2,1,0:T(8,128)(2,1)} %copy-done) | copy-start | bytes 12582916
  103.0 1.5 collective-permute-start.4
  114.0 65.4 %all-to-all-start.2 = ((bf16[128,136,128]{2,1,0:T(8,128)(2,1)}), bf16[128,136,128]{2,1,0:T(8,128)(2,1)}, u32[]{:S(2)}, u32[]{:S(2)}) async-start(bf16[128,136,128]{2,1,0:T(8,128)(2,1)} %grad_terms.1), calls=%async_computation.2 | async-start | bytes 8912896 | tf_op jit(solution)/shard_map/all_to_all | solution.py:491
  124.0 4.1 %copy-start.8 = (f32[4096,128]{1,0:T(8,128)S(1)}, f32[4096,128]{1,0:T(8,128)}, u32[]{:S(2)}) copy-start(f32[4096,128]{1,0:T(8,128)} %table_ref.1) | copy-start | bytes 6291460
Sparse Core Ops, SparseCore 0:
  11.0 79.4 all-gather.1
